TPU v7x, 128 devices: a whole 4x4x4 slice. The times are simulated.
128 devices in a mesh: dp: 64 (over x, y, z), mp: 2 (over core).
Axes of the slice: x: 4, y: 4, z: 4, core: 2. Of those that a mesh axis runs over, the one named last changes fastest.
Arguments:
- block_input: bfloat16 [8192, 2048], P('dp'), may hold values from -6 to 6
- cotangent: bfloat16 [8192, 2048], P('dp'), may hold values from -9 to 9
- head_count: int32 [8192], P('dp'), may hold values from 1 to 16
- width_route: int32 [8192], P('dp'), may hold values from 0 to 3
- forced_width: int32 [64], P('dp'), may hold values from 0 to 4, as said below
- slot_index: int32 [8192], P('dp'), may hold values from -1 to 63, as said below
- qkv_weight: float32 [2048, 3, 16, 128], P('dp', None, 'mp'), may hold values from -0.125 to 0.125
- out_weight: float32 [16, 128, 2048], P('mp', None, 'dp'), may hold values from -0.5 to 0.5
- up_weight: float32 [2048, 8192], P('dp', 'mp'), may hold values from -0.125 to 0.125
- down_weight: float32 [8192, 2048], P('mp', 'dp'), may hold values from -0.1875 to 0.1875
- router_weight: float32 [2048, 4], P('dp'), may hold values from -0.09375 to 0.09375
- norm_gains: float32 [2, 2048], P(None, 'dp'), may hold values from 0.38 to 2.59
- norm_biases: float32 [2, 2048], P(None, 'dp'), may hold values from -1.75 to 1.75
- qkv_first: float32 [2048, 3, 16, 128], P('dp', None, 'mp'), may hold values from -160 to 160
- qkv_second: float32 [2048, 3, 16, 128], P('dp', None, 'mp'), may hold values from 737.28 to 2949.12
- out_first: float32 [16, 128, 2048], P('mp', None, 'dp'), may hold values from -56 to 56
- out_second: float32 [16, 128, 2048], P('mp', None, 'dp'), may hold values from 81.92 to 327.68
- up_first: float32 [2048, 8192], P('dp', 'mp'), may hold values from -112 to 112
- up_second: float32 [2048, 8192], P('dp', 'mp'), may hold values from 327.68 to 1310.72
- down_first: float32 [8192, 2048], P('mp', 'dp'), may hold values from -112 to 112
- down_second: float32 [8192, 2048], P('mp', 'dp'), may hold values from 327.68 to 1310.72
- router_first: float32 [2048, 4], P('dp'), may hold values from -1536 to 1536
- router_second: float32 [2048, 4], P('dp'), may hold values from 73728 to 294912
- norm_first: float32 [4, 2048], P(None, 'dp'), may hold values from -512 to 512
- norm_second: float32 [4, 2048], P(None, 'dp'), may hold values from 8192 to 32768
Outputs:
- block_output: bfloat16 [8192, 2048], P('dp')
- input_grad: float32 [8192, 2048], P('dp')
- qkv_grad: float32 [2048, 3, 16, 128], P('dp', None, 'mp')
- out_grad: float32 [16, 128, 2048], P('mp', None, 'dp')
- up_grad: float32 [2048, 8192], P('dp', 'mp')
- down_grad: float32 [8192, 2048], P('mp', 'dp')
- router_grad: float32 [2048, 4], P('dp')
- norms_grad: float32 [4, 2048], P(None, 'dp')
- qkv_first_new: float32 [2048, 3, 16, 128], P('dp', None, 'mp')
- out_first_new: float32 [16, 128, 2048], P('mp', None, 'dp')
- up_first_new: float32 [2048, 8192], P('dp', 'mp')
- down_first_new: float32 [8192, 2048], P('mp', 'dp')
- router_first_new: float32 [2048, 4], P('dp')
- norms_first_new: float32 [4, 2048], P(None, 'dp')
- qkv_second_new: float32 [2048, 3, 16, 128], P('dp', None, 'mp')
- out_second_new: float32 [16, 128, 2048], P('mp', None, 'dp')
- up_second_new: float32 [2048, 8192], P('dp', 'mp')
- down_second_new: float32 [8192, 2048], P('mp', 'dp')
- router_second_new: float32 [2048, 4], P('dp')
- norms_second_new: float32 [4, 2048], P(None, 'dp')
- qkv_new: float32 [2048, 3, 16, 128], P('dp', None, 'mp')
- out_new: float32 [16, 128, 2048], P('mp', None, 'dp')
- up_new: float32 [2048, 8192], P('dp', 'mp')
- down_new: float32 [8192, 2048], P('mp', 'dp')
- router_new: float32 [2048, 4], P('dp')
- norms_new: float32 [4, 2048], P(None, 'dp')
- qkv_copy: bfloat16 [2048, 3, 16, 128], P('dp', None, 'mp')
- out_copy: bfloat16 [16, 128, 2048], P('mp', None, 'dp')
- up_copy: bfloat16 [2048, 8192], P('dp', 'mp')
- down_copy: bfloat16 [8192, 2048], P('mp', 'dp')
- router_copy: bfloat16 [2048, 4], P('dp')
- norms_copy: bfloat16 [4, 2048], P(None, 'dp')
- lamb_norms: float32 [5, 2], replicated
Inputs may be any that keep to these rules, and one draw needn't show every extreme that they name: `forced_width`: A value of 4 leaves the sequence's tokens to width_route; a smaller value sets that bucket for all 128 tokens of the sequence. -1 marks a token that skips the feed-forward; otherwise slot_index = p * 4 + r with p < 16 and r < 4. Within one sequence, tokens with the same bucket have distinct slots, and a token skips only when more than 64 tokens of its sequence share its bucket.
All inputs are finite; a program needn't handle non-finite values.
Results may differ from a plain program's by a relative error of at most 0.02.
The roundings to bfloat16 on the way count: a program that leaves them out, or rounds other values in their place, can miss the bound.
Values may be sent and summed in bfloat16 or wider, within the bound.
A program may use at most 320 MiB of HBM per device.

v0:
```python
from functools import partial

import jax
import jax.numpy as jnp
from jax import lax
from jax.sharding import PartitionSpec as P

STEP = 5


HIGHEST = lax.Precision.HIGHEST
BETA_ONE = 0.5
BETA_TWO = 0.5
ADAM_EPS = 1e-06
DECAY_RATE = 0.01
LEARN_RATE = 0.5
NORM_RATE = 0.1
NORM_EPS = 1e-05
ROPE_BASE = 10000.0


def for_sending(x):
    return jax.tree.map(lambda a: a.astype(jnp.bfloat16) if a.dtype == jnp.float32 else a, x)


def layer_norm(value, gain_row, shift_row):
    centre = value - jnp.mean(value, axis=-1, keepdims=True)
    spread = jnp.mean(centre * centre, axis=-1, keepdims=True)
    inverse = lax.rsqrt(spread + NORM_EPS)
    scaled = centre * inverse
    return (scaled * gain_row + shift_row, scaled, inverse)


def norm_back(scaled, inverse, gain_row, upstream):
    dscaled = upstream * gain_row
    inner = (
        dscaled
        - jnp.mean(dscaled, axis=-1, keepdims=True)
        - scaled * jnp.mean(dscaled * scaled, axis=-1, keepdims=True)
    )
    return (inner * inverse, jnp.sum(upstream * scaled, axis=0), jnp.sum(upstream, axis=0))


def rotary_tables(length, size):
    half_size = size // 2
    frequency = ROPE_BASE ** (-(jnp.arange(half_size, dtype=jnp.float32) * 2.0 / size))
    angles = jnp.arange(length, dtype=jnp.float32)[:, None] * frequency[None, :]
    cosine_table = jnp.concatenate([jnp.cos(angles), jnp.cos(angles)], axis=-1)
    sine_table = jnp.concatenate([jnp.sin(angles), jnp.sin(angles)], axis=-1)
    return (cosine_table[:, None, :], sine_table[:, None, :])


def rotate(value, cosine_table, sine_table):
    half_size = value.shape[-1] // 2
    turned = jnp.concatenate([-value[..., half_size:], value[..., :half_size]], axis=-1)
    return value * cosine_table + turned * sine_table


def rotate_back(gradient, cosine_table, sine_table):
    half_size = gradient.shape[-1] // 2
    moved = gradient * sine_table
    turned = jnp.concatenate([moved[..., half_size:], -moved[..., :half_size]], axis=-1)
    return gradient * cosine_table + turned


def soft_choice(logits):
    row_top = jnp.max(logits, axis=-1, keepdims=True)
    exponent = jnp.exp(logits - row_top)
    return exponent / jnp.sum(exponent, axis=-1, keepdims=True)


def bucket_forward(units, arrived, up_full, down_full):
    local_units = up_full.shape[1]
    if units == 0:
        return (
            jnp.zeros((arrived.shape[0], down_full.shape[1]), jnp.float32),
            jnp.zeros((arrived.shape[0], local_units), jnp.float32),
        )
    up_value = jnp.dot(arrived, up_full[:, :units], preferred_element_type=jnp.float32)
    activation = jnp.square(jax.nn.relu(up_value)).astype(jnp.bfloat16)
    produced = jnp.dot(activation, down_full[:units], preferred_element_type=jnp.float32)
    return (produced, jnp.pad(up_value, ((0, 0), (0, local_units - units))))


def bucket_backward(units, arrived, arrived_grad, pre_act, up_full, down_full):
    local_units = up_full.shape[1]
    feature_count = up_full.shape[0]
    if units == 0:
        return (
            jnp.zeros((arrived.shape[0], feature_count), jnp.float32),
            jnp.zeros((feature_count, local_units), jnp.float32),
            jnp.zeros((local_units, feature_count), jnp.float32),
        )
    up_value = pre_act[:, :units]
    activation = jnp.square(jax.nn.relu(up_value)).astype(jnp.bfloat16)
    act_grad = jnp.einsum(
        "rd,ud->ru", arrived_grad, down_full[:units], preferred_element_type=jnp.float32
    )
    up_low = (act_grad * 2.0 * jax.nn.relu(up_value)).astype(jnp.bfloat16)
    down_part = jnp.einsum(
        "ru,rd->ud", activation, arrived_grad, preferred_element_type=jnp.float32
    )
    up_part = jnp.einsum("rd,ru->du", arrived, up_low, preferred_element_type=jnp.float32)
    row_part = jnp.einsum(
        "ru,du->rd", up_low, up_full[:, :units], preferred_element_type=jnp.float32
    )
    return (
        row_part,
        jnp.pad(up_part, ((0, 0), (0, local_units - units))),
        jnp.pad(down_part, ((0, local_units - units), (0, 0))),
    )


def moment_step(weight, gradient, first_moment, second_moment, decay_rate):
    first_moment = BETA_ONE * first_moment + (1.0 - BETA_ONE) * gradient
    second_moment = BETA_TWO * second_moment + (1.0 - BETA_TWO) * gradient * gradient
    update = (
        first_moment
        / (1.0 - BETA_ONE**STEP)
        / (jnp.sqrt(second_moment / (1.0 - BETA_TWO**STEP)) + ADAM_EPS)
        + decay_rate * weight
    )
    return (first_moment, second_moment, update)


def local(
    block_input,
    cotangent,
    head_count,
    width_route,
    forced_width,
    slot_index,
    qkv_weight,
    out_weight,
    up_weight,
    down_weight,
    router_weight,
    norm_gains,
    norm_biases,
    qkv_first,
    qkv_second,
    out_first,
    out_second,
    up_first,
    up_second,
    down_first,
    down_second,
    router_first,
    router_second,
    norm_first,
    norm_second,
):
    data_count = lax.axis_size("dp")
    core_count = lax.axis_size("mp")
    core_index = lax.axis_index("mp")
    data_index = lax.axis_index("dp")
    length = block_input.shape[0]
    feature_count = block_input.shape[1]
    local_heads = qkv_weight.shape[2]
    head_size = qkv_weight.shape[3]
    bucket_count = router_weight.shape[1]
    local_units = up_weight.shape[1]
    quarter = local_units * core_count // bucket_count
    capacity = 2 * length // data_count
    buffer_rows = data_count * capacity
    norm_master = jnp.concatenate([norm_gains, norm_biases], axis=0)
    qkv_full, out_full, up_full, down_full, router_full, small_full = (
        lax.all_gather(qkv_weight.astype(jnp.bfloat16), "dp", axis=0, tiled=True),
        lax.all_gather(out_weight.astype(jnp.bfloat16), "dp", axis=2, tiled=True),
        lax.all_gather(up_weight.astype(jnp.bfloat16), "dp", axis=0, tiled=True),
        lax.all_gather(down_weight.astype(jnp.bfloat16), "dp", axis=1, tiled=True),
        lax.all_gather(router_weight.astype(jnp.bfloat16), "dp", axis=0, tiled=True),
        lax.all_gather(norm_master.astype(jnp.bfloat16), "dp", axis=1, tiled=True),
    )
    norm_rows = small_full.astype(jnp.float32)
    inputs = block_input.astype(jnp.float32)
    ln_one, scaled_one, inverse_one = layer_norm(inputs, norm_rows[0], norm_rows[2])
    a_one = ln_one.astype(jnp.bfloat16)
    qkv = jnp.einsum("td,dchk->tchk", a_one, qkv_full, preferred_element_type=jnp.float32)
    cosine_table, sine_table = rotary_tables(length, head_size)
    score_scale = head_size ** (-0.5)
    query_rows = (rotate(qkv[:, 0], cosine_table, sine_table) * score_scale).astype(jnp.bfloat16)
    key_rows = rotate(qkv[:, 1], cosine_table, sine_table).astype(jnp.bfloat16)
    value_rows = qkv[:, 2].astype(jnp.bfloat16)
    positions = jnp.arange(length, dtype=jnp.int32)
    causal = positions[:, None] >= positions[None, :]
    scores = jnp.einsum("qhk,shk->hqs", query_rows, key_rows, preferred_element_type=jnp.float32)
    scores = jnp.where(causal[None, :, :], scores, -1e30)
    row_top = jnp.max(scores, axis=-1, keepdims=True)
    exponent = jnp.exp(scores - row_top)
    row_total = jnp.sum(exponent, axis=-1, keepdims=True)
    attn_probs = exponent / row_total
    log_total = row_top + jnp.log(row_total)
    heads_out = jnp.einsum(
        "hqs,shk->qhk",
        attn_probs.astype(jnp.bfloat16),
        value_rows,
        preferred_element_type=jnp.float32,
    )
    head_ids = core_index * local_heads + jnp.arange(local_heads, dtype=jnp.int32)
    head_used = (head_ids[None, :] < head_count[:, None]).astype(jnp.float32)
    mixed_heads = (heads_out * head_used[:, :, None]).astype(jnp.bfloat16)
    attn_part = jnp.einsum("thk,hkd->td", mixed_heads, out_full, preferred_element_type=jnp.float32)
    attention = lax.psum(attn_part, "mp")
    hidden = inputs + attention
    ln_two, scaled_two, inverse_two = layer_norm(hidden, norm_rows[1], norm_rows[3])
    a_two = ln_two.astype(jnp.bfloat16)
    router = soft_choice(jnp.dot(a_two, router_full, preferred_element_type=jnp.float32))
    chosen = jnp.where(forced_width[0] < bucket_count, forced_width[0], width_route)
    bucket_onehot = (chosen[:, None] == jnp.arange(bucket_count, dtype=jnp.int32)[None, :]).astype(
        jnp.float32
    )
    gate_value = jnp.sum(router * bucket_onehot, axis=-1)
    kept_mask = slot_index >= 0
    kept_float = kept_mask.astype(jnp.float32)
    peer_index = slot_index // capacity
    slot_row = slot_index % capacity
    target = jnp.where(
        kept_mask, (peer_index * bucket_count + chosen) * capacity + slot_row, buffer_rows
    )
    fetch_rows = jnp.where(kept_mask, target, 0)
    send_rows = (
        jnp.zeros((buffer_rows, feature_count), jnp.bfloat16).at[target].set(a_two, mode="drop")
    )
    arrived = lax.all_to_all(
        send_rows.reshape(data_count, capacity, feature_count),
        "dp",
        split_axis=0,
        concat_axis=0,
        tiled=True,
    ).reshape(buffer_rows, feature_count)
    own_bucket = data_index % bucket_count
    per_core = bucket_count // core_count
    used_quarters = jnp.clip(own_bucket + 1 - core_index * per_core, 0, per_core)
    forward_cases = [partial(bucket_forward, count * quarter) for count in range(per_core + 1)]
    partial_out, pre_act = lax.switch(used_quarters, forward_cases, arrived, up_full, down_full)
    summed = jax.tree.map(
        lambda part: part.astype(jnp.float32), lax.psum(for_sending(partial_out), "mp")
    )
    returned = lax.all_to_all(
        summed.astype(jnp.bfloat16).reshape(data_count, capacity, feature_count),
        "dp",
        split_axis=0,
        concat_axis=0,
        tiled=True,
    ).reshape(buffer_rows, feature_count)
    branch_out = returned[fetch_rows].astype(jnp.float32) * kept_float[:, None]
    result = hidden + gate_value[:, None] * branch_out
    block_output = result.astype(jnp.bfloat16)
    qkv_full, out_full, up_full, down_full, router_full, small_full = (
        lax.all_gather(qkv_weight.astype(jnp.bfloat16), "dp", axis=0, tiled=True),
        lax.all_gather(out_weight.astype(jnp.bfloat16), "dp", axis=2, tiled=True),
        lax.all_gather(up_weight.astype(jnp.bfloat16), "dp", axis=0, tiled=True),
        lax.all_gather(down_weight.astype(jnp.bfloat16), "dp", axis=1, tiled=True),
        lax.all_gather(router_weight.astype(jnp.bfloat16), "dp", axis=0, tiled=True),
        lax.all_gather(norm_master.astype(jnp.bfloat16), "dp", axis=1, tiled=True),
    )
    norm_rows = small_full.astype(jnp.float32)
    upstream = cotangent.astype(jnp.float32)
    gate_grad = jnp.sum(upstream * branch_out, axis=-1)
    logit_grad = router * (bucket_onehot - gate_value[:, None]) * gate_grad[:, None]
    branch_grad = (upstream * gate_value[:, None] * kept_float[:, None]).astype(jnp.bfloat16)
    send_grad = (
        jnp.zeros((buffer_rows, feature_count), jnp.bfloat16)
        .at[target]
        .set(branch_grad, mode="drop")
    )
    arrived_grad = lax.all_to_all(
        send_grad.reshape(data_count, capacity, feature_count),
        "dp",
        split_axis=0,
        concat_axis=0,
        tiled=True,
    ).reshape(buffer_rows, feature_count)
    backward_cases = [partial(bucket_backward, count * quarter) for count in range(per_core + 1)]
    row_part, up_grad_w, down_grad_w = lax.switch(
        used_quarters, backward_cases, arrived, arrived_grad, pre_act, up_full, down_full
    )
    row_sum = jax.tree.map(
        lambda part: part.astype(jnp.float32), lax.psum(for_sending(row_part), "mp")
    )
    row_back = lax.all_to_all(
        row_sum.astype(jnp.bfloat16).reshape(data_count, capacity, feature_count),
        "dp",
        split_axis=0,
        concat_axis=0,
        tiled=True,
    ).reshape(buffer_rows, feature_count)
    ffn_back = row_back[fetch_rows].astype(jnp.float32) * kept_float[:, None]
    ln_two_grad = ffn_back + jnp.dot(
        logit_grad, router_full.astype(jnp.float32).T, precision=HIGHEST
    )
    router_grad_w = jnp.dot(a_two.astype(jnp.float32).T, logit_grad, precision=HIGHEST)
    norm_in_two, gain_two_grad, bias_two_grad = norm_back(
        scaled_two, inverse_two, norm_rows[1], ln_two_grad
    )
    hidden_grad = upstream + norm_in_two
    hidden_low = hidden_grad.astype(jnp.bfloat16)
    out_grad_w = jnp.einsum(
        "thk,td->hkd", mixed_heads, hidden_low, preferred_element_type=jnp.float32
    )
    mixed_grad = jnp.einsum(
        "td,hkd->thk", hidden_low, out_full, preferred_element_type=jnp.float32
    ).astype(jnp.bfloat16)
    mixed_grad = mixed_grad * head_used[:, :, None].astype(jnp.bfloat16)
    scores = jnp.einsum("qhk,shk->hqs", query_rows, key_rows, preferred_element_type=jnp.float32)
    attn_probs = jnp.where(causal[None, :, :], jnp.exp(scores - log_total), 0.0)
    value_grad = jnp.einsum(
        "hqs,qhk->shk",
        attn_probs.astype(jnp.bfloat16),
        mixed_grad,
        preferred_element_type=jnp.float32,
    )
    prob_grad = jnp.einsum(
        "qhk,shk->hqs", mixed_grad, value_rows, preferred_element_type=jnp.float32
    )
    inner = jnp.sum(attn_probs * prob_grad, axis=-1, keepdims=True)
    score_grad = (attn_probs * (prob_grad - inner)).astype(jnp.bfloat16)
    query_grad = jnp.einsum(
        "hqs,shk->qhk", score_grad, key_rows, preferred_element_type=jnp.float32
    )
    key_grad = jnp.einsum(
        "hqs,qhk->shk", score_grad, query_rows, preferred_element_type=jnp.float32
    )
    qkv_low = jnp.stack(
        [
            rotate_back(query_grad * score_scale, cosine_table, sine_table),
            rotate_back(key_grad, cosine_table, sine_table),
            value_grad,
        ],
        axis=1,
    ).astype(jnp.bfloat16)
    qkv_grad_w = jnp.einsum("td,tchk->dchk", a_one, qkv_low, preferred_element_type=jnp.float32)
    ln_one_part = jnp.einsum("tchk,dchk->td", qkv_low, qkv_full, preferred_element_type=jnp.float32)
    ln_one_grad = lax.psum(ln_one_part.astype(jnp.bfloat16), "mp").astype(jnp.float32)
    norm_in_one, gain_one_grad, bias_one_grad = norm_back(
        scaled_one, inverse_one, norm_rows[0], ln_one_grad
    )
    input_grad = hidden_grad + norm_in_one
    small_grad = jnp.stack([gain_one_grad, gain_two_grad, bias_one_grad, bias_two_grad], axis=0)
    reduced = (
        lax.psum_scatter(qkv_grad_w, "dp", scatter_dimension=0, tiled=True),
        lax.psum_scatter(out_grad_w, "dp", scatter_dimension=2, tiled=True),
        lax.psum_scatter(up_grad_w, "dp", scatter_dimension=0, tiled=True),
        lax.psum_scatter(down_grad_w, "dp", scatter_dimension=1, tiled=True),
        lax.psum_scatter(router_grad_w, "dp", scatter_dimension=0, tiled=True),
        lax.psum_scatter(small_grad, "dp", scatter_dimension=1, tiled=True),
    )
    masters = (qkv_weight, out_weight, up_weight, down_weight, router_weight)
    firsts = (qkv_first, out_first, up_first, down_first, router_first)
    seconds = (qkv_second, out_second, up_second, down_second, router_second)
    shares = (1.0, 1.0, 1.0, 1.0, 1.0 / core_count)
    stepped = [
        moment_step(masters[index], reduced[index], firsts[index], seconds[index], DECAY_RATE)
        for index in range(5)
    ]
    weight_squares = jnp.stack(
        [jnp.sum(masters[index] * masters[index]) * shares[index] for index in range(5)]
    )
    update_squares = jnp.stack(
        [jnp.sum(stepped[index][2] * stepped[index][2]) * shares[index] for index in range(5)]
    )
    weight_sums, update_sums = lax.psum((weight_squares, update_squares), ("dp", "mp"))
    weight_norm = jnp.sqrt(weight_sums)
    update_norm = jnp.sqrt(update_sums)
    renewed = [
        masters[index] - LEARN_RATE * (weight_norm[index] / update_norm[index]) * stepped[index][2]
        for index in range(5)
    ]
    norm_moment, norm_square, norm_update = moment_step(
        norm_master, reduced[5], norm_first, norm_second, 0.0
    )
    norms_new = norm_master - NORM_RATE * norm_update
    lamb_norms = jnp.stack([weight_norm, update_norm], axis=1)
    return (
        block_output,
        input_grad,
        reduced[0],
        reduced[1],
        reduced[2],
        reduced[3],
        reduced[4],
        reduced[5],
        stepped[0][0],
        stepped[1][0],
        stepped[2][0],
        stepped[3][0],
        stepped[4][0],
        norm_moment,
        stepped[0][1],
        stepped[1][1],
        stepped[2][1],
        stepped[3][1],
        stepped[4][1],
        norm_square,
        renewed[0],
        renewed[1],
        renewed[2],
        renewed[3],
        renewed[4],
        norms_new,
        renewed[0].astype(jnp.bfloat16),
        renewed[1].astype(jnp.bfloat16),
        renewed[2].astype(jnp.bfloat16),
        renewed[3].astype(jnp.bfloat16),
        renewed[4].astype(jnp.bfloat16),
        norms_new.astype(jnp.bfloat16),
        lamb_norms,
    )


def solution(mesh):
    return jax.shard_map(
        local,
        mesh=mesh,
        in_specs=(
            P("dp", None),
            P("dp", None),
            P("dp"),
            P("dp"),
            P("dp"),
            P("dp"),
            P("dp", None, "mp", None),
            P("mp", None, "dp"),
            P("dp", "mp"),
            P("mp", "dp"),
            P("dp", None),
            P(None, "dp"),
            P(None, "dp"),
            P("dp", None, "mp", None),
            P("dp", None, "mp", None),
            P("mp", None, "dp"),
            P("mp", None, "dp"),
            P("dp", "mp"),
            P("dp", "mp"),
            P("mp", "dp"),
            P("mp", "dp"),
            P("dp", None),
            P("dp", None),
            P(None, "dp"),
            P(None, "dp"),
        ),
        out_specs=(
            P("dp", None),
            P("dp", None),
            P("dp", None, "mp", None),
            P("mp", None, "dp"),
            P("dp", "mp"),
            P("mp", "dp"),
            P("dp", None),
            P(None, "dp"),
            P("dp", None, "mp", None),
            P("mp", None, "dp"),
            P("dp", "mp"),
            P("mp", "dp"),
            P("dp", None),
            P(None, "dp"),
            P("dp", None, "mp", None),
            P("mp", None, "dp"),
            P("dp", "mp"),
            P("mp", "dp"),
            P("dp", None),
            P(None, "dp"),
            P("dp", None, "mp", None),
            P("mp", None, "dp"),
            P("dp", "mp"),
            P("mp", "dp"),
            P("dp", None),
            P(None, "dp"),
            P("dp", None, "mp", None),
            P("mp", None, "dp"),
            P("dp", "mp"),
            P("mp", "dp"),
            P("dp", None),
            P(None, "dp"),
            P(),
        ),
        check_vma=False,
    )
```

profile of v0, /device:TPU:0, one launch (start us, length us, event | category | flops | bytes accessed | tf_op | source)
XLA Modules:
  0.0 2985.2 jit_solution(6093478097075708168)
XLA Ops:
  11.4 178.1 %all-gather = bf16[64,32,4]{1,2,0:T(4,128)(2,1)S(1)} all-gather(bf16[1,32,4]{1,2,0:T(4,128)(2,1)S(1)} %fusion.105), channel_id=1, replica_groups=mesh['dp'=64,'mp'=2] {'dp'}, dimensions={0}, use_global_device_ids=true | all-gather | bytes 16640 | tf_op jit(solution)/shard_map/all_gather | solution.py:173
  194.8 8.3 fusion.91
  212.8 169.6 %all-gather.1 = bf16[64,32,4]{1,2,0:T(4,128)(2,1)S(1)} all-gather(bf16[1,32,4]{1,2,0:T(4,128)(2,1)S(1)} %get-tuple-element.331), channel_id=1, replica_groups=mesh['dp'=64,'mp'=2] {'dp'}, dimensions={0}, use_global_device_ids=true | all-gather | bytes 16640 | tf_op jit(solution)/shard_map/all_gather | solution.py:172
  397.6 9.5 all-to-all-done
  407.1 5.9 all-to-all-start.2
  414.4 22.4 all-to-all-done.2
  438.1 25.8 all-gather.13.cloned.1.call-done
  463.9 37.5 %conditional.2 = (bf16[256,2048]{1,0:T(8,128)(2,1)}, f32[256,4096]{1,0:T(8,128)}) conditional(s32[]{:T(128)} %clamp.4, () %tuple.32, (bf16[2048,4096]{1,0:T(8,128)(2,1)}, bf16[256,2048]{1,0:T(8,128)(2,1)S(1)}, bf16[4096,2048]{0,1:T(8,128)(2,1)}) %tuple.33, (bf16[256,2048]{1,0:T(8,128)(2,1)S(1)}, bf16[2048,4096]{1,0:T(8,128)(2,1)}, ...), branch_computations={%region_11.12_spmd, %region_12.13_spmd, %region_13.14_spmd} | conditional | flops 8593080320 | bytes 62914580 | solution.py:236
  464.0 22.6 copy.154
  486.5 5.7 fusion.2
  492.3 6.7 fusion
  503.8 80.2 %conditional.3 = (bf16[256,2048]{1,0:T(8,128)(2,1)}, f32[2048,4096]{0,1:T(8,128)}, f32[4096,2048]{1,0:T(8,128)}) conditional(s32[]{:T(128)} %clamp.4, () %tuple.35, (bf16[4096,2048]{0,1:T(8,128)(2,1)}, bf16[256,2048]{1,0:T(8,128)(2,1)S(1)}, f32[256,4096]{1,0:T(8,128)}, bf16[2048,4096]{1,0:T(8,128)(2,1)}, ...), branch_computations={%region_16.17_spmd, %region_17.18_spmd, %region_18.19_spmd} | conditional | flops 17187209216 | bytes 267386976 | solution.py:276
  518.5 22.6 copy.156
  541.1 6.5 fusion.19
  561.2 11.1 pad.10
  572.4 11.2 pad.11
  586.3 26.0 all-reduce.13.cloned.1.call-done
  612.3 29.4 all_to_all.20
  641.7 5.6 all-to-all-start.3
  649.1 15.2 all-to-all-done.3
  674.9 9.6 fusion.30
  686.3 18.3 all-reduce.11.cloned.1.call-done
  713.1 10.4 fusion.76
  723.5 31.2 %copy.168 = f32[2048,4096]{1,0:T(8,128)} copy(f32[2048,4096]{0,1:T(8,128)} %get-tuple-element.89) | data formatting | bytes 67108864 | tf_op jit(solution)/shard_map/cond | solution.py:276
  754.7 31.2 %copy.169 = f32[4096,2048]{0,1:T(8,128)} copy(f32[4096,2048]{1,0:T(8,128)} %get-tuple-element.90) | data formatting | bytes 67108864 | tf_op jit(solution)/shard_map/cond | solution.py:276
  787.6 273.6 %reduce-scatter.19.cloned.1.call-done = f32[32,4]{1,0:T(8,128)} async-done(((f32[2048,4]{1,0:T(8,128)}), f32[32,4]{1,0:T(8,128)}) %reduce-scatter.19.cloned.1.call-update) | async-done | bytes 528
  1065.4 345.1 %reduce-scatter.21.cloned.1.call-done = f32[32,4]{1,0:T(8,128)} async-done(((f32[2048,4]{1,0:T(8,128)}), f32[32,4]{1,0:T(8,128)}) %reduce-scatter.21.cloned.1.call-update) | async-done | bytes 528
  1411.9 364.0 %reduce-scatter.13.cloned.1.call-done = f32[8,128,32]{1,2,0:T(8,128)} async-done(((f32[8,128,2048]{1,2,0:T(8,128)}), f32[8,128,32]{1,2,0:T(8,128)}) %reduce-scatter.13.cloned.1.call-update) | async-done | bytes 131088 | tf_op jit(solution)/shard_map/reduce_scatter | solution.py:343
  1778.2 247.0 %reduce-scatter.11.cloned.1.call-done = f32[32,3,8,128]{3,0,2,1:T(8,128)} async-done(((f32[2048,3,8,128]{3,0,2,1:T(8,128)}), f32[32,3,8,128]{3,0,2,1:T(8,128)}) %reduce-scatter.11.cloned.1.call-update) | async-done | bytes 393232 | tf_op jit(solution)/shard_map/reduce_scatter | solution.py:342
  2030.1 427.1 %reduce-scatter.15.cloned.1.call-done = f32[32,4096]{1,0:T(8,128)} async-done(((f32[2048,4096]{1,0:T(8,128)}), f32[32,4096]{1,0:T(8,128)}) %reduce-scatter.15.cloned.1.call-update) | async-done | bytes 524304 | tf_op jit(solution)/shard_map/reduce_scatter | solution.py:344
  2459.3 430.0 %reduce-scatter.17.cloned.1.call-done = f32[4096,32]{0,1:T(8,128)} async-done(((f32[4096,2048]{0,1:T(8,128)}), f32[4096,32]{0,1:T(8,128)}) %reduce-scatter.17.cloned.1.call-update) | async-done | bytes 524304 | tf_op jit(solution)/shard_map/reduce_scatter | solution.py:345
  2899.0 62.1 %all-reduce.3 = (f32[5]{0:T(128)}, f32[5]{0:T(128)}) all-reduce(f32[5]{0:T(128)S(1)} %stack.90, f32[5]{0:T(128)S(1)} %stack.96), channel_id=1, replica_groups=mesh['dp'=64,'mp'=2] {'dp','mp'}, use_global_device_ids=true, to_apply=%region_42.43 | all-reduce | flops 10 | bytes 80 | tf_op jit(solution)/shard_map/psum | solution.py:363
  (308 shorter events, 114.0 us)
Async XLA Ops:
  7.2 187.6 %all-gather.7.cloned.1.call-start = ((), (), s32[]{:S(2)}) async-start(), calls=%async_computation.10 | async-start | bytes 12779520 | tf_op jit(solution)/shard_map/all_gather | solution.py:168
  9.0 196.0 %all-gather.9.cloned.1.call-start = ((), (), s32[]{:S(2)}) async-start(), calls=%async_computation.11 | async-start | bytes 4259840 | tf_op jit(solution)/shard_map/all_gather | solution.py:169
  10.7 372.5 %all-reduce.9.cloned.1.call-start = ((), (), s32[]{:S(2)}) async-start(), calls=%async_computation.12 | async-start | bytes 2097152 | tf_op jit(solution)/shard_map/psum | solution.py:204
  209.9 228.2 %all-gather.11.cloned.1.call-start = ((), (), s32[]{:S(2)}) async-start(), calls=%async_computation.13 | async-start | bytes 17039360 | tf_op jit(solution)/shard_map/all_gather | solution.py:170
  210.7 253.2 %all-gather.13.cloned.1.call-start = ((), (), s32[]{:S(2)}) async-start(), calls=%async_computation.14 | async-start | bytes 17039360 | tf_op jit(solution)/shard_map/all_gather | solution.py:171
  388.0 19.0 all-to-all-start
  407.1 29.7 all-to-all-start.2
  413.0 199.3 %all-reduce.13.cloned.1.call-start = ((), (), s32[]{:S(2)}) async-start(), calls=%async_computation.22 | async-start | bytes 4194304 | tf_op jit(solution)/shard_map/psum | solution.py:238
  641.7 22.6 all-to-all-start.3
  647.4 57.2 %all-reduce.11.cloned.1.call-start = ((), (), s32[]{:S(2)}) async-start(), calls=%async_computation.15 | async-start | bytes 1048576 | tf_op jit(solution)/shard_map/psum | solution.py:335
  684.5 376.7 %reduce-scatter.19.cloned.1.call-start = ((), (), s32[]{:S(2)}) async-start(), calls=%async_computation.20 | async-start | bytes 1064960
  686.3 724.2 %reduce-scatter.21.cloned.1.call-start = ((), (), s32[]{:S(2)}) async-start(), calls=%async_computation.21 | async-start | bytes 1064960
  707.6 1068.3 %reduce-scatter.13.cloned.1.call-start = ((), (), s32[]{:S(2)}) async-start(), calls=%async_computation.17 | async-start | bytes 8519680 | tf_op jit(solution)/shard_map/reduce_scatter | solution.py:343
  712.4 1312.8 %reduce-scatter.11.cloned.1.call-start = ((), (), s32[]{:S(2)}) async-start(), calls=%async_computation.16 | async-start | bytes 25559040 | tf_op jit(solution)/shard_map/reduce_scatter | solution.py:342
  723.5 1733.8 %reduce-scatter.15.cloned.1.call-start = ((), (), s32[]{:S(2)}) async-start(), calls=%async_computation.18 | async-start | bytes 34078720 | tf_op jit(solution)/shard_map/reduce_scatter | solution.py:344
  754.7 2134.6 %reduce-scatter.17.cloned.1.call-start = ((), (), s32[]{:S(2)}) async-start(), calls=%async_computation.19 | async-start | bytes 34078720 | tf_op jit(solution)/shard_map/reduce_scatter | solution.py:345
  785.9 278.0 %copy-start.27 = (bf16[128,2048]{1,0:T(8,128)(2,1)S(1)}, bf16[128,2048]{1,0:T(8,128)(2,1)}, u32[]{:S(2)}) copy-start(bf16[128,2048]{1,0:T(8,128)(2,1)} %all-reduce.11.cloned.1.call-done) | copy-start | bytes 1572868
  785.9 625.3 %copy-start.76 = (f32[2,32]{1,0:T(2,128)S(1)}, f32[2,32]{1,0:T(2,128)}, u32[]{:S(2)}) copy-start(f32[2,32]{1,0:T(2,128)} %param.43) | copy-start | bytes 772
  785.9 625.3 %copy-start.77 = (f32[2,32]{1,0:T(2,128)S(1)}, f32[2,32]{1,0:T(2,128)}, u32[]{:S(2)}) copy-start(f32[2,32]{1,0:T(2,128)} %param.42) | copy-start | bytes 772
  786.0 625.3 %copy-start.78 = (f32[4,32]{1,0:T(4,128)S(1)}, f32[4,32]{1,0:T(4,128)}, u32[]{:S(2)}) copy-start(f32[4,32]{1,0:T(4,128)} %param.55) | copy-start | bytes 1540
  786.0 625.3 %copy-start.79 = (f32[4,32]{1,0:T(4,128)S(1)}, f32[4,32]{1,0:T(4,128)}, u32[]{:S(2)}) copy-start(f32[4,32]{1,0:T(4,128)} %param.54) | copy-start | bytes 1540
  786.0 989.9 %copy-start.28 = (f32[8,128,32]{1,2,0:T(8,128)S(1)}, f32[8,128,32]{1,2,0:T(8,128)}, u32[]{:S(2)}) copy-start(f32[8,128,32]{1,2,0:T(8,128)} %param.38) | copy-start | bytes 393220
  786.0 989.9 %copy-start.46 = (f32[8,128,32]{1,2,0:T(8,128)S(1)}, f32[8,128,32]{1,2,0:T(8,128)}, u32[]{:S(2)}) copy-start(f32[8,128,32]{1,2,0:T(8,128)} %param.47) | copy-start | bytes 393220
  786.0 989.9 %copy-start.47 = (f32[8,128,32]{1,2,0:T(8,128)S(1)}, f32[8,128,32]{1,2,0:T(8,128)}, u32[]{:S(2)}) copy-start(f32[8,128,32]{1,2,0:T(8,128)} %param.46) | copy-start | bytes 393220
  787.6 1669.6 %copy-start.14 = (f32[32,4096]{1,0:T(8,128)S(1)}, f32[32,4096]{1,0:T(8,128)}, u32[]{:S(2)}) copy-start(f32[32,4096]{1,0:T(8,128)} %param.39) | copy-start | bytes 1572868
  1062.0 1397.3 %copy-start.67 = (f32[32,4]{0,1:T(4,128)}, f32[32,4]{0,1:T(4,128)S(1)}, u32[]{:S(2)}) copy-start(f32[32,4]{0,1:T(4,128)S(1)} %copy.200) | copy-start | bytes 1540
  1065.4 1391.9 %copy-start.38 = (f32[32,4096]{1,0:T(8,128)S(1)}, f32[32,4096]{1,0:T(8,128)}, u32[]{:S(2)}) copy-start(f32[32,4096]{1,0:T(8,128)} %param.49) | copy-start | bytes 1572868
  1065.4 1823.9 %copy-start.12 = (f32[4096,32]{0,1:T(8,128)S(1)}, f32[4096,32]{0,1:T(8,128)}, u32[]{:S(2)}) copy-start(f32[4096,32]{0,1:T(8,128)} %param.40) | copy-start | bytes 1572868
  1411.3 1480.4 %copy-start.66 = (f32[4,32]{1,0:T(4,128)}, f32[4,32]{1,0:T(4,128)S(1)}, u32[]{:S(2)}) copy-start(f32[4,32]{1,0:T(4,128)S(1)} %copy.202) | copy-start | bytes 1540
  1778.2 679.0 %copy-start.39 = (f32[32,4096]{1,0:T(8,128)S(1)}, f32[32,4096]{1,0:T(8,128)}, u32[]{:S(2)}) copy-start(f32[32,4096]{1,0:T(8,128)} %param.48) | copy-start | bytes 1572868
  2459.3 518.0 %copy-start.23 = (f32[32,4096]{1,0:T(8,128)}, f32[32,4096]{1,0:T(8,128)S(1)}, u32[]{:S(2)}) copy-start(f32[32,4096]{1,0:T(8,128)S(1)} %get-tuple-element.297) | copy-start | bytes 1572868
  2459.3 518.0 %copy-start.24 = (f32[32,4096]{1,0:T(8,128)}, f32[32,4096]{1,0:T(8,128)S(1)}, u32[]{:S(2)}) copy-start(f32[32,4096]{1,0:T(8,128)S(1)} %get-tuple-element.298) | copy-start | bytes 1572868
  (69 other events, 2479.7 us)
Sparse Core Ops, SparseCore 0:
  11.3 106.4 all-gather.6
  121.0 72.1 all-gather.8
  210.0 18.4 all-reduce.8
  232.3 105.9 all-gather.10
  342.0 121.8 all-gather.12
  586.4 25.8 all-reduce.12
  684.6 19.9 all-reduce.10
  707.6 353.5 reduce-scatter.18
  1063.6 346.8 reduce-scatter.20
  1413.4 362.4 reduce-scatter.12
  1781.3 243.8 reduce-scatter.10
  2028.2 429.0 reduce-scatter.14
  2460.3 428.8 reduce-scatter.16
where the time goes:
time: 3000 us; the launch traced here: 2990 us
  waiting for transfers between devices  2200 us (73%)
  blocking collectives  439 us (15%)
  local copies, waits for them, and re-layouts  170 us (6%)
  matrix products  75.4 us (3%)
  other arithmetic  40.1 us (1%)
    unnamed x15, waiting for transfers between devices  619 us
    reduce_scatter x1, waiting for transfers between devices, local(): lax.psum_scatter(down_grad_w, 'dp', scatter_dimension=1, tiled=True)  430 us
    reduce_scatter x1, waiting for transfers between devices, local(): lax.psum_scatter(up_grad_w, 'dp', scatter_dimension=0, tiled=True)  427 us
    reduce_scatter x1, waiting for transfers between devices, local(): lax.psum_scatter(out_grad_w, 'dp', scatter_dimension=2, tiled=True)  364 us
    reduce_scatter x1, waiting for transfers between devices, local(): lax.psum_scatter(qkv_grad_w, 'dp', scatter_dimension=0, tiled=True)  247 us
    all_gather x1, blocking collectives, local(): lax.all_gather(norm_master.astype(jnp.bfloat16), 'dp', axis=1, tiled=True)  178 us
    all_gather x1, blocking collectives, local(): lax.all_gather(router_weight.astype(jnp.bfloat16), 'dp', axis=0, tiled=True)  170 us
    cond x2, local copies, waits for them, and re-layouts, local(): lax.switch(used_quarters, backward_cases, arrived, arrived_grad, pre_act,...  62.3 us
  transfers between devices with their start and end apart: 16, of which 12 were waited for; matrix products, arithmetic and copies ran while one was open for 4% of the time, Pallas kernels for 0%

commit v1 on v0

v1 whole, which is shorter than its diff:
```python
from functools import partial

import jax
import jax.numpy as jnp
from jax import lax
from jax.experimental import pallas as pl
from jax.experimental.pallas import tpu as pltpu
from jax.sharding import PartitionSpec as P

STEP = 5

HIGHEST = lax.Precision.HIGHEST
BETA_ONE = 0.5
BETA_TWO = 0.5
ADAM_EPS = 1e-06
DECAY_RATE = 0.01
LEARN_RATE = 0.5
NORM_RATE = 0.1
NORM_EPS = 1e-05
ROPE_BASE = 10000.0

MESH = pl.DeviceIdType.MESH
BF16 = jnp.bfloat16
F32 = jnp.float32
VMEM = pl.BlockSpec(memory_space=pltpu.VMEM)
ANY = pl.BlockSpec(memory_space=pl.ANY)
DMA = pltpu.SemaphoreType.DMA

EXTRA, QKV, OUT, UP, DOWN = (0, 128), (128, 896), (896, 1152), (1152, 2176), (2176, 3200)
WIDE = 3200
SPLIT = 1536


def place():
    index = lax.axis_index("dp")
    return lax.div(index, 16), lax.rem(lax.div(index, 4), 4), lax.rem(index, 4), lax.axis_index("mp")


def ring(value, step):
    return lax.rem(value + (step + 4), 4)


def device(x, y, z, core):
    return (x * 16 + y * 4 + z, core)


def greet(peers):
    barrier = pltpu.get_barrier_semaphore()
    for peer in peers:
        pl.semaphore_signal(barrier, inc=1, device_id=peer, device_id_type=MESH)
    pl.semaphore_wait(barrier, len(peers))


def send(src, dst, send_sem, recv_sem, peer):
    copy = pltpu.make_async_remote_copy(
        src_ref=src, dst_ref=dst, send_sem=send_sem, recv_sem=recv_sem, device_id=peer, device_id_type=MESH
    )
    copy.start()
    return copy


def gather_kernel(packed, meta, full, metas, z_send, z_recv, m_send, m_recv, own_sem, p_send, p_recv):
    x, y, z, core = place()
    z_peers = [device(x, y, ring(z, k), core) for k in (1, 2, 3)]
    xp, xm = device(ring(x, 1), y, z, core), device(ring(x, -1), y, z, core)
    yp, ym = device(x, ring(y, 1), z, core), device(x, ring(y, -1), z, core)
    greet(z_peers + [xp, xm, yp, ym])
    rows = pl.ds(pl.multiple_of(z * 32, 32), 32)
    flying = []
    for k in (2, 1, 3):
        flying.append(
            send(packed.at[ring(z, k)], full.at[x, y, rows, :], z_send.at[k - 1], z_recv.at[k - 1], z_peers[k - 1])
        )
        flying.append(send(meta, metas.at[z], m_send.at[k - 1], m_recv.at[k - 1], z_peers[k - 1]))
    own = pltpu.make_async_copy(packed.at[z], full.at[x, y, rows, :], own_sem.at[0])
    own.start()
    own_meta = pltpu.make_async_copy(meta, metas.at[z], own_sem.at[1])
    own_meta.start()
    for copy in flying:
        copy.wait()
    own.wait()
    own_meta.wait()
    low, high = pl.ds(0, 64), pl.ds(64, 64)
    every = slice(None)
    first, second = pl.ds(0, SPLIT), pl.ds(SPLIT, WIDE - SPLIT)

    def step(number, moves):
        copies = []
        for index, (where, peer) in enumerate(moves):
            part = full.at[where]
            copies.append(send(part, part, p_send.at[number, index], p_recv.at[number, index], peer))
        for copy in copies:
            copy.wait()

    x_before, x_after, y_before, y_after = ring(x, -1), ring(x, 1), ring(y, -1), ring(y, 1)
    step(0, [
        ((x, y, every, first), xp), ((x, y, every, first), xm),
        ((x, y, every, second), yp), ((x, y, every, second), ym),
    ])
    step(1, [
        ((x_before, y, low, first), xp), ((x_after, y, high, first), xm),
        ((x, y_before, low, second), yp), ((x, y_after, high, second), ym),
    ])
    step(2, [
        ((every, y, every, first), yp), ((every, y, every, first), ym),
        ((x, every, every, second), xp), ((x, every, every, second), xm),
    ])
    step(3, [
        ((every, y_before, low, first), yp), ((every, y_after, high, first), ym),
        ((x_before, every, low, second), xp), ((x_after, every, high, second), xm),
    ])


def gather_weights(packed, meta):
    return pl.pallas_call(
        gather_kernel,
        out_shape=(
            jax.ShapeDtypeStruct((4, 4, 128, WIDE), BF16),
            jax.ShapeDtypeStruct((4, 8, 128), F32),
        ),
        in_specs=[ANY, ANY],
        out_specs=(ANY, ANY),
        scratch_shapes=[DMA((3,)), DMA((3,)), DMA((3,)), DMA((3,)), DMA((2,)), DMA((4, 4)), DMA((4, 4))],
        compiler_params=pltpu.CompilerParams(collective_id=0, has_side_effects=True),
        name="gather_weights",
    )(packed, meta)


def add_into(target, target_at, source, source_at, blocks, row, count, columns, width):
    def one(index, carry):
        xi = index // (count // 16)
        step = pl.multiple_of(lax.rem(index, count // 16) * 16, 16)
        to = target_at(xi) + (pl.ds(row + step, 16), columns)
        here = target[to].astype(F32)
        for ref, first_row in source:
            here = here + ref[source_at(xi) + (pl.ds(first_row + step, 16), pl.ds(0, width))].astype(F32)
        target[to] = here.astype(BF16)
        return carry

    lax.fori_loop(0, blocks * (count // 16), one, 0)


def scatter_kernel(
    grads_in, out, grads, one_a, one_b, two_a, two_b, one_c, one_d, two_c, two_d, load_sem, s_send, s_recv, z_send, z_recv, own_sem
):
    x, y, z, core = place()
    z_peers = [device(x, y, ring(z, k), core) for k in (1, 2, 3)]
    xp, xm = device(ring(x, 1), y, z, core), device(ring(x, -1), y, z, core)
    yp, ym = device(x, ring(y, 1), z, core), device(x, ring(y, -1), z, core)
    load = pltpu.make_async_copy(grads_in, grads, load_sem)
    load.start()
    greet(z_peers + [xp, xm, yp, ym])
    load.wait()
    low, high = pl.ds(0, 64), pl.ds(64, 64)
    every = slice(None)
    first, second = pl.ds(0, SPLIT), pl.ds(SPLIT, WIDE - SPLIT)
    wa, wb = SPLIT, WIDE - SPLIT
    x_before, x_after, y_before, y_after = ring(x, -1), ring(x, 1), ring(y, -1), ring(y, 1)
    x_far, y_far = ring(x, 2), ring(y, 2)

    def go(number, index, where, dst, peer):
        return send(grads.at[where], dst, s_send.at[number, index], s_recv.at[number, index], peer)

    halves = [
        go(0, 0, (every, y_far, low, first), one_a.at[0], yp),
        go(0, 1, (every, y_far, high, first), one_a.at[1], ym),
        go(0, 2, (x_far, every, low, second), one_b.at[0], xp),
        go(0, 3, (x_far, every, high, second), one_b.at[1], xm),
    ]
    rest = [
        go(0, 4, (every, y_after, high, first), two_a.at[0, :, high, :], yp),
        go(0, 5, (every, y_before, low, first), two_a.at[1, :, low, :], ym),
        go(0, 6, (x_after, every, high, second), two_b.at[0, :, high, :], xp),
        go(0, 7, (x_before, every, low, second), two_b.at[1, :, low, :], xm),
    ]
    halves[0].wait()
    add_into(grads, lambda i: (i, y_after), [(one_a.at[0], 0)], lambda i: (i,), 4, 0, 64, first, wa)
    last = [go(0, 8, (every, y_after, low, first), two_a.at[0, :, low, :], yp)]
    halves[2].wait()
    add_into(grads, lambda i: (x_after, i), [(one_b.at[0], 0)], lambda i: (i,), 4, 0, 64, second, wb)
    last.append(go(0, 9, (x_after, every, low, second), two_b.at[0, :, low, :], xp))
    halves[1].wait()
    add_into(grads, lambda i: (i, y_before), [(one_a.at[1], 0)], lambda i: (i,), 4, 64, 64, first, wa)
    last.append(go(0, 10, (every, y_before, high, first), two_a.at[1, :, high, :], ym))
    halves[3].wait()
    add_into(grads, lambda i: (x_before, i), [(one_b.at[1], 0)], lambda i: (i,), 4, 64, 64, second, wb)
    last.append(go(0, 11, (x_before, every, high, second), two_b.at[1, :, high, :], xm))
    for copy in rest + last:
        copy.wait()
    add_into(grads, lambda i: (i, y), [(two_a.at[0], 0), (two_a.at[1], 0)], lambda i: (i,), 4, 0, 128, first, wa)
    add_into(grads, lambda i: (x, i), [(two_b.at[0], 0), (two_b.at[1], 0)], lambda i: (i,), 4, 0, 128, second, wb)

    halves = [
        go(1, 0, (x_far, y, low, first), one_c.at[0], xp),
        go(1, 1, (x_far, y, high, first), one_c.at[1], xm),
        go(1, 2, (x, y_far, low, second), one_d.at[0], yp),
        go(1, 3, (x, y_far, high, second), one_d.at[1], ym),
    ]
    rest = [
        go(1, 4, (x_after, y, high, first), two_c.at[0, high, :], xp),
        go(1, 5, (x_before, y, low, first), two_c.at[1, low, :], xm),
        go(1, 6, (x, y_after, high, second), two_d.at[0, high, :], yp),
        go(1, 7, (x, y_before, low, second), two_d.at[1, low, :], ym),
    ]
    halves[0].wait()
    add_into(grads, lambda i: (x_after, y), [(one_c.at[0], 0)], lambda i: (), 1, 0, 64, first, wa)
    last = [go(1, 8, (x_after, y, low, first), two_c.at[0, low, :], xp)]
    halves[2].wait()
    add_into(grads, lambda i: (x, y_after), [(one_d.at[0], 0)], lambda i: (), 1, 0, 64, second, wb)
    last.append(go(1, 9, (x, y_after, low, second), two_d.at[0, low, :], yp))
    halves[1].wait()
    add_into(grads, lambda i: (x_before, y), [(one_c.at[1], 0)], lambda i: (), 1, 64, 64, first, wa)
    last.append(go(1, 10, (x_before, y, high, first), two_c.at[1, high, :], xm))
    halves[3].wait()
    add_into(grads, lambda i: (x, y_before), [(one_d.at[1], 0)], lambda i: (), 1, 64, 64, second, wb)
    last.append(go(1, 11, (x, y_before, high, second), two_d.at[1, high, :], ym))
    for copy in rest + last:
        copy.wait()
    add_into(grads, lambda i: (x, y), [(two_c.at[0], 0), (two_c.at[1], 0)], lambda i: (), 1, 0, 128, first, wa)
    add_into(grads, lambda i: (x, y), [(two_d.at[0], 0), (two_d.at[1], 0)], lambda i: (), 1, 0, 128, second, wb)

    copies = []
    for k in (2, 1, 3):
        rows = pl.ds(pl.multiple_of(ring(z, k) * 32, 32), 32)
        copies.append(send(grads.at[x, y, rows, :], out.at[z], z_send.at[k - 1], z_recv.at[k - 1], z_peers[k - 1]))
    rows = pl.ds(pl.multiple_of(z * 32, 32), 32)
    own = pltpu.make_async_copy(grads.at[x, y, rows, :], out.at[z], own_sem)
    own.start()
    for copy in copies:
        copy.wait()
    own.wait()


def scatter_gradients(grads):
    wa, wb = SPLIT, WIDE - SPLIT
    return pl.pallas_call(
        scatter_kernel,
        out_shape=jax.ShapeDtypeStruct((4, 32, WIDE), BF16),
        in_specs=[ANY],
        out_specs=VMEM,
        scratch_shapes=[
            pltpu.VMEM((4, 4, 128, WIDE), BF16),
            pltpu.VMEM((2, 4, 64, wa), BF16),
            pltpu.VMEM((2, 4, 64, wb), BF16),
            pltpu.VMEM((2, 4, 128, wa), BF16),
            pltpu.VMEM((2, 4, 128, wb), BF16),
            pltpu.VMEM((2, 64, wa), BF16),
            pltpu.VMEM((2, 64, wb), BF16),
            pltpu.VMEM((2, 128, wa), BF16),
            pltpu.VMEM((2, 128, wb), BF16),
            DMA, DMA((2, 12)), DMA((2, 12)), DMA((3,)), DMA((3,)), DMA,
        ],
        compiler_params=pltpu.CompilerParams(collective_id=1, has_side_effects=True, vmem_limit_bytes=56 * 2**20),
        name="scatter_gradients",
    )(grads)


def spread_kernel(count, *refs):
    ins, outs = refs[:count], refs[count : 2 * count]
    own_sem, z_send, z_recv, c_send, c_recv = refs[2 * count :]
    x, y, z, core = place()
    z_peers = [device(x, y, ring(z, k), core) for k in (1, 2, 3)]
    partner = device(x, y, z, 1 - core)
    greet(z_peers + [partner])
    half = pl.ds(pl.multiple_of(core * 1024, 1024), 1024)
    flying, own = [], []
    for a in range(count):
        for k in (2, 1, 3):
            flying.append(
                (a, k, send(ins[a].at[:, half], outs[a].at[z, :, half], z_send.at[a, k - 1], z_recv.at[a, k - 1],
                            z_peers[k - 1]))
            )
    for a in range(count):
        own.append(pltpu.make_async_copy(ins[a], outs[a].at[z], own_sem.at[a]))
        own[-1].start()
    passed = []
    for a, k, copy in flying:
        copy.wait_recv()
        part = outs[a].at[ring(z, -k), :, half]
        passed.append(send(part, part, c_send.at[a, k - 1], c_recv.at[a, k - 1], partner))
    for copy in own:
        copy.wait()
    for _, _, copy in flying:
        copy.wait_send()
    for copy in passed:
        copy.wait()


def spread_rows(number, *arrays):
    count = len(arrays)
    return pl.pallas_call(
        partial(spread_kernel, count),
        out_shape=(jax.ShapeDtypeStruct((4, 128, 2048), BF16),) * count,
        in_specs=[VMEM] * count,
        out_specs=(VMEM,) * count,
        scratch_shapes=[DMA((count,)), DMA((count, 3)), DMA((count, 3)), DMA((count, 3)), DMA((count, 3))],
        compiler_params=pltpu.CompilerParams(
            collective_id=number, has_side_effects=True, vmem_limit_bytes=40 * 2**20
        ),
        name=f"spread_rows_{number}",
    )(*arrays)


def merge_kernel(count, *refs):
    parts, outs = refs[:count], refs[count : 2 * count]
    c_out, c_in, z_out, z_in, kept, c_send, c_recv, z_send, z_recv, e_send, e_recv = refs[2 * count :]
    x, y, z, core = place()
    z_peers = [device(x, y, ring(z, k), core) for k in (1, 2, 3)]
    partner = device(x, y, z, 1 - core)
    mine = pl.ds(pl.multiple_of(core * 1024, 1024), 1024)
    other = pl.ds(pl.multiple_of((1 - core) * 1024, 1024), 1024)
    order = (2, 1, 3, 0)
    for a in range(count):
        for j, k in enumerate(order):
            c_out[a, j] = parts[a][ring(z, k), :, other].astype(BF16)
    greet(z_peers + [partner])
    crossing = [
        [send(c_out.at[a, j], c_in.at[a, j], c_send.at[a, j], c_recv.at[a, j], partner) for j in range(4)]
        for a in range(count)
    ]
    flying = []
    for a in range(count):
        for j, k in enumerate(order):
            crossing[a][j].wait()
            joined = parts[a][ring(z, k), :, mine] + c_in[a, j].astype(F32)
            if k:
                z_out[a, j] = joined.astype(BF16)
                flying.append(
                    (a, j, send(z_out.at[a, j], z_in.at[a, j], z_send.at[a, j], z_recv.at[a, j], z_peers[k - 1]))
                )
            else:
                kept[a] = joined
    ends = []
    for a in range(count):
        for b, j, copy in flying:
            if b == a:
                copy.wait()
        outs[a][:, mine] = kept[a] + z_in[a, 0].astype(F32) + z_in[a, 1].astype(F32) + z_in[a, 2].astype(F32)
        part = outs[a].at[:, mine]
        ends.append(send(part, part, e_send.at[a], e_recv.at[a], partner))
    for copy in ends:
        copy.wait()


def merge_rows(number, *arrays):
    count = len(arrays)
    return pl.pallas_call(
        partial(merge_kernel, count),
        out_shape=(jax.ShapeDtypeStruct((128, 2048), F32),) * count,
        in_specs=[VMEM] * count,
        out_specs=(VMEM,) * count,
        scratch_shapes=[
            pltpu.VMEM((count, 4, 128, 1024), BF16),
            pltpu.VMEM((count, 4, 128, 1024), BF16),
            pltpu.VMEM((count, 3, 128, 1024), BF16),
            pltpu.VMEM((count, 3, 128, 1024), BF16),
            pltpu.VMEM((count, 128, 1024), F32),
            DMA((count, 4)), DMA((count, 4)), DMA((count, 3)), DMA((count, 3)), DMA((count,)), DMA((count,)),
        ],
        compiler_params=pltpu.CompilerParams(
            collective_id=number, has_side_effects=True, vmem_limit_bytes=48 * 2**20
        ),
        name=f"merge_rows_{number}",
    )(*arrays)


def total_kernel(value, out, slots, t_send, t_recv):
    x, y, z, core = place()
    along = (
        [device(x, y, z, 1 - core)],
        [device(x, y, ring(z, k), core) for k in (1, 2, 3)],
        [device(x, ring(y, k), z, core) for k in (1, 2, 3)],
        [device(ring(x, k), y, z, core) for k in (1, 2, 3)],
    )
    greet([peer for peers in along for peer in peers])
    out[...] = value[...]
    for axis, (me, peers) in enumerate(zip((core, z, y, x), along)):
        slots[axis, me] = out[...]
        here = slots.at[axis, me]
        copies = [
            send(here, here, t_send.at[axis, k], t_recv.at[axis, k], peer) for k, peer in enumerate(peers)
        ]
        for copy in copies:
            copy.wait()
        result = slots[axis, 0]
        for k in range(1, len(peers) + 1):
            result = result + slots[axis, k]
        out[...] = result


def total(value):
    return pl.pallas_call(
        total_kernel,
        out_shape=jax.ShapeDtypeStruct((8, 128), F32),
        in_specs=[VMEM],
        out_specs=VMEM,
        scratch_shapes=[pltpu.VMEM((4, 4, 8, 128), F32), DMA((4, 3)), DMA((4, 3))],
        compiler_params=pltpu.CompilerParams(collective_id=2, has_side_effects=True),
        name="total",
    )(value)


def layer_norm(value, gain_row, shift_row):
    centre = value - jnp.mean(value, axis=-1, keepdims=True)
    spread = jnp.mean(centre * centre, axis=-1, keepdims=True)
    inverse = lax.rsqrt(spread + NORM_EPS)
    scaled = centre * inverse
    return (scaled * gain_row + shift_row, scaled, inverse)


def norm_back(scaled, inverse, gain_row, upstream):
    dscaled = upstream * gain_row
    inner = (
        dscaled
        - jnp.mean(dscaled, axis=-1, keepdims=True)
        - scaled * jnp.mean(dscaled * scaled, axis=-1, keepdims=True)
    )
    return (inner * inverse, jnp.sum(upstream * scaled, axis=0), jnp.sum(upstream, axis=0))


def rotary_tables(length, size):
    half_size = size // 2
    frequency = ROPE_BASE ** (-(jnp.arange(half_size, dtype=F32) * 2.0 / size))
    angles = jnp.arange(length, dtype=F32)[:, None] * frequency[None, :]
    cosine_table = jnp.concatenate([jnp.cos(angles), jnp.cos(angles)], axis=-1)
    sine_table = jnp.concatenate([jnp.sin(angles), jnp.sin(angles)], axis=-1)
    return (cosine_table[:, None, :], sine_table[:, None, :])


def rotate(value, cosine_table, sine_table):
    half_size = value.shape[-1] // 2
    turned = jnp.concatenate([-value[..., half_size:], value[..., :half_size]], axis=-1)
    return value * cosine_table + turned * sine_table


def rotate_back(gradient, cosine_table, sine_table):
    half_size = gradient.shape[-1] // 2
    moved = gradient * sine_table
    turned = jnp.concatenate([moved[..., half_size:], -moved[..., :half_size]], axis=-1)
    return gradient * cosine_table + turned


def soft_choice(logits):
    row_top = jnp.max(logits, axis=-1, keepdims=True)
    exponent = jnp.exp(logits - row_top)
    return exponent / jnp.sum(exponent, axis=-1, keepdims=True)


def moment_step(weight, gradient, first_moment, second_moment, decay_rate):
    first_moment = BETA_ONE * first_moment + (1.0 - BETA_ONE) * gradient
    second_moment = BETA_TWO * second_moment + (1.0 - BETA_TWO) * gradient * gradient
    update = (
        first_moment
        / (1.0 - BETA_ONE**STEP)
        / (jnp.sqrt(second_moment / (1.0 - BETA_TWO**STEP)) + ADAM_EPS)
        + decay_rate * weight
    )
    return (first_moment, second_moment, update)


def dot(left, right, dims):
    return lax.dot_general(left, right, ((dims[:1], dims[1:]), ((), ())), preferred_element_type=F32)


def local(
    block_input,
    cotangent,
    head_count,
    width_route,
    forced_width,
    slot_index,
    qkv_weight,
    out_weight,
    up_weight,
    down_weight,
    router_weight,
    norm_gains,
    norm_biases,
    qkv_first,
    qkv_second,
    out_first,
    out_second,
    up_first,
    up_second,
    down_first,
    down_second,
    router_first,
    router_second,
    norm_first,
    norm_second,
):
    core = lax.axis_index("mp")
    z = lax.rem(lax.axis_index("dp"), 4)
    norm_master = jnp.concatenate([norm_gains, norm_biases], axis=0)
    bucket = jnp.where(forced_width[0] < 4, forced_width[0], width_route)
    kept_float = (slot_index >= 0).astype(F32)

    extra = jnp.concatenate([router_weight, norm_master.T, jnp.zeros((32, 120), F32)], axis=1).astype(BF16)
    packed = jnp.concatenate(
        [
            jnp.broadcast_to(extra[None], (4, 32, 128)),
            qkv_weight.astype(BF16).reshape(32, 3, 4, 2, 128).transpose(2, 0, 1, 3, 4).reshape(4, 32, 768),
            out_weight.astype(BF16).transpose(2, 0, 1).reshape(32, 4, 256).transpose(1, 0, 2),
            up_weight.astype(BF16).reshape(32, 4, 1024).transpose(1, 0, 2),
            down_weight.T.astype(BF16).reshape(32, 4, 1024).transpose(1, 0, 2),
        ],
        axis=2,
    )
    meta = jnp.concatenate(
        [head_count.astype(F32)[None], bucket.astype(F32)[None], jnp.zeros((6, 128), F32)], axis=0
    )
    full, metas = gather_weights(packed, meta)
    full = full.reshape(2048, WIDE)
    qkv_full, out_full, up_full, down_full = (full[:, a:b] for a, b in (QKV, OUT, UP, DOWN))
    small = full[:, :8].astype(F32).T
    router_rows, norm_rows = small[:4].astype(BF16), small[4:]
    head_all = metas[:, 0, :].reshape(512)
    bucket_all = metas[:, 1, :].reshape(512)

    inputs = block_input.astype(F32)
    ln_one, scaled_one, inverse_one = layer_norm(inputs, norm_rows[0], norm_rows[2])
    (a_one,) = spread_rows(3, ln_one.astype(BF16))
    a_one = a_one.reshape(512, 2048)
    qkv = dot(a_one, qkv_full, (1, 0)).reshape(4, 128, 3, 2, 128)
    cosine_table, sine_table = rotary_tables(128, 128)
    score_scale = 128 ** (-0.5)
    query_rows = (rotate(qkv[:, :, 0], cosine_table, sine_table) * score_scale).astype(BF16)
    key_rows = rotate(qkv[:, :, 1], cosine_table, sine_table).astype(BF16)
    value_rows = qkv[:, :, 2].astype(BF16)
    positions = jnp.arange(128, dtype=jnp.int32)
    causal = positions[:, None] >= positions[None, :]
    scores = jnp.einsum("nqhk,nshk->nhqs", query_rows, key_rows, preferred_element_type=F32)
    attn_probs = soft_choice(jnp.where(causal, scores, -1e30))
    probs_low = attn_probs.astype(BF16)
    heads_out = jnp.einsum("nhqs,nshk->nqhk", probs_low, value_rows, preferred_element_type=F32)
    head_ids = (core * 8 + z * 2 + jnp.arange(2, dtype=jnp.int32)).astype(F32)
    head_used = (head_ids[None, :] < head_all[:, None]).astype(F32)
    mixed = (heads_out.reshape(512, 2, 128) * head_used[:, :, None]).astype(BF16).reshape(512, 256)
    (attention,) = merge_rows(4, dot(mixed, out_full, (1, 1)).reshape(4, 128, 2048))
    hidden = inputs + attention

    ln_two, scaled_two, inverse_two = layer_norm(hidden, norm_rows[1], norm_rows[3])
    a_two_own = ln_two.astype(BF16)
    router = soft_choice(dot(a_two_own, router_rows, (1, 1)))
    bucket_onehot = (bucket[:, None] == jnp.arange(4, dtype=jnp.int32)[None, :]).astype(F32)
    gate_value = jnp.sum(router * bucket_onehot, axis=-1)
    upstream = cotangent.astype(F32)
    branch_grad = (upstream * gate_value[:, None] * kept_float[:, None]).astype(BF16)
    a_two, branch_rows = spread_rows(5, a_two_own, branch_grad)
    a_two, branch_rows = a_two.reshape(512, 2048), branch_rows.reshape(512, 2048)

    unit_ids = core * 4096 + z * 1024 + jnp.arange(1024, dtype=jnp.int32)
    used = (unit_ids.astype(F32)[None, :] < (bucket_all[:, None] + 1.0) * 2048.0).astype(F32)
    up_value = jax.nn.relu(dot(a_two, up_full, (1, 0))) * used
    activation = jnp.square(up_value).astype(BF16)
    up_low = (dot(branch_rows, down_full, (1, 0)) * 2.0 * up_value).astype(BF16)
    produced = dot(activation, down_full, (1, 1)).reshape(4, 128, 2048)
    row_part = dot(up_low, up_full, (1, 1)).reshape(4, 128, 2048)
    produced, row_sum = merge_rows(6, produced, row_part)
    branch_out = produced.astype(BF16).astype(F32) * kept_float[:, None]
    block_output = (hidden + gate_value[:, None] * branch_out).astype(BF16)
    gate_grad = jnp.sum(upstream * branch_out, axis=-1)
    logit_grad = router * (bucket_onehot - gate_value[:, None]) * gate_grad[:, None]
    ln_two_grad = row_sum.astype(BF16).astype(F32) + jnp.dot(
        logit_grad, router_rows.astype(F32), precision=HIGHEST
    )
    router_grad_w = lax.dot_general(
        logit_grad, a_two_own.astype(F32), (((0,), (0,)), ((), ())), precision=HIGHEST
    )
    norm_in_two, gain_two_grad, bias_two_grad = norm_back(scaled_two, inverse_two, norm_rows[1], ln_two_grad)
    hidden_grad = upstream + norm_in_two
    (hidden_low,) = spread_rows(7, hidden_grad.astype(BF16))
    hidden_low = hidden_low.reshape(512, 2048)

    used_low = head_used.astype(BF16)[:, :, None]
    mixed_grad = (dot(hidden_low, out_full, (1, 0)).astype(BF16).reshape(512, 2, 128) * used_low).reshape(
        4, 128, 2, 128
    )
    value_grad = jnp.einsum("nhqs,nqhk->nshk", probs_low, mixed_grad, preferred_element_type=F32)
    prob_grad = jnp.einsum("nqhk,nshk->nhqs", mixed_grad, value_rows, preferred_element_type=F32)
    inner = jnp.sum(attn_probs * prob_grad, axis=-1, keepdims=True)
    score_grad = (attn_probs * (prob_grad - inner)).astype(BF16)
    query_grad = jnp.einsum("nhqs,nshk->nqhk", score_grad, key_rows, preferred_element_type=F32)
    key_grad = jnp.einsum("nhqs,nqhk->nshk", score_grad, query_rows, preferred_element_type=F32)
    qkv_low = (
        jnp.stack(
            [
                rotate_back(query_grad * score_scale, cosine_table, sine_table),
                rotate_back(key_grad, cosine_table, sine_table),
                value_grad,
            ],
            axis=2,
        )
        .astype(BF16)
        .reshape(512, 768)
    )
    (ln_one_grad,) = merge_rows(8, dot(qkv_low, qkv_full, (1, 1)).reshape(4, 128, 2048))
    norm_in_one, gain_one_grad, bias_one_grad = norm_back(scaled_one, inverse_one, norm_rows[0], ln_one_grad)
    input_grad = hidden_grad + norm_in_one

    small_grad = jnp.concatenate(
        [
            router_grad_w,
            jnp.stack([gain_one_grad, gain_two_grad, bias_one_grad, bias_two_grad], axis=0),
            jnp.zeros((120, 2048), F32),
        ],
        axis=0,
    )
    grads = jnp.concatenate(
        [
            small_grad.astype(BF16).T,
            dot(a_one, qkv_low, (0, 0)).astype(BF16),
            dot(hidden_low, mixed, (0, 0)).astype(BF16),
            dot(a_two, up_low, (0, 0)).astype(BF16),
            dot(branch_rows, activation, (0, 0)).astype(BF16),
        ],
        axis=1,
    )
    own = scatter_gradients(grads.reshape(4, 4, 128, WIDE))
    small_own = jnp.sum(own[:, :, :8].astype(F32), axis=0)
    own_qkv, own_out, own_up, own_down = (own[:, :, a:b].astype(F32) for a, b in (QKV, OUT, UP, DOWN))
    reduced = (
        own_qkv.reshape(4, 32, 3, 2, 128).transpose(1, 2, 0, 3, 4).reshape(32, 3, 8, 128),
        own_out.reshape(4, 32, 2, 128).transpose(0, 2, 3, 1).reshape(8, 128, 32),
        own_up.transpose(1, 0, 2).reshape(32, 4096),
        own_down.transpose(0, 2, 1).reshape(4096, 32),
        small_own[:, :4],
        small_own[:, 4:].T,
    )

    masters = (qkv_weight, out_weight, up_weight, down_weight, router_weight)
    firsts = (qkv_first, out_first, up_first, down_first, router_first)
    seconds = (qkv_second, out_second, up_second, down_second, router_second)
    shares = (1.0, 1.0, 1.0, 1.0, 0.5)
    stepped = [
        moment_step(masters[index], reduced[index], firsts[index], seconds[index], DECAY_RATE)
        for index in range(5)
    ]
    squares = [jnp.sum(masters[index] * masters[index]) * shares[index] for index in range(5)]
    squares += [jnp.sum(stepped[index][2] * stepped[index][2]) * shares[index] for index in range(5)]
    tile = jnp.broadcast_to(jnp.concatenate([jnp.stack(squares), jnp.zeros((118,), F32)])[None], (8, 128))
    norms = jnp.sqrt(total(tile)[0, :10])
    weight_norm, update_norm = norms[:5], norms[5:]
    renewed = [
        masters[index] - LEARN_RATE * (weight_norm[index] / update_norm[index]) * stepped[index][2]
        for index in range(5)
    ]
    norm_moment, norm_square, norm_update = moment_step(norm_master, reduced[5], norm_first, norm_second, 0.0)
    norms_new = norm_master - NORM_RATE * norm_update
    lamb_norms = jnp.stack([weight_norm, update_norm], axis=1)
    return (
        block_output,
        input_grad,
        *reduced,
        *(step[0] for step in stepped),
        norm_moment,
        *(step[1] for step in stepped),
        norm_square,
        *renewed,
        norms_new,
        *(value.astype(BF16) for value in renewed),
        norms_new.astype(BF16),
        lamb_norms,
    )


def solution(mesh):
    qkv, out = P("dp", None, "mp", None), P("mp", None, "dp")
    up, down, router, norms = P("dp", "mp"), P("mp", "dp"), P("dp", None), P(None, "dp")
    rows, tokens = P("dp", None), P("dp")
    matrices = (qkv, out, up, down, router)
    return jax.shard_map(
        local,
        mesh=mesh,
        in_specs=(
            rows, rows, tokens, tokens, tokens, tokens,
            *matrices, norms, norms,
            qkv, qkv, out, out, up, up, down, down, router, router, norms, norms,
        ),
        out_specs=(rows, rows, *((*matrices, norms) * 5), P()),
        check_vma=False,
    )
```

time: 3000 us -> 519 us (0.17)
  waiting for transfers between devices: 2200 us -> 0 us
  blocking collectives: 439 us -> 0 us
  Pallas kernels: 0 us -> 334 us
  local copies, waits for them, and re-layouts: 170 us -> 61.8 us
    reduce_scatter x4 -> x0, waiting for transfers between devices: 1470 us -> none  [the longest x1 430 us: local(): lax.psum_scatter(down_grad_w, 'dp', scatter_dimension=1, tiled=True)]
    unnamed x15 -> x0, waiting for transfers between devices: 619 us -> none
    all_gather x2 -> x0, blocking collectives: 348 us -> none  [the longest x1 178 us: local(): lax.all_gather(norm_master.astype(jnp.bfloat16), 'dp', axis=1, tiled=True)]
    pallas_call x0 -> x9, Pallas kernels: none -> 334 us  [the longest x1 93.7 us: gather_weights(): pl.pallas_call(gather_kernel, out_shape=(jax.ShapeDtypeStruct((4, 4, 128,...]
    cond x6 -> x0, local copies, waits for them, and re-layouts: 64.9 us -> none  [the longest x2 62.3 us: local(): lax.switch(used_quarters, backward_cases, arrived, arrived_grad, pre_act,...]
    psum x1 -> x0, blocking collectives: 62.1 us -> none  [local(): lax.psum((weight_squares, update_squares), ('dp', 'mp'))]
    another operation x4 -> x5, local copies, waits for them, and re-layouts: 50.5 us -> 0.14 us
    all_to_all x3 -> x0, waiting for transfers between devices: 47 us -> none  [the longest x1 22.4 us: local(): lax.all_to_all(send_grad.reshape(data_count, capacity, feature_count), 'd...]
  transfers between devices with their start and end apart: 16 -> 0, of which waited for: 12 -> 0; matrix products, arithmetic and copies ran while one was open for 4% -> 0% of each run, Pallas kernels for 0% -> 0%
where the time goes in v1:
time: 519 us; the launch traced here: 509 us
  Pallas kernels  334 us (64%)
  local copies, waits for them, and re-layouts  61.8 us (12%)
  matrix products  60.6 us (12%)
  other arithmetic  40.8 us (8%)
  between operations  11.1 us (2%)
    pallas_call x1, Pallas kernels, gather_weights(): pl.pallas_call(gather_kernel, out_shape=(jax.ShapeDtypeStruct((4, 4, 128,...  93.7 us
    pallas_call x1, Pallas kernels, scatter_gradients(): pl.pallas_call(scatter_kernel, out_shape=jax.ShapeDtypeStruct((4, 32, WID...  91.9 us
    pallas_call x3, Pallas kernels, merge_rows(): pl.pallas_call(partial(merge_kernel, count), out_shape=(jax.ShapeDtypeStr...  72.9 us
    pallas_call x3, Pallas kernels, spread_rows(): pl.pallas_call(partial(spread_kernel, count), out_shape=(jax.ShapeDtypeSt...  60.6 us
    dot_general x13, matrix products, dot(): lax.dot_general(left, right, ((dims[:1], dims[1:]), ((), ())), preferred_...  51.4 us
    concatenate x1, local copies, waits for them, and re-layouts, local(): jnp.concatenate([small_grad.astype(BF16).T, dot(a_one, qkv_low, (0, 0)).a...  17.3 us
    pallas_call x1, Pallas kernels, total(): pl.pallas_call(total_kernel, out_shape=jax.ShapeDtypeStruct((8, 128), F32...  15.4 us

profile of v1, /device:TPU:0, one launch (start us, length us, event | category | flops | bytes accessed | tf_op | source)
XLA Modules:
  0.0 508.7 jit_solution(17425391429513918123)
XLA Ops:
  8.8 93.7 %gather_weights.1 = (bf16[4,4,128,3200]{3,2,1,0:T(8,128)(2,1)}, f32[4,8,128]{2,1,0:T(8,128)}) custom-call(bf16[4,32,3200]{2,1,0:T(8,128)(2,1)} %copy-done.36, f32[8,128]{1,0:T(8,128)} %maximum_maximum_fusion.1.meta), custom_call_target="tpu_custom_call" | custom-call | tf_op jit(solution)/shard_map/gather_weights/pallas_call | solution.py:115
  106.7 2.9 copy.212
  111.6 2.3 slice_reduce_fusion.1
  114.8 14.7 %spread_rows_3.1 = bf16[4,128,2048]{2,1,0:T(8,128)(2,1)S(1)} custom-call(bf16[128,2048]{1,0:T(8,128)(2,1)S(1)} %fusion.27.refs_0_), custom_call_target="tpu_custom_call" | custom-call | tf_op jit(solution)/shard_map/spread_rows_3/pallas_call | solution.py:291
  134.8 2.5 fusion.50
  141.4 2.3 mul.548
  143.8 2.3 mul.549
  148.2 19.5 %merge_rows_4.1 = f32[128,2048]{1,0:T(8,128)S(1)} custom-call(f32[4,128,2048]{2,1,0:T(8,128)S(1)} %fusion.37.refs_0_), custom_call_target="tpu_custom_call" | custom-call | tf_op jit(solution)/shard_map/merge_rows_4/pallas_call | solution.py:347
  170.7 28.7 %spread_rows_5.1 = (bf16[4,128,2048]{2,1,0:T(8,128)(2,1)S(1)}, bf16[4,128,2048]{2,1,0:T(8,128)(2,1)S(1)}) custom-call(bf16[128,2048]{1,0:T(8,128)(2,1)S(1)} %add_convert_fusion.1.refs_0_, bf16[128,2048]{1,0:T(8,128)(2,1)S(1)} %fusion.35.refs_1_), custom_call_target="tpu_custom_call" | custom-call | tf_op jit(solution)/shard_map/spread_rows_5/pallas_call | solution.py:291
  202.0 5.9 %fusion.7 = f32[512,1024]{1,0:T(8,128)} fusion(bf16[512,2048]{1,0:T(8,128)(2,1)S(1)} %bitcast.173, bf16[2048,3200]{1,0:T(8,128)(2,1)} %bitcast.186), kind=kOutput, calls=%fused_computation.9 | convolution fusion | flops 2147483648 | bytes 8388608 | tf_op jit(solution)/shard_map/dot_general | solution.py:462
  207.9 7.3 %fusion.3 = f32[512,2048]{1,0:T(8,128)} fusion(bf16[2048,3200]{1,0:T(8,128)(2,1)} %bitcast.187, f32[512,1024]{1,0:T(8,128)} %fusion.7, f32[1024]{0:T(1024)S(1)} %add_convert_fusion.2, f32[512]{0:T(512)} %bitcast.207), kind=kOutput, calls=%fused_computation.5 | convolution fusion | flops 2150105088 | bytes 10491904 | tf_op jit(solution)/shard_map/dot_general | solution.py:462
  215.3 4.6 multiply_convert_fusion
  219.9 6.9 %fusion.5 = f32[512,2048]{1,0:T(8,128)} fusion(bf16[512,1024]{1,0:T(8,128)(2,1)S(1)} %multiply_convert_fusion, bf16[2048,3200]{1,0:T(8,128)(2,1)} %bitcast.189), kind=kOutput, calls=%fused_computation.7 | convolution fusion | flops 2147483648 | bytes 9437184 | tf_op jit(solution)/shard_map/dot_general | solution.py:462
  226.9 34.2 %merge_rows_6.1 = (f32[128,2048]{1,0:T(8,128)S(1)}, f32[128,2048]{1,0:T(8,128)S(1)}) custom-call(f32[4,128,2048]{2,1,0:T(8,128)} %bitcast.176, f32[4,128,2048]{2,1,0:T(8,128)} %bitcast.177), custom_call_target="tpu_custom_call" | custom-call | tf_op jit(solution)/shard_map/merge_rows_6/pallas_call | solution.py:347
  265.4 17.2 %spread_rows_7.1 = bf16[4,128,2048]{2,1,0:T(8,128)(2,1)S(1)} custom-call(bf16[128,2048]{1,0:T(8,128)(2,1)S(1)} %get-tuple-element.157.refs_0_), custom_call_target="tpu_custom_call" | custom-call | tf_op jit(solution)/shard_map/spread_rows_7/pallas_call | solution.py:291
  283.9 2.7 convolution_convert_fusion.3
  290.1 2.4 convolution_bitcast_fusion
  296.6 3.7 fusion.10.refs_0_
  300.4 19.2 %merge_rows_8.1 = f32[128,2048]{1,0:T(8,128)S(1)} custom-call(f32[4,128,2048]{2,1,0:T(8,128)S(1)} %fusion.10.refs_0_), custom_call_target="tpu_custom_call" | custom-call | tf_op jit(solution)/shard_map/merge_rows_8/pallas_call | solution.py:347
  328.2 2.7 convert_element_type.230
  330.9 3.5 fusion.9
  334.6 3.5 fusion.13
  338.1 4.5 convert_dynamic-update-slice_fusion.1
  342.5 4.6 convert_dynamic-update-slice_fusion
  347.1 17.3 %copy.229 = bf16[2048,3200]{1,0:T(8,128)(2,1)} copy(bf16[2048,3200]{0,1:T(8,128)(2,1)} %convert_dynamic-update-slice_fusion) | data formatting | bytes 26214400 | tf_op jit(solution)/shard_map/concatenate | solution.py:609
  364.5 91.9 %scatter_gradients.1 = bf16[4,32,3200]{2,1,0:T(8,128)(2,1)} custom-call(bf16[4,4,128,3200]{3,2,1,0:T(8,128)(2,1)} %bitcast.175), custom_call_target="tpu_custom_call" | custom-call | tf_op jit(solution)/shard_map/scatter_gradients/pallas_call | solution.py:236
  459.2 2.9 multiply_reduce_fusion.10
  462.1 2.5 multiply_reduce_fusion.12
  464.6 2.2 multiply_reduce_fusion.6
  471.4 5.3 %concatenate.57 = f32[128]{0:T(128)S(1)} concatenate(f32[1]{0:T(128)} %bitcast.50, f32[1]{0:T(128)} %bitcast.51, f32[1]{0:T(128)} %bitcast.52, f32[1]{0:T(128)} %bitcast.53, f32[1]{0:T(128)} %bitcast.54, f32[1]{0:T(128)} %bitcast.55, f32[1]{0:T(128)} %bitcast.56, f32[1]{0:T(128)} %bitcast.57, f32[1]{0:T(128)} %bitcast.58, f32[1]{0:T(128)} %bitcast.59, f32[118]{0:T(128)S(1)} %broadcast_in_dim.37), dimensions={0} | concatenate | bytes 1024 | tf_op jit(solution)/shard_map/concatenate | solution.py:641
  477.3 15.4 %total.1 = f32[8,128]{1,0:T(8,128)} custom-call(f32[8,128]{1,0:T(8,128)} %broadcast_in_dim.38.value), custom_call_target="tpu_custom_call" | custom-call | tf_op jit(solution)/shard_map/total/pallas_call | solution.py:392
  495.3 2.2 fusion.93
  (301 shorter events, 66.3 us)
Async XLA Ops:
  0.7 6.1 %copy-start.11 = (f32[32,4096]{1,0:T(8,128)S(1)}, f32[32,4096]{1,0:T(8,128)}, u32[]{:S(2)}) copy-start(f32[32,4096]{1,0:T(8,128)} %param.33) | copy-start | bytes 1572868
  0.7 6.1 %copy-start.13 = (f32[4096,32]{0,1:T(8,128)S(1)}, f32[4096,32]{0,1:T(8,128)}, u32[]{:S(2)}) copy-start(f32[4096,32]{0,1:T(8,128)} %param.34) | copy-start | bytes 1572868
  114.1 15.4 %copy-start.56 = (f32[128]{0:T(128)}, f32[128]{0:T(128)S(1)}, u32[]{:S(2)}) copy-start(f32[128]{0:T(128)S(1)} %broadcast_multiply_fusion.9) | copy-start | bytes 1540
  114.1 15.4 %copy-start.22 = (bf16[768,2048]{1,0:T(8,128)(2,1)S(1)}, bf16[768,2048]{1,0:T(8,128)(2,1)}, u32[]{:S(2)}) copy-start(bf16[768,2048]{1,0:T(8,128)(2,1)} %copy.212) | copy-start | bytes 9437188
  114.4 17.0 %copy-start.65 = (f32[128]{0:T(128)}, f32[128]{0:T(128)S(1)}, u32[]{:S(2)}) copy-start(f32[128]{0:T(128)S(1)} %add_rsqrt_fusion.1) | copy-start | bytes 1540
  132.7 4.6 copy-start.24
  207.9 7.4 %copy-start.71 = (f32[1024]{0:T(1024)}, f32[1024]{0:T(1024)S(1)}, u32[]{:S(2)}) copy-start(f32[1024]{0:T(1024)S(1)} %add_convert_fusion.2) | copy-start | bytes 12292
  207.9 7.4 %copy-start.2 = (bf16[4,128,2048]{2,1,0:T(8,128)(2,1)S(1)}, bf16[4,128,2048]{2,1,0:T(8,128)(2,1)}, u32[]{:S(2)}) copy-start(bf16[4,128,2048]{2,1,0:T(8,128)(2,1)} %copy-done.1) | copy-start | bytes 6291460
  207.9 7.4 %copy-start.81 = (f32[4,1,128]{2,1,0:T(1,128)S(1)}, f32[4,1,128]{2,1,0:T(1,128)}, u32[]{:S(2)}) copy-start(f32[4,1,128]{2,1,0:T(1,128)} %get-tuple-element.189) | copy-start | bytes 6148
  207.9 7.4 %copy-start.88 = (f32[512,1024]{1,0:T(8,128)S(1)}, f32[512,1024]{1,0:T(8,128)}, u32[]{:S(2)}) copy-start(f32[512,1024]{1,0:T(8,128)} %fusion.7) | copy-start | bytes 6291460
  219.9 6.9 %copy-start.90 = (bf16[512,1024]{1,0:T(8,128)(2,1)}, bf16[512,1024]{1,0:T(8,128)(2,1)S(1)}, u32[]{:S(2)}) copy-start(bf16[512,1024]{1,0:T(8,128)(2,1)S(1)} %multiply_convert_fusion) | copy-start | bytes 3145732
  226.8 34.3 %copy-start.7 = (f32[128,2048]{1,0:T(8,128)S(1)}, f32[128,2048]{1,0:T(8,128)}, u32[]{:S(2)}) copy-start(f32[128,2048]{1,0:T(8,128)} %copy-done.6) | copy-start | bytes 3145732
  226.8 34.3 %copy-start.16 = (bf16[128,2048]{1,0:T(8,128)(2,1)S(1)}, bf16[128,2048]{1,0:T(8,128)(2,1)}, u32[]{:S(2)}) copy-start(bf16[128,2048]{1,0:T(8,128)(2,1)} %param.26) | copy-start | bytes 1572868
  226.8 34.3 %copy-start.54 = (f32[128]{0:T(128)S(1)}, f32[128]{0:T(128)}, u32[]{:S(2)}) copy-start(f32[128]{0:T(128)} %copy-done.53) | copy-start | bytes 1540
  226.8 34.3 %copy-start.77 = (f32[128]{0:T(128)S(1)}, f32[128]{0:T(128)}, u32[]{:S(2)}) copy-start(f32[128]{0:T(128)} %compare_convert_fusion.2) | copy-start | bytes 1540
  283.9 6.2 %copy-start.50 = (f32[4,2,128]{2,1,0:T(2,128)S(1)}, f32[4,2,128]{2,1,0:T(2,128)}, u32[]{:S(2)}) copy-start(f32[4,2,128]{2,1,0:T(2,128)} %copy-done.49) | copy-start | bytes 12292
  283.9 6.2 %copy-start.80 = (bf16[4,128,2]{1,2,0:T(2,128)(2,1)S(1)}, bf16[4,128,2]{1,2,0:T(2,128)(2,1)}, u32[]{:S(2)}) copy-start(bf16[4,128,2]{1,2,0:T(2,128)(2,1)} %get-tuple-element.192) | copy-start | bytes 6148
  300.3 19.2 %copy-start.57 = (f32[128]{0:T(128)S(1)}, f32[128]{0:T(128)}, u32[]{:S(2)}) copy-start(f32[128]{0:T(128)} %copy-done.56) | copy-start | bytes 1540
  300.4 19.2 %copy-start.66 = (f32[128]{0:T(128)S(1)}, f32[128]{0:T(128)}, u32[]{:S(2)}) copy-start(f32[128]{0:T(128)} %copy-done.65) | copy-start | bytes 1540
  338.0 4.5 copy-start.72
  458.1 6.5 %copy-start.32 = (f32[4,4,8,1024]{3,2,0,1:T(8,128)}, f32[4,4,8,1024]{3,2,0,1:T(8,128)S(1)}, u32[]{:S(2)}) copy-start(f32[4,4,8,1024]{3,2,0,1:T(8,128)S(1)} %copy.251) | copy-start | bytes 1572868
  458.1 6.5 %copy-start.12 = (f32[32,4096]{1,0:T(8,128)S(1)}, f32[32,4096]{1,0:T(8,128)}, u32[]{:S(2)}) copy-start(f32[32,4096]{1,0:T(8,128)} %param.33) | copy-start | bytes 1572868
  459.1 9.1 %copy-start.59 = (f32[32,4]{0,1:T(4,128)}, f32[32,4]{0,1:T(4,128)S(1)}, u32[]{:S(2)}) copy-start(f32[32,4]{0,1:T(4,128)S(1)} %copy.247) | copy-start | bytes 1540
  459.2 10.3 %copy-start.58 = (f32[32,4]{0,1:T(4,128)}, f32[32,4]{0,1:T(4,128)S(1)}, u32[]{:S(2)}) copy-start(f32[32,4]{0,1:T(4,128)S(1)} %copy.248) | copy-start | bytes 1540
  462.1 4.8 copy-start.14
  462.1 4.8 copy-start.33
  462.1 4.8 copy-start.38
  462.1 4.9 copy-start.39
  466.9 35.1 %copy-start.26 = (f32[32,4096]{1,0:T(8,128)}, f32[32,4096]{1,0:T(8,128)S(1)}, u32[]{:S(2)}) copy-start(f32[32,4096]{1,0:T(8,128)S(1)} %get-tuple-element.151) | copy-start | bytes 1572868
  466.9 35.1 %copy-start.27 = (f32[32,4096]{1,0:T(8,128)}, f32[32,4096]{1,0:T(8,128)S(1)}, u32[]{:S(2)}) copy-start(f32[32,4096]{1,0:T(8,128)S(1)} %get-tuple-element.152) | copy-start | bytes 1572868
  468.2 36.3 %copy-start.28 = (f32[4096,32]{0,1:T(8,128)}, f32[4096,32]{0,1:T(8,128)S(1)}, u32[]{:S(2)}) copy-start(f32[4096,32]{0,1:T(8,128)S(1)} %get-tuple-element.149) | copy-start | bytes 1572868
  468.2 36.3 %copy-start.29 = (f32[4096,32]{0,1:T(8,128)}, f32[4096,32]{0,1:T(8,128)S(1)}, u32[]{:S(2)}) copy-start(f32[4096,32]{0,1:T(8,128)S(1)} %get-tuple-element.150) | copy-start | bytes 1572868
  (60 other events, 119.5 us)

commit v2 on v1

v2 whole, which is shorter than its diff:
```python
import jax
import jax.numpy as jnp
from jax import lax
from jax.experimental import pallas as pl
from jax.experimental.pallas import tpu as pltpu
from jax.sharding import PartitionSpec as P

STEP = 5

BETA_ONE = 0.5
BETA_TWO = 0.5
ADAM_EPS = 1e-06
DECAY_RATE = 0.01
LEARN_RATE = 0.5
NORM_RATE = 0.1
NORM_EPS = 1e-05
ROPE_BASE = 10000.0

MESH = pl.DeviceIdType.MESH
BF16 = jnp.bfloat16
F32 = jnp.float32
VMEM = pl.BlockSpec(memory_space=pltpu.VMEM)
ANY = pl.BlockSpec(memory_space=pl.ANY)
DMA = pltpu.SemaphoreType.DMA
ALL = slice(None)
LOW, HIGH = pl.ds(0, 64), pl.ds(64, 64)


def place():
    index = lax.axis_index("dp")
    return lax.div(index, 16), lax.rem(lax.div(index, 4), 4), lax.rem(index, 4), lax.axis_index("mp")


def ring(value, step):
    return lax.rem(value + (step + 4), 4)


def device(x, y, z, core):
    return (x * 16 + y * 4 + z, core)


def greet(peers):
    barrier = pltpu.get_barrier_semaphore()
    for peer in peers:
        pl.semaphore_signal(barrier, inc=1, device_id=peer, device_id_type=MESH)
    pl.semaphore_wait(barrier, len(peers))


def send(src, dst, send_sem, recv_sem, peer):
    copy = pltpu.make_async_remote_copy(
        src_ref=src, dst_ref=dst, send_sem=send_sem, recv_sem=recv_sem, device_id=peer, device_id_type=MESH
    )
    copy.start()
    return copy


def span(index, size):
    return pl.ds(pl.multiple_of(index * size, size), size)


def dot(left, right, dims):
    return lax.dot_general(left, right, ((dims[:1], dims[1:]), ((), ())), preferred_element_type=F32)


class Links:
    def __init__(self, send_sems, recv_sems):
        self.x, self.y, self.z, self.core = x, y, z, core = place()
        self.xs = {k: device(ring(x, k), y, z, core) for k in (1, 2, 3)}
        self.ys = {k: device(x, ring(y, k), z, core) for k in (1, 2, 3)}
        self.zs = {k: device(x, y, ring(z, k), core) for k in (1, 2, 3)}
        self.partner = device(x, y, z, 1 - core)
        self.send_sems, self.recv_sems, self.used = send_sems, recv_sems, 0

    def go(self, src, dst, peer):
        number = self.used
        self.used += 1
        return send(src, dst, self.send_sems.at[number], self.recv_sems.at[number], peer)


class Gather:
    def __init__(self, links, first, second):
        self.links, self.parts, self.number, self.copies = links, (first, second), 0, []

    def advance(self):
        for copy in self.copies:
            copy.wait()
        x, y = self.links.x, self.links.y
        xp, xm, yp, ym = self.links.xs[1], self.links.xs[3], self.links.ys[1], self.links.ys[3]
        xb, xa, yb, ya = ring(x, -1), ring(x, 1), ring(y, -1), ring(y, 1)
        moves = {
            0: (((x, y, ALL), xp), ((x, y, ALL), xm), ((x, y, ALL), yp), ((x, y, ALL), ym)),
            1: (((xb, y, LOW), xp), ((xa, y, HIGH), xm), ((x, yb, LOW), yp), ((x, ya, HIGH), ym)),
            2: (((ALL, y, ALL), yp), ((ALL, y, ALL), ym), ((x, ALL, ALL), xp), ((x, ALL, ALL), xm)),
            3: (((ALL, yb, LOW), yp), ((ALL, ya, HIGH), ym), ((xb, ALL, LOW), xp), ((xa, ALL, HIGH), xm)),
        }.get(self.number, ())
        self.number += 1
        self.copies = []
        for index, (where, peer) in enumerate(moves):
            ref, columns = self.parts[index // 2]
            block = ref.at[where + (columns,)]
            self.copies.append(self.links.go(block, block, peer))


def add_into(ref, blocks, columns, sources, row, count):
    steps = count // 16

    def one(index, carry):
        number = lax.div(index, steps)
        step = pl.multiple_of(lax.rem(index, steps) * 16, 16)
        to = blocks[1](number) + (pl.ds(row + step, 16), columns)
        here = ref[to].astype(F32)
        for source, first_row in sources:
            place_in = ((number,) if blocks[0] > 1 else ()) + (pl.ds(first_row + step, 16), ALL)
            here = here + source[place_in].astype(F32)
        ref[to] = here.astype(BF16)
        return carry

    lax.fori_loop(0, blocks[0] * steps, one, 0)


class Scatter:
    def __init__(self, links, first, second, buffers):
        self.links, self.parts = links, (first, second)
        self.buffers = (buffers[:4], buffers[4:])
        self.number, self.halves, self.rest = 0, [], []

    def lanes(self, phase):
        x, y = self.links.x, self.links.y
        found = []
        for part in (0, 1):
            ref, columns = self.parts[part]
            along_y = part == phase
            peers = self.links.ys if along_y else self.links.xs
            if phase == 0 and along_y:
                where, count, each = (lambda k: (ALL, ring(y, k))), 4, (lambda k: lambda i: (i, ring(y, k)))
            elif phase == 0:
                where, count, each = (lambda k: (ring(x, k), ALL)), 4, (lambda k: lambda i: (ring(x, k), i))
            elif along_y:
                where, count, each = (lambda k: (x, ring(y, k))), 1, (lambda k: lambda i: (x, ring(y, k)))
            else:
                where, count, each = (lambda k: (ring(x, k), y)), 1, (lambda k: lambda i: (ring(x, k), y))
            one, two = self.buffers[part][2 * phase : 2 * phase + 2]
            found.append((ref, columns, where, count, each, peers, one, two))
        return found

    def begin(self, phase):
        self.halves, self.rest = [], []
        for ref, columns, where, count, each, peers, one, two in self.lanes(phase):
            lead = (ALL,) if count > 1 else ()
            self.halves.append(self.links.go(ref.at[where(2) + (LOW, columns)], one.at[0], peers[1]))
            self.halves.append(self.links.go(ref.at[where(2) + (HIGH, columns)], one.at[1], peers[3]))
        for ref, columns, where, count, each, peers, one, two in self.lanes(phase):
            lead = (ALL,) if count > 1 else ()
            self.rest.append(
                self.links.go(ref.at[where(1) + (HIGH, columns)], two.at[(0,) + lead + (HIGH,)], peers[1])
            )
            self.rest.append(
                self.links.go(ref.at[where(-1) + (LOW, columns)], two.at[(1,) + lead + (LOW,)], peers[3])
            )

    def middle(self, phase):
        lanes = self.lanes(phase)
        for side in (0, 1):
            for part in (0, 1):
                ref, columns, where, count, each, peers, one, two = lanes[part]
                lead = (ALL,) if count > 1 else ()
                step, rows, row = ((1, LOW, 0), (-1, HIGH, 64))[side]
                self.halves[2 * part + side].wait()
                add_into(ref, (count, each(step)), columns, [(one.at[side], 0)], row, 64)
                self.rest.append(
                    self.links.go(
                        ref.at[where(step) + (rows, columns)], two.at[(side,) + lead + (rows,)], peers[(1, 3)[side]]
                    )
                )

    def end(self, phase):
        for copy in self.rest:
            copy.wait()
        for ref, columns, where, count, each, peers, one, two in self.lanes(phase):
            add_into(ref, (count, each(0)), columns, [(two.at[0], 0), (two.at[1], 0)], 0, 128)

    def advance(self):
        if self.number == 0:
            self.begin(0)
        elif self.number == 1:
            self.middle(0)
        elif self.number == 2:
            self.end(0)
            self.begin(1)
        elif self.number == 3:
            self.middle(1)
        elif self.number == 4:
            self.end(1)
        self.number += 1


class Spread:
    def __init__(self, links, ref):
        self.links, self.ref = links, ref
        self.half = span(links.core, 1024)

    def start(self):
        here = self.ref.at[span(self.links.z, 128), self.half]
        self.flying = [(k, self.links.go(here, here, self.links.zs[k])) for k in (2, 1, 3)]
        return self

    def finish(self):
        passed = []
        for k, copy in self.flying:
            copy.wait_recv()
            block = self.ref.at[span(ring(self.links.z, -k), 128), self.half]
            passed.append(self.links.go(block, block, self.links.partner))
        for _, copy in self.flying:
            copy.wait_send()
        for copy in passed:
            copy.wait()


class Merge:
    def __init__(self, links, left, weights, buffers, out):
        self.links, self.left, self.weights, self.out = links, left, weights, out
        self.c_out, self.c_in, self.z_out, self.z_in, self.kept, self.tmp = buffers
        self.crossing, self.flying = [], []

    def tile(self, half, j):
        rows = self.weights[2 * half + j // 2, 2 * (j % 2) : 2 * (j % 2) + 2]
        return dot(self.left[...], rows.reshape(256, rows.shape[-1]), (1, 1))

    def cross(self):
        for j in range(4):
            columns = pl.ds(256 * j, 256)
            self.c_out[:, columns] = self.tile(1 - self.links.core, j).astype(BF16)
            self.crossing.append(
                self.links.go(self.c_out.at[:, columns], self.c_in.at[:, columns], self.links.partner)
            )
        return self

    def along(self):
        links = self.links
        for j in range(4):
            columns = pl.ds(256 * j, 256)
            value = self.tile(links.core, j)
            self.crossing[j].wait()
            value = value + self.c_in[:, columns].astype(F32)
            self.tmp[...] = value
            self.z_out[:, columns] = value.astype(BF16)
            for k in (2, 1, 3):
                self.flying.append(
                    links.go(
                        self.z_out.at[span(ring(links.z, k), 128), columns],
                        self.z_in.at[k - 1, :, columns],
                        links.zs[k],
                    )
                )
            self.kept[:, columns] = self.tmp[span(links.z, 128), :]
        return self

    def sum(self):
        links = self.links
        for copy in self.flying:
            copy.wait()

        def one(i, carry):
            rows = span(i, 16)
            value = self.kept[rows, :]
            for k in range(3):
                value = value + self.z_in[k, rows, :].astype(F32)
            self.out[rows, span(links.core, 1024)] = value
            return carry

        lax.fori_loop(0, 8, one, 0)
        part = self.out.at[:, span(links.core, 1024)]
        self.last = links.go(part, part, links.partner)
        return self

    def finish(self):
        self.last.wait()


def norm_parts(value):
    centre = value - jnp.mean(value, axis=-1, keepdims=True)
    inverse = lax.rsqrt(jnp.mean(centre * centre, axis=-1, keepdims=True) + NORM_EPS)
    return centre * inverse, inverse


def norm_back(scaled, inverse, gain_row, upstream):
    dscaled = upstream * gain_row
    inner = (
        dscaled
        - jnp.mean(dscaled, axis=-1, keepdims=True)
        - scaled * jnp.mean(dscaled * scaled, axis=-1, keepdims=True)
    )
    return inner * inverse


def fold(value):
    return value[0:8, :] + value[8:16, :]


def columns_tile(columns):
    lane = lax.broadcasted_iota(jnp.int32, (16, 128), 1)
    tile = jnp.zeros((16, 128), F32)
    for index, column in enumerate(columns):
        tile = jnp.where(lane == index, column, tile)
    return tile


def turn(value):
    return pltpu.roll(value, 64, 1)


LINK_COPIES = 400


def layer_kernel(
    qkv_own, out_own, up_own, down_own, small_own, token_in, rows_in, cotangent, cosines, sines,
    block_out, input_grad, qkv_grad, out_grad, up_grad, down_grad, small_grad,
    wq, wo, wu, wd, small_slots, small_grid, small,
    tokens, gates, info,
    a_one, a_two, branch, hidden_low,
    hidden, n_one, n_two, merged, merged_too,
    qkv_wide, qkv, probs, mixed, d_mixed, d_qkv, act, up_low,
    c_out_a, c_in_a, z_out_a, z_in_a, kept_a, c_out_b, c_in_b, z_out_b, z_in_b, kept_b, tmp,
    small_sum, sx_in, sy_in, sz_in,
    *rest,
):
    buffers, (local_sems, send_sems, recv_sems) = rest[:-3], rest[-3:]
    links = Links(send_sems, recv_sems)
    x, y, z, core = links.x, links.y, links.z, links.core
    plane = 4 * x + y
    own_rows, own_32 = span(z, 128), span(z, 32)
    set_a = (c_out_a, c_in_a, z_out_a, z_in_a, kept_a, tmp)
    set_b = (c_out_b, c_in_b, z_out_b, z_in_b, kept_b, tmp)

    local_used = [0]

    def keep(src, dst):
        copy = pltpu.make_async_copy(src, dst, local_sems.at[local_used[0]])
        local_used[0] += 1
        copy.start()
        return copy

    greet([*links.xs.values(), *links.ys.values(), *links.zs.values(), links.partner])

    def to_group(moves):
        copies = []
        for k in (2, 1, 3):
            for src, dst in moves(ring(z, k)):
                copies.append(links.go(src, dst, links.zs[k]))
        for src, dst in moves(z):
            copies.append(keep(src, dst))
        return copies

    def wait(copies):
        for copy in copies:
            copy.wait()

    flying_q = to_group(lambda to: [(qkv_own.at[to], wq.at[x, y, own_32, :])])
    flying_s = []
    small_slots[z] = small_own[...]
    tokens[z] = token_in[...]
    for k in (2, 1, 3):
        flying_s.append(links.go(small_own, small_slots.at[z], links.zs[k]))
    flying_t = [links.go(token_in, tokens.at[z], links.zs[k]) for k in (2, 1, 3)]
    flying_o = to_group(
        lambda to: [(out_own.at[2 * to + h], wo.at[x, y, own_32, pl.ds(128 * h, 128)]) for h in (0, 1)]
    )
    flying_f = to_group(
        lambda to: [
            (up_own.at[:, span(to, 1024)], wu.at[x, y, own_32, :]),
            (down_own.at[:, span(to, 1024)], wd.at[x, y, own_32, :]),
        ]
    )
    wait(flying_q)
    ring_q = Gather(links, (wq, pl.ds(0, 384)), (wq, pl.ds(384, 384)))
    ring_o = Gather(links, (wo, pl.ds(0, 128)), (wo, pl.ds(128, 128)))
    ring_f = Gather(links, (wu, ALL), (wd, ALL))
    ring_q.advance()
    wait(flying_s)
    small_grid[x, y] = small_slots[0] + small_slots[1] + small_slots[2] + small_slots[3]
    here = small_grid.at[x, y]
    wait([links.go(here, here, links.xs[k]) for k in (1, 2, 3)])
    here = small_grid.at[:, y]
    flying_s = [links.go(here, here, links.ys[k]) for k in (1, 2, 3)]
    ring_q.advance()
    wait(flying_s)
    for p in range(16):
        small[:, 128 * p : 128 * p + 128] = small_grid[p // 4, p % 4]

    def norm_one(i, carry):
        rows = span(i, 16)
        scaled, inverse = norm_parts(rows_in[rows, :].astype(F32))
        n_one[rows, :] = scaled
        info[0, rows, :] = columns_tile([inverse])
        a_one[span(z * 8 + i, 16), :] = (scaled * small[4:5, :] + small[6:7, :]).astype(BF16)
        return carry

    lax.fori_loop(0, 8, norm_one, 0)
    rows_one = Spread(links, a_one).start()
    ring_q.advance()
    wait(flying_o)
    ring_o.advance()
    wait(flying_t)
    wait(flying_f)
    rows_one.finish()
    ring_q.advance()
    ring_o.advance()
    branch[own_rows, :] = cotangent[...]
    rows_branch = Spread(links, branch).start()
    ring_q.advance()
    ring_o.advance()
    ring_f.advance()

    for c in range(3):
        part = wq[:, :, :, 256 * c : 256 * c + 256].reshape(2048, 256)
        qkv_wide[:, 256 * c : 256 * c + 256] = dot(a_one[...], part, (1, 0))
    ring_o.advance()
    ring_f.advance()
    lane = lax.broadcasted_iota(jnp.int32, (128, 128), 1)
    causal = lax.broadcasted_iota(jnp.int32, (128, 128), 0) >= lane
    turned_sines = jnp.where(lane < 64, -sines[...], sines[...])
    scale = 128 ** (-0.5)

    def spots(index):
        row, head = lax.div(index, 2), lax.rem(index, 2)
        used = jnp.where((core * 8 + z * 2 + head).astype(F32) < tokens[row][:, 0:1], 1.0, 0.0)
        return span(row, 128), [span(2 * c + head, 128) for c in range(3)], used

    def attend(index, carry):
        rows, (q_at, k_at, v_at), used = spots(index)

        def rotate(value):
            return value * cosines[...] + turn(value) * turned_sines

        q = (rotate(qkv_wide[rows, q_at]) * scale).astype(BF16)
        k = rotate(qkv_wide[rows, k_at]).astype(BF16)
        v = qkv_wide[rows, v_at].astype(BF16)
        qkv[rows, q_at], qkv[rows, k_at], qkv[rows, v_at] = q, k, v
        scores = jnp.where(causal, dot(q, k, (1, 1)), -1e30)
        powers = jnp.exp(scores - jnp.max(scores, axis=-1, keepdims=True))
        share = powers / jnp.sum(powers, axis=-1, keepdims=True)
        probs[index] = share
        mixed[rows, q_at] = (dot(share.astype(BF16), v, (1, 0)) * used).astype(BF16)
        return carry

    lax.fori_loop(0, 8, attend, 0)
    ring_o.advance()
    ring_f.advance()
    merge_one = Merge(links, mixed, wo, set_a, merged).cross().along()
    rows_branch.finish()
    merge_one.sum().finish()

    def norm_two(i, carry):
        rows = span(i, 16)
        value = rows_in[rows, :].astype(F32) + merged[rows, :]
        hidden[rows, :] = value
        scaled, inverse = norm_parts(value)
        n_two[rows, :] = scaled
        low = (scaled * small[5:6, :] + small[7:8, :]).astype(BF16)
        a_two[span(z * 8 + i, 16), :] = low
        low = low.astype(F32)
        logits = [jnp.sum(low * small[b : b + 1, :], axis=-1, keepdims=True) for b in range(4)]
        top = jnp.maximum(jnp.maximum(logits[0], logits[1]), jnp.maximum(logits[2], logits[3]))
        powers = [jnp.exp(logit - top) for logit in logits]
        whole = powers[0] + powers[1] + powers[2] + powers[3]
        chances = [power / whole for power in powers]
        own = token_in[rows, :]
        bucket, kept = own[:, 1:2], own[:, 2:3]
        gate = jnp.zeros_like(bucket)
        for b in range(4):
            gate = jnp.where(bucket == b, chances[b], gate)
        info[1, rows, :] = columns_tile([inverse, gate, *chances])
        gates[z, rows, :] = columns_tile([gate * kept])
        return carry

    lax.fori_loop(0, 8, norm_two, 0)
    rows_two = Spread(links, a_two).start()
    here = gates.at[z]
    flying_g = [links.go(here, here, links.zs[k]) for k in (2, 1, 3)]
    ring_f.advance()
    rows_two.finish()
    wait(flying_g)

    def branch_rows(i, carry):
        rows = span(i, 16)
        gate = gates[lax.div(i, 8), span(lax.rem(i, 8), 16), :][:, 0:1]
        branch[rows, :] = (branch[rows, :].astype(F32) * gate).astype(BF16)
        return carry

    lax.fori_loop(0, 32, branch_rows, 0)
    ring_f.advance()

    quarter = (core * 2 + lax.div(z, 2)).astype(F32)
    used_units = tokens[...].reshape(512, 128)[:, 1:2] >= quarter

    def units(t, carry):
        at = span(t, 256)
        up = dot(a_two[...], wu[:, :, :, at].reshape(2048, 256), (1, 0))
        up = jnp.where(used_units, jnp.maximum(up, 0.0), 0.0)
        act[:, at] = (up * up).astype(BF16)
        back = dot(branch[...], wd[:, :, :, at].reshape(2048, 256), (1, 0))
        up_low[:, at] = (back * 2.0 * up).astype(BF16)
        return carry

    lax.fori_loop(0, 4, units, 0)
    merge_f = Merge(links, act, wd, set_a, merged).cross()
    merge_u = Merge(links, up_low, wu, set_b, merged_too).cross()
    merge_f.along()
    merge_u.along()

    def outer(left, right, target):
        def one(i, carry):
            value = dot(left[:, span(i, 256)], right[...], (0, 0)).astype(BF16)
            row, first = lax.div(i, 2), lax.rem(i, 2) * 2
            target[row, first] = value[0:128]
            target[row, first + 1] = value[128:256]
            return carry

        lax.fori_loop(0, 8, one, 0)

    outer(a_two, up_low, wu)
    outer(branch, act, wd)
    sums_f = Scatter(links, (wu, ALL), (wd, ALL), buffers[0:8])
    sums_f.advance()
    merge_f.sum()
    merge_u.sum()
    merge_f.finish()
    merge_u.finish()

    def back_two(i, carry):
        rows = span(i, 16)
        upstream = cotangent[rows, :].astype(F32)
        own, tile = token_in[rows, :], info[1, rows, :]
        bucket, kept = own[:, 1:2], own[:, 2:3]
        inverse, gate = tile[:, 0:1], tile[:, 1:2]
        produced = merged[rows, :].astype(BF16).astype(F32) * kept
        block_out[rows, :] = (hidden[rows, :] + gate * produced).astype(BF16)
        gate_grad = jnp.sum(upstream * produced, axis=-1, keepdims=True)
        low = a_two[span(z * 8 + i, 16), :].astype(F32)
        grad = merged_too[rows, :].astype(BF16).astype(F32)
        for b in range(4):
            hot = jnp.where(bucket == b, 1.0, 0.0)
            logit_grad = tile[:, 2 + b : 3 + b] * (hot - gate) * gate_grad
            grad = grad + logit_grad * small[b : b + 1, :]
            small_sum[b] += fold(logit_grad * low)
        scaled = n_two[rows, :]
        small_sum[5] += fold(grad * scaled)
        small_sum[7] += fold(grad)
        back = upstream + norm_back(scaled, inverse, small[5:6, :], grad)
        hidden[rows, :] = back
        hidden_low[span(z * 8 + i, 16), :] = back.astype(BF16)
        return carry

    small_sum[...] = jnp.zeros_like(small_sum)
    lax.fori_loop(0, 8, back_two, 0)
    rows_back = Spread(links, hidden_low).start()
    sums_f.advance()
    rows_back.finish()

    d_mixed[...] = dot(hidden_low[...], wo[...].reshape(2048, 256), (1, 0)).astype(BF16)
    sums_f.advance()

    def attend_back(index, carry):
        rows, (q_at, k_at, v_at), used = spots(index)
        share = probs[index]
        q, k, v = qkv[rows, q_at], qkv[rows, k_at], qkv[rows, v_at]
        grad = (d_mixed[rows, q_at].astype(F32) * used).astype(BF16)
        value_grad = dot(share.astype(BF16), grad, (0, 0))
        share_grad = dot(grad, v, (1, 1))
        inner = jnp.sum(share * share_grad, axis=-1, keepdims=True)
        score_grad = (share * (share_grad - inner)).astype(BF16)

        def rotate_back(value):
            return value * cosines[...] - turn(value * sines[...]) * jnp.where(lane < 64, -1.0, 1.0)

        d_qkv[rows, q_at] = rotate_back(dot(score_grad, k, (1, 0)) * scale).astype(BF16)
        d_qkv[rows, k_at] = rotate_back(dot(score_grad, q, (0, 0))).astype(BF16)
        d_qkv[rows, v_at] = value_grad.astype(BF16)
        return carry

    lax.fori_loop(0, 8, attend_back, 0)
    sums_f.advance()
    merge_q = Merge(links, d_qkv, wq, set_a, merged).cross().along()
    outer(a_one, d_qkv, wq)
    outer(hidden_low, mixed, wo)
    sums_q = Scatter(links, (wq, pl.ds(0, 384)), (wq, pl.ds(384, 384)), buffers[8:16])
    sums_o = Scatter(links, (wo, pl.ds(0, 128)), (wo, pl.ds(128, 128)), buffers[16:24])
    sums_f.advance()
    sums_q.advance()
    sums_o.advance()

    def to_owner(moves):
        copies = []
        for k in (2, 1, 3):
            for src, dst in moves(ring(z, k)):
                copies.append(links.go(src, dst, links.zs[k]))
        for src, dst in moves(z):
            copies.append(keep(src, dst))
        return copies

    moved = to_owner(
        lambda to: [
            (wu.at[x, y, span(to, 32), :], up_grad.at[:, span(z, 1024)]),
            (wd.at[x, y, span(to, 32), :], down_grad.at[:, span(z, 1024)]),
        ]
    )
    merge_q.sum().finish()

    def back_one(i, carry):
        rows = span(i, 16)
        grad = merged[rows, :]
        scaled, inverse = n_one[rows, :], info[0, rows, :][:, 0:1]
        small_sum[4] += fold(grad * scaled)
        small_sum[6] += fold(grad)
        input_grad[rows, :] = hidden[rows, :] + norm_back(scaled, inverse, small[4:5, :], grad)
        return carry

    lax.fori_loop(0, 8, back_one, 0)
    for r in range(8):
        small[r : r + 1, :] = jnp.sum(small_sum[r], axis=0, keepdims=True)

    def of_x(to):
        return small.at[:, span(to, 512)]

    copies = [links.go(of_x(ring(x, k)), sx_in.at[k], links.xs[k]) for k in (1, 2, 3)]
    sums_q.advance()
    sums_o.advance()
    wait(copies)
    sx_in[0] = small[:, span(x, 512)]
    sx_in[0] = sx_in[0] + sx_in[1] + sx_in[2] + sx_in[3]
    copies = [
        links.go(sx_in.at[0, :, span(ring(y, k), 128)], sy_in.at[k], links.ys[k]) for k in (1, 2, 3)
    ]
    wait(copies)
    sz_in[z] = sx_in[0, :, span(y, 128)] + sy_in[1] + sy_in[2] + sy_in[3]
    here = sz_in.at[z]
    copies = [links.go(here, here, links.zs[k]) for k in (1, 2, 3)]
    sums_q.advance()
    sums_o.advance()
    wait(copies)
    small_grad[...] = sz_in[0] + sz_in[1] + sz_in[2] + sz_in[3]
    sums_q.advance()
    sums_o.advance()
    sums_q.advance()
    sums_o.advance()
    moved += to_owner(
        lambda to: [
            (wq.at[x, y, span(to, 32), :], qkv_grad.at[z]),
            *((wo.at[x, y, span(to, 32), pl.ds(128 * h, 128)], out_grad.at[2 * z + h]) for h in (0, 1)),
        ]
    )
    wait(moved)


def layer(*operands):
    def vmem(*shape, kind=BF16):
        return pltpu.VMEM(shape, kind)

    def merge_buffers():
        return [vmem(512, 1024), vmem(512, 1024), vmem(512, 1024), vmem(3, 128, 1024), vmem(128, 1024, kind=F32)]

    def sum_buffers(width):
        return [
            vmem(2, 4, 64, width), vmem(2, 4, 128, width), vmem(2, 64, width), vmem(2, 128, width),
        ] * 2

    wide = vmem(128, 2048, kind=F32)
    return pl.pallas_call(
        layer_kernel,
        out_shape=(
            jax.ShapeDtypeStruct((128, 2048), BF16),
            jax.ShapeDtypeStruct((128, 2048), F32),
            jax.ShapeDtypeStruct((4, 32, 768), BF16),
            jax.ShapeDtypeStruct((8, 32, 128), BF16),
            jax.ShapeDtypeStruct((32, 4096), BF16),
            jax.ShapeDtypeStruct((32, 4096), BF16),
            jax.ShapeDtypeStruct((8, 128), F32),
        ),
        in_specs=[ANY] * 4 + [VMEM] * 6,
        out_specs=(VMEM, VMEM, ANY, ANY, ANY, ANY, VMEM),
        scratch_shapes=[
            vmem(4, 4, 128, 768), vmem(4, 4, 128, 256), vmem(4, 4, 128, 1024), vmem(4, 4, 128, 1024),
            vmem(4, 8, 128, kind=F32), vmem(4, 4, 8, 128, kind=F32), vmem(8, 2048, kind=F32),
            vmem(4, 128, 128, kind=F32), vmem(4, 128, 128, kind=F32), vmem(2, 128, 128, kind=F32),
            vmem(512, 2048), vmem(512, 2048), vmem(512, 2048), vmem(512, 2048),
            wide, wide, wide, wide, wide,
            vmem(512, 768, kind=F32), vmem(512, 768), vmem(8, 128, 128, kind=F32),
            vmem(512, 256), vmem(512, 256), vmem(512, 768), vmem(512, 1024), vmem(512, 1024),
            *merge_buffers(), *merge_buffers(), vmem(512, 256, kind=F32),
            vmem(8, 8, 2048, kind=F32), vmem(4, 8, 512, kind=F32), vmem(4, 8, 128, kind=F32),
            vmem(4, 8, 128, kind=F32),
            *sum_buffers(1024), *sum_buffers(384), *sum_buffers(128),
            DMA((20,)), DMA((LINK_COPIES,)), DMA((LINK_COPIES,)),
        ],
        compiler_params=pltpu.CompilerParams(
            collective_id=0, has_side_effects=True, vmem_limit_bytes=63 * 2**20
        ),
        name="layer",
    )(*operands)


def total_kernel(value, out, slots, t_send, t_recv):
    x, y, z, core = place()
    along = (
        [device(x, y, z, 1 - core)],
        [device(x, y, ring(z, k), core) for k in (1, 2, 3)],
        [device(x, ring(y, k), z, core) for k in (1, 2, 3)],
        [device(ring(x, k), y, z, core) for k in (1, 2, 3)],
    )
    greet([peer for peers in along for peer in peers])
    out[...] = value[...]
    for axis, (me, peers) in enumerate(zip((core, z, y, x), along)):
        slots[axis, me] = out[...]
        here = slots.at[axis, me]
        copies = [
            send(here, here, t_send.at[axis, k], t_recv.at[axis, k], peer) for k, peer in enumerate(peers)
        ]
        for copy in copies:
            copy.wait()
        result = slots[axis, 0]
        for k in range(1, len(peers) + 1):
            result = result + slots[axis, k]
        out[...] = result


def total(value):
    return pl.pallas_call(
        total_kernel,
        out_shape=jax.ShapeDtypeStruct((8, 128), F32),
        in_specs=[VMEM],
        out_specs=VMEM,
        scratch_shapes=[pltpu.VMEM((4, 4, 8, 128), F32), DMA((4, 3)), DMA((4, 3))],
        compiler_params=pltpu.CompilerParams(collective_id=2, has_side_effects=True),
        name="total",
    )(value)


def rotary_tables(length, size):
    half_size = size // 2
    frequency = ROPE_BASE ** (-(jnp.arange(half_size, dtype=F32) * 2.0 / size))
    angles = jnp.arange(length, dtype=F32)[:, None] * frequency[None, :]
    cosine_table = jnp.concatenate([jnp.cos(angles), jnp.cos(angles)], axis=-1)
    sine_table = jnp.concatenate([jnp.sin(angles), jnp.sin(angles)], axis=-1)
    return (cosine_table, sine_table)


def moment_step(weight, gradient, first_moment, second_moment, decay_rate):
    first_moment = BETA_ONE * first_moment + (1.0 - BETA_ONE) * gradient
    second_moment = BETA_TWO * second_moment + (1.0 - BETA_TWO) * gradient * gradient
    update = (
        first_moment
        / (1.0 - BETA_ONE**STEP)
        / (jnp.sqrt(second_moment / (1.0 - BETA_TWO**STEP)) + ADAM_EPS)
        + decay_rate * weight
    )
    return (first_moment, second_moment, update)


def local(
    block_input,
    cotangent,
    head_count,
    width_route,
    forced_width,
    slot_index,
    qkv_weight,
    out_weight,
    up_weight,
    down_weight,
    router_weight,
    norm_gains,
    norm_biases,
    qkv_first,
    qkv_second,
    out_first,
    out_second,
    up_first,
    up_second,
    down_first,
    down_second,
    router_first,
    router_second,
    norm_first,
    norm_second,
):
    z = lax.rem(lax.axis_index("dp"), 4)
    norm_master = jnp.concatenate([norm_gains, norm_biases], axis=0)
    bucket = jnp.where(forced_width[0] < 4, forced_width[0], width_route)

    small = jnp.concatenate([router_weight.T, norm_master], axis=0).astype(BF16).astype(F32)
    small = lax.dynamic_update_slice(jnp.zeros((8, 128), F32), small, (0, 32 * z))
    token = jnp.stack([head_count, bucket, (slot_index >= 0).astype(jnp.int32)], axis=1).astype(F32)
    token = jnp.pad(token, ((0, 0), (0, 125)))
    block_output, input_grad, own_qkv, own_out, own_up, own_down, own_small = layer(
        qkv_weight.astype(BF16).reshape(32, 3, 4, 2, 128).transpose(2, 0, 1, 3, 4).reshape(4, 32, 768),
        out_weight.astype(BF16).transpose(0, 2, 1),
        up_weight.astype(BF16),
        down_weight.astype(BF16).T,
        small,
        token,
        block_input,
        cotangent,
        *rotary_tables(128, 128),
    )
    own_small = lax.dynamic_slice(own_small, (0, 32 * z), (8, 32))
    reduced = (
        own_qkv.astype(F32).reshape(4, 32, 3, 2, 128).transpose(1, 2, 0, 3, 4).reshape(32, 3, 8, 128),
        own_out.astype(F32).transpose(0, 2, 1),
        own_up.astype(F32),
        own_down.astype(F32).T,
        own_small[:4].T,
        own_small[4:],
    )

    masters = (qkv_weight, out_weight, up_weight, down_weight, router_weight)
    firsts = (qkv_first, out_first, up_first, down_first, router_first)
    seconds = (qkv_second, out_second, up_second, down_second, router_second)
    shares = (1.0, 1.0, 1.0, 1.0, 0.5)
    stepped = [
        moment_step(masters[index], reduced[index], firsts[index], seconds[index], DECAY_RATE)
        for index in range(5)
    ]
    squares = [jnp.sum(masters[index] * masters[index]) * shares[index] for index in range(5)]
    squares += [jnp.sum(stepped[index][2] * stepped[index][2]) * shares[index] for index in range(5)]
    tile = jnp.broadcast_to(jnp.concatenate([jnp.stack(squares), jnp.zeros((118,), F32)])[None], (8, 128))
    norms = jnp.sqrt(total(tile)[0, :10])
    weight_norm, update_norm = norms[:5], norms[5:]
    renewed = [
        masters[index] - LEARN_RATE * (weight_norm[index] / update_norm[index]) * stepped[index][2]
        for index in range(5)
    ]
    norm_moment, norm_square, norm_update = moment_step(norm_master, reduced[5], norm_first, norm_second, 0.0)
    norms_new = norm_master - NORM_RATE * norm_update
    lamb_norms = jnp.stack([weight_norm, update_norm], axis=1)
    return (
        block_output,
        input_grad,
        *reduced,
        *(step[0] for step in stepped),
        norm_moment,
        *(step[1] for step in stepped),
        norm_square,
        *renewed,
        norms_new,
        *(value.astype(BF16) for value in renewed),
        norms_new.astype(BF16),
        lamb_norms,
    )


def solution(mesh):
    qkv, out = P("dp", None, "mp", None), P("mp", None, "dp")
    up, down, router, norms = P("dp", "mp"), P("mp", "dp"), P("dp", None), P(None, "dp")
    rows, tokens = P("dp", None), P("dp")
    matrices = (qkv, out, up, down, router)
    return jax.shard_map(
        local,
        mesh=mesh,
        in_specs=(
            rows, rows, tokens, tokens, tokens, tokens,
            *matrices, norms, norms,
            qkv, qkv, out, out, up, up, down, down, router, router, norms, norms,
        ),
        out_specs=(rows, rows, *((*matrices, norms) * 5), P()),
        check_vma=False,
    )
```

time: 519 us -> 283 us (0.55); the launches traced: 509 us -> 282 us
  Pallas kernels: 334 us -> 236 us
  matrix products: 60.6 us -> 0 us
  local copies, waits for them, and re-layouts: 61.8 us -> 16.4 us
  other arithmetic: 40.8 us -> 19.9 us
    pallas_call x8 -> x1, Pallas kernels: 319 us -> 222 us  [layer(): pl.pallas_call(layer_kernel, out_shape=(jax.ShapeDtypeStruct((128, 2048),...]
    dot_general x21 -> x0, matrix products: 60.6 us -> none  [the longest x13 51.4 us: dot(): lax.dot_general(left, right, ((dims[:1], dims[1:]), ((), ())), preferred_...]
    concatenate x5 -> x0, local copies, waits for them, and re-layouts: 19.5 us -> none  [the longest x1 17.3 us: local(): jnp.concatenate([small_grad.astype(BF16).T, dot(a_one, qkv_low, (0, 0)).a...]
    convert_element_type x5 -> x1, local copies, waits for them, and re-layouts: 6.32 us -> 0.11 us  [local(): jnp.stack([head_count, bucket, (slot_index >= 0).astype(jnp.int32)], axis=1)]
    convert_element_type x14 -> x3, other arithmetic: 6.18 us -> 0.75 us  [the longest x1 0.73 us: local(): up_weight.astype(BF16)]
where the time goes in v2:
time: 283 us; the launch traced here: 282 us
  Pallas kernels  236 us (83%)
  other arithmetic  19.9 us (7%)
  local copies, waits for them, and re-layouts  16.4 us (6%)
  between operations  9.77 us (3%)
    pallas_call x1, Pallas kernels, layer(): pl.pallas_call(layer_kernel, out_shape=(jax.ShapeDtypeStruct((128, 2048),...  222 us
    pallas_call x1, Pallas kernels, total(): pl.pallas_call(total_kernel, out_shape=jax.ShapeDtypeStruct((8, 128), F32...  14.4 us
    reduce_sum x5, other arithmetic, local(): jnp.sum(stepped[index][2] * stepped[index][2]) * shares[index]  8.15 us
    convert_element_type x5, other arithmetic, local(): value.astype(BF16)  6.8 us
    unnamed x76, local copies, waits for them, and re-layouts  5.91 us

profile of v2, /device:TPU:0, one launch (start us, length us, event | category | flops | bytes accessed | tf_op | source)
XLA Modules:
  0.0 282.4 jit_solution(14776735240927367850)
XLA Ops:
  1.6 0.6 multiply_reduce_fusion.9
  3.7 0.6 pad.4.token_in
  4.3 0.6 convert_bitcast_fusion.3.out_own
  5.2 0.8 pad_maximum_fusion
  6.2 0.8 reshape.140.qkv_own
  7.1 0.7 convert_element_type.48.up_own
  7.8 0.7 convert_bitcast_fusion.1.down_own
  8.5 221.9 %layer.1 = (bf16[128,2048]{1,0:T(8,128)(2,1)}, f32[128,2048]{1,0:T(8,128)}, bf16[4,32,768]{2,1,0:T(8,128)(2,1)}, bf16[8,32,128]{2,1,0:T(8,128)(2,1)}, bf16[32,40...) custom-call(bf16[4,32,768]{2,1,0:T(8,128)(2,1)} %reshape.140.qkv_own, ...), custom_call_target="tpu_custom_call" | custom-call | tf_op jit(solution)/shard_map/layer/pallas_call | solution.py:668
  230.4 0.7 copy-done.27
  231.2 0.6 copy-done.28
  231.8 1.2 multiply_reduce_fusion.8
  233.7 0.7 copy-done.31
  234.3 0.6 fusion.10
  234.9 1.1 reshape.149
  236.3 0.7 copy-done.11
  237.1 1.4 multiply_reduce_fusion.6
  238.5 1.8 multiply_reduce_fusion.4
  240.4 1.8 multiply_reduce_fusion.1
  242.2 2.0 multiply_reduce_fusion
  244.2 5.4 %concatenate.20 = f32[128]{0:T(128)S(1)} concatenate(f32[1]{0:T(128)} %bitcast.14, f32[1]{0:T(128)} %bitcast.15, f32[1]{0:T(128)} %bitcast.16, f32[1]{0:T(128)} %bitcast.17, f32[1]{0:T(128)} %bitcast.18, f32[1]{0:T(128)} %bitcast.19, f32[1]{0:T(128)} %bitcast.20, f32[1]{0:T(128)} %bitcast.21, f32[1]{0:T(128)} %bitcast.22, f32[1]{0:T(128)} %bitcast.23, f32[118]{0:T(128)S(1)} %broadcast_in_dim.20), dimensions={0} | concatenate | bytes 1024 | tf_op jit(solution)/shard_map/concatenate | solution.py:825
  249.6 0.6 broadcast_in_dim.21.value
  250.2 14.4 %total.1 = f32[8,128]{1,0:T(8,128)} custom-call(f32[8,128]{1,0:T(8,128)} %broadcast_in_dim.21.value), custom_call_target="tpu_custom_call" | custom-call | tf_op jit(solution)/shard_map/total/pallas_call | solution.py:727
  264.6 0.7 slice_sqrt_fusion
  265.9 0.6 fusion.22
  273.2 0.6 fusion.12
  273.8 1.8 fusion.15
  275.6 2.1 fusion.16
  277.7 1.2 fusion.13
  278.9 1.2 fusion.14
  280.1 0.8 copy.75
  280.9 0.6 copy-done.12
  281.5 1.0 copy.76
  (87 shorter events, 2.5 us)
Async XLA Ops:
  0.7 0.8 copy-start.35
  0.7 0.8 copy-start.36
  0.7 0.8 copy-start.33
  0.7 0.8 copy-start.32
  0.7 0.8 copy-start.34
  0.7 0.8 copy-start.25
  0.7 3.6 %copy-start.10 = (f32[8,128,32]{1,2,0:T(8,128)S(1)}, f32[8,128,32]{1,2,0:T(8,128)}, u32[]{:S(2)}) copy-start(f32[8,128,32]{1,2,0:T(8,128)} %param.32) | copy-start | bytes 393220
  3.1 2.9 %copy-start.3 = (f32[32,3,8,128]{3,2,1,0:T(8,128)S(1)}, f32[32,3,8,128]{3,2,1,0:T(8,128)}, u32[]{:S(2)}) copy-start(f32[32,3,8,128]{3,2,1,0:T(8,128)} %param.31) | copy-start | bytes 1179652
  6.0 1.0 copy-start.1
  6.2 1.6 copy-start
  231.1 0.7 copy-start.29
  236.1 0.9 copy-start.11
  236.1 1.0 copy-start.22
  236.1 1.0 copy-start.23
  236.1 1.0 copy-start.24
  236.3 2.2 copy-start.8
  237.1 1.4 copy-start.18
  237.1 1.4 copy-start.19
  238.5 1.8 copy-start.2
  238.5 1.8 copy-start.13
  238.5 1.8 copy-start.14
  238.5 1.8 copy-start.21
  240.3 1.9 copy-start.15
  240.3 1.8 copy-start.16
  240.4 1.8 copy-start.20
  242.2 36.7 %copy-start.4 = (f32[32,4096]{1,0:T(8,128)}, f32[32,4096]{1,0:T(8,128)S(1)}, u32[]{:S(2)}) copy-start(f32[32,4096]{1,0:T(8,128)S(1)} %get-tuple-element.153) | copy-start | bytes 1572868
  242.2 36.7 %copy-start.5 = (f32[32,4096]{1,0:T(8,128)}, f32[32,4096]{1,0:T(8,128)S(1)}, u32[]{:S(2)}) copy-start(f32[32,4096]{1,0:T(8,128)S(1)} %get-tuple-element.147) | copy-start | bytes 1572868
  244.2 33.5 %copy-start.6 = (f32[4096,32]{0,1:T(8,128)}, f32[4096,32]{0,1:T(8,128)S(1)}, u32[]{:S(2)}) copy-start(f32[4096,32]{0,1:T(8,128)S(1)} %get-tuple-element.154) | copy-start | bytes 1572868
  244.2 31.4 %copy-start.9 = (f32[32,3,8,128]{3,2,1,0:T(8,128)S(1)}, f32[32,3,8,128]{3,2,1,0:T(8,128)}, u32[]{:S(2)}) copy-start(f32[32,3,8,128]{3,2,1,0:T(8,128)} %get-tuple-element.151) | copy-start | bytes 1179652
  275.6 2.1 copy-start.7
  278.9 1.2 copy-start.17
  280.1 1.4 copy-start.12
  (5 other events, 3.3 us)

commit v3 on v2

v3 whole, which is shorter than its diff:
```python
import jax
import jax.numpy as jnp
import numpy as np
from jax import lax
from jax.experimental import pallas as pl
from jax.experimental.pallas import tpu as pltpu
from jax.sharding import PartitionSpec as P

STEP = 5

BETA_ONE = 0.5
BETA_TWO = 0.5
ADAM_EPS = 1e-06
DECAY_RATE = 0.01
LEARN_RATE = 0.5
NORM_RATE = 0.1
NORM_EPS = 1e-05
ROPE_BASE = 10000.0

MESH = pl.DeviceIdType.MESH
BF16 = jnp.bfloat16
F32 = jnp.float32
VMEM = pl.BlockSpec(memory_space=pltpu.VMEM)
ANY = pl.BlockSpec(memory_space=pl.ANY)
DMA = pltpu.SemaphoreType.DMA
ALL = slice(None)
LOW, HIGH = pl.ds(0, 64), pl.ds(64, 64)


def place():
    index = lax.axis_index("dp")
    return lax.div(index, 16), lax.rem(lax.div(index, 4), 4), lax.rem(index, 4), lax.axis_index("mp")


def ring(value, step):
    return lax.rem(value + (step + 4), 4)


def device(x, y, z, core):
    return (x * 16 + y * 4 + z, core)


def greet(peers):
    barrier = pltpu.get_barrier_semaphore()
    for peer in peers:
        pl.semaphore_signal(barrier, inc=1, device_id=peer, device_id_type=MESH)
    return lambda: pl.semaphore_wait(barrier, len(peers))


def send(src, dst, send_sem, recv_sem, peer):
    copy = pltpu.make_async_remote_copy(
        src_ref=src, dst_ref=dst, send_sem=send_sem, recv_sem=recv_sem, device_id=peer, device_id_type=MESH
    )
    copy.start()
    return copy


def span(index, size):
    return pl.ds(pl.multiple_of(index * size, size), size)


def dot(left, right, dims):
    return lax.dot_general(left, right, ((dims[:1], dims[1:]), ((), ())), preferred_element_type=F32)


class Links:
    def __init__(self, send_sems, recv_sems):
        self.x, self.y, self.z, self.core = x, y, z, core = place()
        self.xs = {k: device(ring(x, k), y, z, core) for k in (1, 2, 3)}
        self.ys = {k: device(x, ring(y, k), z, core) for k in (1, 2, 3)}
        self.zs = {k: device(x, y, ring(z, k), core) for k in (1, 2, 3)}
        self.partner = device(x, y, z, 1 - core)
        self.send_sems, self.recv_sems, self.used = send_sems, recv_sems, 0

    def go(self, src, dst, peer):
        number = self.used
        self.used += 1
        return send(src, dst, self.send_sems.at[number], self.recv_sems.at[number], peer)


class Gather:
    def __init__(self, links, first, second):
        self.links, self.parts, self.number, self.copies = links, (first, second), 0, []

    def advance(self):
        for copy in self.copies:
            copy.wait()
        x, y = self.links.x, self.links.y
        xp, xm, yp, ym = self.links.xs[1], self.links.xs[3], self.links.ys[1], self.links.ys[3]
        xb, xa, yb, ya = ring(x, -1), ring(x, 1), ring(y, -1), ring(y, 1)
        moves = {
            0: (((x, y, ALL), xp), ((x, y, ALL), xm), ((x, y, ALL), yp), ((x, y, ALL), ym)),
            1: (((xb, y, LOW), xp), ((xa, y, HIGH), xm), ((x, yb, LOW), yp), ((x, ya, HIGH), ym)),
            2: (((ALL, y, ALL), yp), ((ALL, y, ALL), ym), ((x, ALL, ALL), xp), ((x, ALL, ALL), xm)),
            3: (((ALL, yb, LOW), yp), ((ALL, ya, HIGH), ym), ((xb, ALL, LOW), xp), ((xa, ALL, HIGH), xm)),
        }.get(self.number, ())
        self.number += 1
        self.copies = []
        for index, (where, peer) in enumerate(moves):
            ref, columns = self.parts[index // 2]
            block = ref.at[where + (columns,)]
            self.copies.append(self.links.go(block, block, peer))


def add_into(ref, blocks, columns, sources, row, count):
    steps = count // 16

    def one(index, carry):
        number = lax.div(index, steps)
        step = pl.multiple_of(lax.rem(index, steps) * 16, 16)
        to = blocks[1](number) + (pl.ds(row + step, 16), columns)
        here = ref[to].astype(F32)
        for source, first_row in sources:
            place_in = ((number,) if blocks[0] > 1 else ()) + (pl.ds(first_row + step, 16), ALL)
            here = here + source[place_in].astype(F32)
        ref[to] = here.astype(BF16)
        return carry

    lax.fori_loop(0, blocks[0] * steps, one, 0)


class Scatter:
    def __init__(self, links, first, second, buffers):
        self.links, self.parts = links, (first, second)
        self.buffers = (buffers[:4], buffers[4:])
        self.number, self.halves, self.rest = 0, [], []

    def lanes(self, phase):
        x, y = self.links.x, self.links.y
        found = []
        for part in (0, 1):
            ref, columns = self.parts[part]
            along_y = part == phase
            peers = self.links.ys if along_y else self.links.xs
            if phase == 0 and along_y:
                where, count, each = (lambda k: (ALL, ring(y, k))), 4, (lambda k: lambda i: (i, ring(y, k)))
            elif phase == 0:
                where, count, each = (lambda k: (ring(x, k), ALL)), 4, (lambda k: lambda i: (ring(x, k), i))
            elif along_y:
                where, count, each = (lambda k: (x, ring(y, k))), 1, (lambda k: lambda i: (x, ring(y, k)))
            else:
                where, count, each = (lambda k: (ring(x, k), y)), 1, (lambda k: lambda i: (ring(x, k), y))
            one, two = self.buffers[part][2 * phase : 2 * phase + 2]
            found.append((ref, columns, where, count, each, peers, one, two))
        return found

    def begin(self, phase):
        self.halves, self.rest = [], []
        for ref, columns, where, count, each, peers, one, two in self.lanes(phase):
            self.halves.append(self.links.go(ref.at[where(2) + (LOW, columns)], one.at[0], peers[1]))
            self.halves.append(self.links.go(ref.at[where(2) + (HIGH, columns)], one.at[1], peers[3]))
        for ref, columns, where, count, each, peers, one, two in self.lanes(phase):
            lead = (ALL,) if count > 1 else ()
            self.rest.append(
                self.links.go(ref.at[where(1) + (HIGH, columns)], two.at[(0,) + lead + (HIGH,)], peers[1])
            )
            self.rest.append(
                self.links.go(ref.at[where(-1) + (LOW, columns)], two.at[(1,) + lead + (LOW,)], peers[3])
            )

    def middle(self, phase):
        lanes = self.lanes(phase)
        for side in (0, 1):
            for part in (0, 1):
                ref, columns, where, count, each, peers, one, two = lanes[part]
                lead = (ALL,) if count > 1 else ()
                step, rows, row = ((1, LOW, 0), (-1, HIGH, 64))[side]
                self.halves[2 * part + side].wait()
                add_into(ref, (count, each(step)), columns, [(one.at[side], 0)], row, 64)
                self.rest.append(
                    self.links.go(
                        ref.at[where(step) + (rows, columns)], two.at[(side,) + lead + (rows,)], peers[(1, 3)[side]]
                    )
                )

    def end(self, phase):
        for copy in self.rest:
            copy.wait()
        for ref, columns, where, count, each, peers, one, two in self.lanes(phase):
            add_into(ref, (count, each(0)), columns, [(two.at[0], 0), (two.at[1], 0)], 0, 128)

    def advance(self):
        if self.number == 0:
            self.begin(0)
        elif self.number == 1:
            self.middle(0)
        elif self.number == 2:
            self.end(0)
            self.begin(1)
        elif self.number == 3:
            self.middle(1)
        elif self.number == 4:
            self.end(1)
        self.number += 1


class Spread:
    def __init__(self, links, ref):
        self.links, self.ref = links, ref
        self.half = span(links.core, 1024)

    def start(self):
        here = self.ref.at[span(self.links.z, 128), self.half]
        self.flying = [(k, self.links.go(here, here, self.links.zs[k])) for k in (2, 1, 3)]
        return self

    def finish(self):
        passed = []
        for k, copy in self.flying:
            copy.wait_recv()
            block = self.ref.at[span(ring(self.links.z, -k), 128), self.half]
            passed.append(self.links.go(block, block, self.links.partner))
        for _, copy in self.flying:
            copy.wait_send()
        for copy in passed:
            copy.wait()


class Merge:
    def __init__(self, links, left, weights, buffers, out):
        self.links, self.left, self.weights, self.out = links, left, weights, out
        self.near, self.near_in, self.far_in, self.tmp = buffers
        self.crossing, self.flying = [], []

    def tile(self, half, j):
        rows = self.weights[2 * half + j // 2, 2 * (j % 2) : 2 * (j % 2) + 2]
        return dot(self.left[...], rows.reshape(256, rows.shape[-1]), (1, 1))

    def cross(self):
        for j in range(4):
            columns = pl.ds(256 * j, 256)
            self.near[:, columns] = self.tile(1 - self.links.core, j).astype(BF16)
            self.crossing.append(
                self.links.go(self.near.at[:, columns], self.near_in.at[:, columns], self.links.partner)
            )
        return self

    def along(self, leave=True):
        for j in range(4):
            columns = pl.ds(256 * j, 256)
            value = self.tile(self.links.core, j)
            self.crossing[j].wait()
            value = value + self.near_in[:, columns].astype(F32)
            self.tmp[...] = value
            self.near[:, columns] = value.astype(BF16)
            if leave:
                self.leave(columns)
            self.out[:, span(self.links.core * 4 + j, 256)] = self.tmp[span(self.links.z, 128), :]
        return self

    def leave(self, columns=ALL):
        links = self.links
        for k in (2, 1, 3):
            self.flying.append(
                links.go(
                    self.near.at[span(ring(links.z, k), 128), columns], self.far_in.at[k - 1, :, columns], links.zs[k]
                )
            )

    def sum(self):
        links = self.links
        for copy in self.flying:
            copy.wait()

        def one(i, carry):
            rows, half = span(i, 16), span(links.core, 1024)
            value = self.out[rows, half]
            for k in range(3):
                value = value + self.far_in[k, rows, :].astype(F32)
            self.out[rows, half] = value
            return carry

        lax.fori_loop(0, 8, one, 0)
        part = self.out.at[:, span(links.core, 1024)]
        self.last = links.go(part, part, links.partner)
        return self

    def finish(self):
        self.last.wait()


def norm_parts(value):
    centre = value - jnp.mean(value, axis=-1, keepdims=True)
    inverse = lax.rsqrt(jnp.mean(centre * centre, axis=-1, keepdims=True) + NORM_EPS)
    return centre * inverse, inverse


def norm_back(scaled, inverse, gain_row, upstream):
    dscaled = upstream * gain_row
    inner = (
        dscaled
        - jnp.mean(dscaled, axis=-1, keepdims=True)
        - scaled * jnp.mean(dscaled * scaled, axis=-1, keepdims=True)
    )
    return inner * inverse


def fold(value):
    return value[0:8, :] + value[8:16, :]


def fold_lanes(value):
    total = None
    for row in range(0, value.shape[0], 8):
        for lane in range(0, value.shape[1], 128):
            part = value[row : row + 8, lane : lane + 128]
            total = part if total is None else total + part
    return total


def columns_tile(columns):
    lane = lax.broadcasted_iota(jnp.int32, (16, 128), 1)
    tile = jnp.zeros((16, 128), F32)
    for index, column in enumerate(columns):
        tile = jnp.where(lane == index, column, tile)
    return tile


def as_columns(rows):
    return jnp.concatenate([rows, jnp.zeros((120, 128), F32)], axis=0).T


def turn(value):
    return pltpu.roll(value, 64, 1)


def moment_step(weight, gradient, first_moment, second_moment, decay_rate):
    first_moment = BETA_ONE * first_moment + (1.0 - BETA_ONE) * gradient
    second_moment = BETA_TWO * second_moment + (1.0 - BETA_TWO) * gradient * gradient
    update = (
        first_moment
        / (1.0 - BETA_ONE**STEP)
        / (jnp.sqrt(second_moment / (1.0 - BETA_TWO**STEP)) + ADAM_EPS)
        + decay_rate * weight
    )
    return (first_moment, second_moment, update)


LINK_COPIES = 400


def layer_kernel(
    qkv_w, out_w, up_w, down_w, qkv_m, qkv_v, out_m, out_v, up_m, up_v, down_m, down_v,
    router_w, router_m, router_v, gains, biases, head_count, width_route, forced_width, slot_index,
    rows_in, cotangent, cosines, sines,
    block_out, input_grad, qkv_grad, out_grad, up_grad, down_grad, small_grad, norms,
    own_q, own_o, own_u, own_d, pack_q, pack_o, pack_u, pack_d, mom_q, mom_o, mom_f,
    wq, wo, wu, wd, small_slots, small_grid, small,
    token_rows, tokens, gate_rows, gates, info,
    a_one, a_two, branch, hidden_low,
    hidden, n_one, n_two, merged, merged_too,
    wide, qkv, probs, mixed, d_mixed, d_qkv, act, up_low,
    near_a, near_in_a, far_in_a, near_b, near_in_b, far_in_b, tmp,
    gate_part, gate_near, gate_far, small_sum, sx_in, sy_in, sz_in, got_q, squares, slots,
    *rest,
):
    buffers, (local_sems, send_sems, recv_sems) = rest[:-3], rest[-3:]
    links = Links(send_sems, recv_sems)
    x, y, z, core = links.x, links.y, links.z, links.core
    own_rows, own_32 = span(z, 128), span(z, 32)
    set_a = (near_a, near_in_a, far_in_a, tmp)
    set_b = (near_b, near_in_b, far_in_b, tmp)
    local_used = [0]

    def keep(src, dst):
        copy = pltpu.make_async_copy(src, dst, local_sems.at[local_used[0]])
        local_used[0] += 1
        copy.start()
        return copy

    def wait(copies):
        for copy in copies:
            copy.wait()

    greeted = greet([*links.xs.values(), *links.ys.values(), *links.zs.values(), links.partner])

    loads = [keep(qkv_w, own_q), keep(out_w, own_o), keep(up_w, own_u), keep(down_w, own_d)]
    later = [
        keep(up_m, mom_f.at[0]), keep(up_v, mom_f.at[1]), keep(qkv_m, mom_q.at[0]), keep(qkv_v, mom_q.at[1]),
        keep(out_m, mom_o.at[0]), keep(out_v, mom_o.at[1]),
    ]
    small_slots[z] = jnp.zeros((8, 128), F32)
    small_slots[z, 0:4, 0:32] = router_w[...].astype(BF16).astype(F32)
    small_slots[z, 4:6, 0:32] = gains[...].astype(BF16).astype(F32)
    small_slots[z, 6:8, 0:32] = biases[...].astype(BF16).astype(F32)
    small_slots[z] = pltpu.roll(small_slots[z], 32 * z, 1)
    bucket_row = jnp.where(forced_width[...] < 4, forced_width[...], width_route[...])
    token_rows[z] = jnp.zeros((8, 128), F32)
    token_rows[z, 0:1, :] = head_count[...].astype(F32)
    token_rows[z, 1:2, :] = bucket_row.astype(F32)
    token_rows[z, 2:3, :] = jnp.where(slot_index[...] >= 0, 1.0, 0.0)
    loads[0].wait()
    for c in range(3):
        for head in range(8):
            at = 256 * c + 128 * (head % 2)
            pack_q[head // 2, :, at : at + 128] = own_q[:, c, head, :].astype(BF16)
    wait(loads[1:])

    def pack(i, carry):
        rows = span(i, 16)
        pack_u[rows, :] = own_u[rows, :].astype(BF16)
        pack_d[rows, :] = own_d[rows, :].astype(BF16)
        for head in range(8):
            pack_o[head, rows, :] = own_o[head, rows, :].astype(BF16)
        return carry

    lax.fori_loop(0, 2, pack, 0)
    greeted()

    def to_group(moves):
        copies = []
        for k in (2, 1, 3):
            for src, dst in moves(ring(z, k)):
                copies.append(links.go(src, dst, links.zs[k]))
        for src, dst in moves(z):
            copies.append(keep(src, dst))
        return copies

    def to_all(ref, peers):
        return [links.go(ref, ref, peers[k]) for k in (1, 2, 3)]

    flying_q = to_group(lambda to: [(pack_q.at[to], wq.at[x, y, own_32, :])])
    flying_s = to_all(small_slots.at[z], links.zs)
    flying_t = to_all(token_rows.at[z], links.zs)
    flying_o = to_group(
        lambda to: [(pack_o.at[2 * to + h], wo.at[x, y, own_32, pl.ds(128 * h, 128)]) for h in (0, 1)]
    )
    flying_f = to_group(
        lambda to: [
            (pack_d.at[:, span(to, 1024)], wd.at[x, y, own_32, :]),
            (pack_u.at[:, span(to, 1024)], wu.at[x, y, own_32, :]),
        ]
    )
    ring_q = Gather(links, (wq, pl.ds(0, 384)), (wq, pl.ds(384, 384)))
    ring_o = Gather(links, (wo, pl.ds(0, 128)), (wo, pl.ds(128, 128)))
    ring_d = Gather(links, (wd, pl.ds(0, 512)), (wd, pl.ds(512, 512)))
    ring_u = Gather(links, (wu, pl.ds(0, 512)), (wu, pl.ds(512, 512)))
    wait(flying_q)
    ring_q.advance()
    wait(flying_s)
    small_grid[x, y] = small_slots[0] + small_slots[1] + small_slots[2] + small_slots[3]
    wait(to_all(small_grid.at[x, y], links.xs))
    flying_s = to_all(small_grid.at[:, y], links.ys)
    ring_q.advance()
    wait(flying_s)
    for p in range(16):
        small[:, 128 * p : 128 * p + 128] = small_grid[p // 4, p % 4]
    ring_q.advance()

    def norm_one(i, carry):
        rows = span(i, 16)
        scaled, inverse = norm_parts(rows_in[rows, :].astype(F32))
        n_one[rows, :] = scaled
        info[0, rows, :] = columns_tile([inverse])
        a_one[span(z * 8 + i, 16), :] = (scaled * small[4:5, :] + small[6:7, :]).astype(BF16)
        return carry

    lax.fori_loop(0, 8, norm_one, 0)
    rows_one = Spread(links, a_one).start()
    branch[own_rows, :] = cotangent[...]
    wait(flying_t)
    for row in range(4):
        tokens[row] = as_columns(token_rows[row])
    ring_q.advance()
    wait(flying_o)
    wait(flying_f)
    ring_o.advance()
    ring_d.advance()
    rows_one.finish()
    rows_branch = Spread(links, branch).start()
    ring_q.advance()
    ring_o.advance()
    ring_d.advance()
    ring_u.advance()

    for c in range(3):
        part = wq[:, :, :, 256 * c : 256 * c + 256].reshape(2048, 256)
        wide[:, 256 * c : 256 * c + 256] = dot(a_one[...], part, (1, 0))
    ring_o.advance()
    ring_d.advance()
    lane = lax.broadcasted_iota(jnp.int32, (128, 128), 1)
    causal = lax.broadcasted_iota(jnp.int32, (128, 128), 0) >= lane
    turned_sines = jnp.where(lane < 64, -sines[...], sines[...])
    scale = 128 ** (-0.5)

    def spots(index):
        row, head = lax.div(index, 2), lax.rem(index, 2)
        used = jnp.where((core * 8 + z * 2 + head).astype(F32) < tokens[row][:, 0:1], 1.0, 0.0)
        return span(row, 128), [span(2 * c + head, 128) for c in range(3)], used

    def attend(index, carry):
        rows, (q_at, k_at, v_at), used = spots(index)

        def rotate(value):
            return value * cosines[...] + turn(value) * turned_sines

        q = (rotate(wide[rows, q_at]) * scale).astype(BF16)
        k = rotate(wide[rows, k_at]).astype(BF16)
        v = wide[rows, v_at].astype(BF16)
        qkv[rows, q_at], qkv[rows, k_at], qkv[rows, v_at] = q, k, v
        scores = jnp.where(causal, dot(q, k, (1, 1)), -1e30)
        powers = jnp.exp(scores - jnp.max(scores, axis=-1, keepdims=True))
        share = powers / jnp.sum(powers, axis=-1, keepdims=True)
        probs[index] = share
        mixed[rows, q_at] = (dot(share.astype(BF16), v, (1, 0)) * used).astype(BF16)
        return carry

    lax.fori_loop(0, 4, attend, 0)
    ring_o.advance()
    ring_u.advance()
    lax.fori_loop(4, 8, attend, 0)
    ring_o.advance()
    merge_one = Merge(links, mixed, wo, set_a, merged).cross().along()
    rows_branch.finish()
    ring_d.advance()
    ring_u.advance()
    merge_one.sum().finish()

    def norm_two(i, carry):
        rows = span(i, 16)
        value = rows_in[rows, :].astype(F32) + merged[rows, :]
        hidden[rows, :] = value
        scaled, inverse = norm_parts(value)
        n_two[rows, :] = scaled
        low = (scaled * small[5:6, :] + small[7:8, :]).astype(BF16)
        a_two[span(z * 8 + i, 16), :] = low
        low = low.astype(F32)
        logits = [jnp.sum(low * small[b : b + 1, :], axis=-1, keepdims=True) for b in range(4)]
        top = jnp.maximum(jnp.maximum(logits[0], logits[1]), jnp.maximum(logits[2], logits[3]))
        powers = [jnp.exp(logit - top) for logit in logits]
        whole = powers[0] + powers[1] + powers[2] + powers[3]
        chances = [power / whole for power in powers]
        own = tokens[z, rows, :]
        bucket, kept = own[:, 1:2], own[:, 2:3]
        gate = jnp.zeros_like(bucket)
        for b in range(4):
            gate = jnp.where(bucket == b, chances[b], gate)
        info[1, rows, :] = columns_tile([inverse, gate, *chances])
        gates[z, rows, :] = columns_tile([gate * kept])
        return carry

    lax.fori_loop(0, 8, norm_two, 0)
    rows_two = Spread(links, a_two).start()
    gate_rows[z] = gates[z].T[0:8, :]
    flying_g = to_all(gate_rows.at[z], links.zs)
    ring_d.advance()

    def units_back(t, carry):
        at = span(t, 256)
        wide[:, at] = dot(branch[...], wd[:, :, :, at].reshape(2048, 256), (1, 0))
        return carry

    lax.fori_loop(0, 4, units_back, 0)
    ring_u.advance()
    rows_two.finish()
    wait(flying_g)
    for row in range(4):
        gates[row] = as_columns(gate_rows[row])
    ring_u.advance()
    quarter = (core * 2 + lax.div(z, 2)).astype(F32)
    used_units = tokens[...].reshape(512, 128)[:, 1:2] >= quarter
    gate_all = gates[...].reshape(512, 128)[:, 0:1]
    gate_part[...] = jnp.zeros((8, 512), F32)

    def units(t, carry):
        at = span(t, 256)
        up = dot(a_two[...], wu[:, :, :, at].reshape(2048, 256), (1, 0))
        up = jnp.where(used_units, jnp.maximum(up, 0.0), 0.0)
        low = (up * up).astype(BF16)
        act[:, at] = low
        back = wide[:, at]
        up_low[:, at] = (back * gate_all * 2.0 * up).astype(BF16)
        pairs = (low.astype(F32) * back).astype(BF16)
        gate_part[...] += dot(jnp.ones((8, 256), BF16), pairs, (1, 1))
        return carry

    lax.fori_loop(0, 4, units, 0)
    crossing_g = links.go(gate_part, gate_near, links.partner)
    merge_u = Merge(links, up_low, wu, set_b, merged_too).cross()
    crossing_g.wait()
    gate_part[...] = gate_part[...] + gate_near[...]
    flying_g = [
        links.go(gate_part.at[:, span(ring(z, k), 128)], gate_far.at[k - 1], links.zs[k]) for k in (1, 2, 3)
    ]
    merge_u.along()

    def outer(left, right, target):
        def one(i, carry):
            value = dot(left[:, span(i, 256)], right[...], (0, 0)).astype(BF16)
            row, first = lax.div(i, 2), lax.rem(i, 2) * 2
            target[row, first] = value[0:128]
            target[row, first + 1] = value[128:256]
            return carry

        lax.fori_loop(0, 8, one, 0)

    outer(a_two, up_low, wu)
    sums_u = Scatter(links, (wu, pl.ds(0, 512)), (wu, pl.ds(512, 512)), buffers[0:8])
    sums_d = Scatter(links, (wd, pl.ds(0, 512)), (wd, pl.ds(512, 512)), buffers[8:16])
    sums_q = Scatter(links, (wq, pl.ds(0, 384)), (wq, pl.ds(384, 384)), buffers[16:24])
    sums_o = Scatter(links, (wo, pl.ds(0, 128)), (wo, pl.ds(128, 128)), buffers[24:32])
    sums_u.advance()
    merge_f = Merge(links, act, wd, set_a, merged).cross().along(leave=False)
    wait(flying_g)
    gate_far[3] = gate_part[:, own_rows] + gate_far[0] + gate_far[1] + gate_far[2]
    gate_grads = as_columns(gate_far[3])
    sums_u.advance()
    merge_u.sum()
    info[2] = gate_grads
    small_sum[...] = jnp.zeros_like(small_sum)
    merge_u.finish()

    def back_two(i, carry):
        rows = span(i, 16)
        upstream = cotangent[rows, :].astype(F32)
        own, tile = tokens[z, rows, :], info[1, rows, :]
        bucket, kept = own[:, 1:2], own[:, 2:3]
        inverse, gate = tile[:, 0:1], tile[:, 1:2]
        gate_grad = info[2, rows, :][:, 0:1] * kept
        low = a_two[span(z * 8 + i, 16), :].astype(F32)
        grad = merged_too[rows, :].astype(BF16).astype(F32)
        for b in range(4):
            hot = jnp.where(bucket == b, 1.0, 0.0)
            logit_grad = tile[:, 2 + b : 3 + b] * (hot - gate) * gate_grad
            grad = grad + logit_grad * small[b : b + 1, :]
            small_sum[b] += fold(logit_grad * low)
        scaled = n_two[rows, :]
        small_sum[5] += fold(grad * scaled)
        small_sum[7] += fold(grad)
        back = upstream + norm_back(scaled, inverse, small[5:6, :], grad)
        n_two[rows, :] = back
        hidden_low[span(z * 8 + i, 16), :] = back.astype(BF16)
        return carry

    lax.fori_loop(0, 8, back_two, 0)
    rows_back = Spread(links, hidden_low).start()

    def branch_rows(i, carry):
        rows = span(i, 16)
        gate = gates[lax.div(i, 8), span(lax.rem(i, 8), 16), :][:, 0:1]
        branch[rows, :] = (branch[rows, :].astype(F32) * gate).astype(BF16)
        return carry

    lax.fori_loop(0, 32, branch_rows, 0)
    outer(branch, act, wd)
    sums_d.advance()
    sums_u.advance()
    rows_back.finish()
    merge_f.leave()

    d_mixed[...] = dot(hidden_low[...], wo[...].reshape(2048, 256), (1, 0)).astype(BF16)
    outer(hidden_low, mixed, wo)
    sums_o.advance()
    sums_u.advance()

    def attend_back(index, carry):
        rows, (q_at, k_at, v_at), used = spots(index)
        share = probs[index]
        q, k, v = qkv[rows, q_at], qkv[rows, k_at], qkv[rows, v_at]
        grad = (d_mixed[rows, q_at].astype(F32) * used).astype(BF16)
        value_grad = dot(share.astype(BF16), grad, (0, 0))
        share_grad = dot(grad, v, (1, 1))
        inner = jnp.sum(share * share_grad, axis=-1, keepdims=True)
        score_grad = (share * (share_grad - inner)).astype(BF16)

        def rotate_back(value):
            return value * cosines[...] - turn(value * sines[...]) * jnp.where(lane < 64, -1.0, 1.0)

        d_qkv[rows, q_at] = rotate_back(dot(score_grad, k, (1, 0)) * scale).astype(BF16)
        d_qkv[rows, k_at] = rotate_back(dot(score_grad, q, (0, 0))).astype(BF16)
        d_qkv[rows, v_at] = value_grad.astype(BF16)
        return carry

    lax.fori_loop(0, 8, attend_back, 0)
    sums_u.advance()
    sums_d.advance()
    merge_f.sum()
    merge_q = Merge(links, d_qkv, wq, set_b, merged_too).cross().along()
    outer(a_one, d_qkv, wq)
    sums_q.advance()
    moved_u = to_group(lambda to: [(wu.at[x, y, span(to, 32), :], up_grad.at[:, span(z, 1024)])])
    sums_d.advance()
    sums_o.advance()
    merge_f.finish()

    def output_rows(i, carry):
        rows = span(i, 16)
        tile, kept = info[1, rows, :], tokens[z, rows, :][:, 2:3]
        produced = merged[rows, :].astype(BF16).astype(F32) * kept
        block_out[rows, :] = (hidden[rows, :] + tile[:, 1:2] * produced).astype(BF16)
        return carry

    lax.fori_loop(0, 8, output_rows, 0)
    wait(moved_u)
    wait(later)

    def add_squares(number, weight, update):
        squares[2 * number] += fold_lanes(weight * weight)
        squares[2 * number + 1] += fold_lanes(update * update)

    squares[...] = jnp.zeros_like(squares)

    def squares_wide(number, weights, grads):
        def one(i, carry):
            at = lax.div(i, 4), lax.rem(i, 4)
            rows, columns = span(at[0], 16), span(at[1], 1024)
            weight = weights[rows, columns]
            _, _, update = moment_step(
                weight, grads[rows, columns].astype(F32), mom_f[0, rows, columns], mom_f[1, rows, columns], DECAY_RATE
            )
            add_squares(number, weight, update)
            return carry

        lax.fori_loop(0, 8, one, 0)

    squares_wide(2, own_u, up_grad)
    later = [keep(down_m, mom_f.at[0]), keep(down_v, mom_f.at[1])]
    merge_q.sum().finish()

    def back_one(i, carry):
        rows = span(i, 16)
        grad = merged_too[rows, :]
        scaled, inverse = n_one[rows, :], info[0, rows, :][:, 0:1]
        small_sum[4] += fold(grad * scaled)
        small_sum[6] += fold(grad)
        input_grad[rows, :] = n_two[rows, :] + norm_back(scaled, inverse, small[4:5, :], grad)
        return carry

    lax.fori_loop(0, 8, back_one, 0)
    for r in range(8):
        small[r : r + 1, :] = jnp.sum(small_sum[r], axis=0, keepdims=True)

    copies = [links.go(small.at[:, span(ring(x, k), 512)], sx_in.at[k], links.xs[k]) for k in (1, 2, 3)]
    sums_q.advance()
    sums_d.advance()
    sums_o.advance()
    wait(copies)
    sx_in[0] = small[:, span(x, 512)] + sx_in[1] + sx_in[2] + sx_in[3]
    copies = [
        links.go(sx_in.at[0, :, span(ring(y, k), 128)], sy_in.at[k], links.ys[k]) for k in (1, 2, 3)
    ]
    sums_d.advance()
    moved_d = to_group(lambda to: [(wd.at[x, y, span(to, 32), :], down_grad.at[:, span(z, 1024)])])
    wait(copies)
    sz_in[z] = sx_in[0, :, span(y, 128)] + sy_in[1] + sy_in[2] + sy_in[3]
    flying_s = to_all(sz_in.at[z], links.zs)
    sums_q.advance()
    sums_o.advance()
    sums_q.advance()
    sums_o.advance()
    moved_o = to_group(
        lambda to: [
            (wo.at[x, y, span(to, 32), pl.ds(128 * h, 128)], out_grad.at[2 * z + h]) for h in (0, 1)
        ]
    )
    wait(moved_d)
    wait(later)
    squares_wide(3, own_d, down_grad)
    wait(flying_s)
    small_slots[0] = pltpu.roll(sz_in[0] + sz_in[1] + sz_in[2] + sz_in[3], 128 - 32 * z, 1)
    small_grad[...] = small_slots[0]
    sums_q.advance()
    moved_q = to_group(lambda to: [(wq.at[x, y, span(to, 32), :], got_q.at[z])])
    wait(moved_o)

    def squares_out(head, carry):
        _, _, update = moment_step(
            own_o[head], out_grad[head].astype(F32), mom_o[0, head], mom_o[1, head], DECAY_RATE
        )
        add_squares(1, own_o[head], update)
        return carry

    lax.fori_loop(0, 8, squares_out, 0)
    _, _, update = moment_step(
        router_w[...], small_slots[0, 0:4, 0:32], router_m[...], router_v[...], DECAY_RATE
    )
    squares[8, 0:4, 0:32] = 0.5 * router_w[...] * router_w[...]
    squares[9, 0:4, 0:32] = 0.5 * update * update
    wait(moved_q)
    for c in range(3):
        for head in range(8):
            at = 256 * c + 128 * (head % 2)
            qkv_grad[:, c, head, :] = got_q[head // 2, :, at : at + 128].astype(F32)

    def squares_qkv(i, carry):
        rows = pl.ds(i * 4, 4)
        _, _, update = moment_step(
            own_q[rows], qkv_grad[rows], mom_q[0, rows], mom_q[1, rows], DECAY_RATE
        )
        squares[0] += jnp.sum(jnp.sum(own_q[rows] * own_q[rows], axis=0), axis=0)
        squares[1] += jnp.sum(jnp.sum(update * update, axis=0), axis=0)
        return carry

    lax.fori_loop(0, 8, squares_qkv, 0)

    lanes = lax.broadcasted_iota(jnp.int32, (8, 128), 1)
    tile = jnp.zeros((8, 128), F32)
    for number in range(10):
        value = jnp.sum(jnp.sum(squares[number], axis=0, keepdims=True), axis=1, keepdims=True)
        tile = jnp.where(lanes == number // 2 + 5 * (number % 2), value, tile)
    for axis, (me, peers) in enumerate(
        ((core, {1: links.partner}), (z, links.zs), (y, links.ys), (x, links.xs))
    ):
        slots[axis, me] = tile
        here = slots.at[axis, me]
        wait([links.go(here, here, peer) for peer in peers.values()])
        tile = slots[axis, 0] + slots[axis, 1]
        if axis:
            tile = tile + slots[axis, 2] + slots[axis, 3]
    norms[...] = tile


def layer(*operands):
    def vmem(*shape, kind=BF16):
        return pltpu.VMEM(shape, kind)

    def merge_buffers():
        return [vmem(512, 1024), vmem(512, 1024), vmem(3, 128, 1024)]

    def sum_buffers(width):
        return [
            vmem(2, 4, 64, width), vmem(2, 4, 128, width), vmem(2, 64, width), vmem(2, 128, width),
        ] * 2

    rows = vmem(128, 2048, kind=F32)
    return pl.pallas_call(
        layer_kernel,
        out_shape=(
            jax.ShapeDtypeStruct((128, 2048), BF16),
            jax.ShapeDtypeStruct((128, 2048), F32),
            jax.ShapeDtypeStruct((32, 3, 8, 128), F32),
            jax.ShapeDtypeStruct((8, 32, 128), BF16),
            jax.ShapeDtypeStruct((32, 4096), BF16),
            jax.ShapeDtypeStruct((32, 4096), BF16),
            jax.ShapeDtypeStruct((8, 128), F32),
            jax.ShapeDtypeStruct((8, 128), F32),
        ),
        in_specs=[ANY] * 12 + [VMEM] * 13,
        out_specs=(VMEM,) * 8,
        scratch_shapes=[
            vmem(32, 3, 8, 128, kind=F32), vmem(8, 32, 128, kind=F32), vmem(32, 4096, kind=F32),
            vmem(32, 4096, kind=F32),
            vmem(4, 32, 768), vmem(8, 32, 128), vmem(32, 4096), vmem(32, 4096),
            vmem(2, 32, 3, 8, 128, kind=F32), vmem(2, 8, 32, 128, kind=F32), vmem(2, 32, 4096, kind=F32),
            vmem(4, 4, 128, 768), vmem(4, 4, 128, 256), vmem(4, 4, 128, 1024), vmem(4, 4, 128, 1024),
            vmem(4, 8, 128, kind=F32), vmem(4, 4, 8, 128, kind=F32), vmem(8, 2048, kind=F32),
            vmem(4, 8, 128, kind=F32), vmem(4, 128, 128, kind=F32), vmem(4, 8, 128, kind=F32),
            vmem(4, 128, 128, kind=F32), vmem(3, 128, 128, kind=F32),
            vmem(512, 2048), vmem(512, 2048), vmem(512, 2048), vmem(512, 2048),
            rows, rows, rows, rows, rows,
            vmem(512, 1024, kind=F32), vmem(512, 768), vmem(8, 128, 128, kind=F32),
            vmem(512, 256), vmem(512, 256), vmem(512, 768), vmem(512, 1024), vmem(512, 1024),
            *merge_buffers(), *merge_buffers(), vmem(512, 256, kind=F32),
            vmem(8, 512, kind=F32), vmem(8, 512, kind=F32), vmem(4, 8, 128, kind=F32),
            vmem(8, 8, 2048, kind=F32), vmem(4, 8, 512, kind=F32), vmem(4, 8, 128, kind=F32),
            vmem(4, 8, 128, kind=F32), vmem(4, 32, 768), vmem(10, 8, 128, kind=F32), vmem(4, 4, 8, 128, kind=F32),
            *sum_buffers(512), *sum_buffers(512), *sum_buffers(384), *sum_buffers(128),
            DMA((40,)), DMA((LINK_COPIES,)), DMA((LINK_COPIES,)),
        ],
        compiler_params=pltpu.CompilerParams(
            collective_id=0, has_side_effects=True, vmem_limit_bytes=63 * 2**20
        ),
        name="layer",
    )(*operands)


def renew_kernel(norms, small_grad, gains, biases, norm_m, norm_v, *refs):
    ins, outs = refs[:20], refs[20:]
    sums = norms[0:1, :]
    for index in range(5):
        weight, grad, m, v = (ref[...] for ref in ins[4 * index : 4 * index + 4])
        grad = grad[0:4, 0:32] if index == 4 else grad.astype(F32)
        first, second, update = moment_step(weight, grad, m, v, DECAY_RATE)
        ratio = LEARN_RATE * (jnp.sqrt(sums[:, index : index + 1]) / jnp.sqrt(sums[:, index + 5 : index + 6]))
        ratio = ratio.reshape((1,) * weight.ndim)
        new = weight - ratio * update
        for ref, value in zip(outs[5 * index : 5 * index + 5], (grad, first, second, new, new.astype(BF16))):
            ref[...] = value
    grad = small_grad[4:8, 0:32]
    master = jnp.concatenate([gains[...], biases[...]], axis=0)
    first, second, update = moment_step(master, grad, norm_m[...], norm_v[...], 0.0)
    new = master - NORM_RATE * update
    for ref, value in zip(outs[25:30], (grad, first, second, new, new.astype(BF16))):
        ref[...] = value
    row = lax.broadcasted_iota(jnp.int32, (8, 128), 0)
    lane = lax.broadcasted_iota(jnp.int32, (8, 128), 1)
    tile = jnp.zeros((8, 128), F32)
    for index in range(10):
        here = (row == index % 5) & (lane == index // 5)
        tile = jnp.where(here, jnp.sqrt(sums[:, index : index + 1]), tile)
    outs[30][...] = tile[0:5, 0:2]


def renew(norms, small_grad, gains, biases, norm_m, norm_v, *matrices):
    steps = 4

    def whole(shape):
        return pl.BlockSpec(shape, lambda i: (0,) * len(shape))

    blocks = (
        pl.BlockSpec((32 // steps, 3, 8, 128), lambda i: (i, 0, 0, 0)),
        pl.BlockSpec((8 // steps, 32, 128), lambda i: (i, 0, 0)),
        pl.BlockSpec((32, 4096 // steps), lambda i: (0, i)),
        pl.BlockSpec((32, 4096 // steps), lambda i: (0, i)),
        whole((4, 32)),
    )
    shapes = ((32, 3, 8, 128), (8, 32, 128), (32, 4096), (32, 4096), (4, 32), (4, 32))
    in_specs = [whole((8, 128)), whole((8, 128)), whole((2, 32)), whole((2, 32)), whole((4, 32)), whole((4, 32))]
    out_specs, out_shape = [], []
    for index, block in enumerate(blocks):
        in_specs += [block, whole((8, 128)) if index == 4 else block, block, block]
    for block, shape in zip((*blocks, whole((4, 32))), shapes):
        out_specs += [block] * 5
        out_shape += [jax.ShapeDtypeStruct(shape, kind) for kind in (F32, F32, F32, F32, BF16)]
    out_specs.append(whole((5, 2)))
    out_shape.append(jax.ShapeDtypeStruct((5, 2), F32))
    return pl.pallas_call(
        renew_kernel,
        grid=(steps,),
        in_specs=in_specs,
        out_specs=out_specs,
        out_shape=out_shape,
        compiler_params=pltpu.CompilerParams(vmem_limit_bytes=63 * 2**20),
        name="renew",
    )(norms, small_grad, gains, biases, norm_m, norm_v, *matrices)


def rotary_tables(length, size):
    half_size = size // 2
    frequency = ROPE_BASE ** (-(np.arange(half_size) * 2.0 / size))
    angles = np.arange(length)[:, None] * frequency[None, :]
    cosine_table = np.concatenate([np.cos(angles), np.cos(angles)], axis=-1)
    sine_table = np.concatenate([np.sin(angles), np.sin(angles)], axis=-1)
    return (cosine_table.astype(np.float32), sine_table.astype(np.float32))


def local(
    block_input,
    cotangent,
    head_count,
    width_route,
    forced_width,
    slot_index,
    qkv_weight,
    out_weight,
    up_weight,
    down_weight,
    router_weight,
    norm_gains,
    norm_biases,
    qkv_first,
    qkv_second,
    out_first,
    out_second,
    up_first,
    up_second,
    down_first,
    down_second,
    router_first,
    router_second,
    norm_first,
    norm_second,
):
    def turned(value):
        return value.transpose(0, 2, 1)

    out = turned(out_weight), turned(out_first), turned(out_second)
    down = down_weight.T, down_first.T, down_second.T
    router = router_weight.T, router_first.T, router_second.T
    block_output, input_grad, *grads, small_grad, norms = layer(
        qkv_weight, out[0], up_weight, down[0],
        qkv_first, qkv_second, *out[1:], up_first, up_second, *down[1:],
        *router, norm_gains, norm_biases,
        *(value.reshape(1, -1) for value in (head_count, width_route, forced_width, slot_index)),
        block_input, cotangent, *rotary_tables(128, 128),
    )
    *results, lamb_norms = renew(
        norms, small_grad, norm_gains, norm_biases, norm_first, norm_second,
        qkv_weight, grads[0], qkv_first, qkv_second,
        out[0], grads[1], *out[1:],
        up_weight, grads[2], up_first, up_second,
        down[0], grads[3], *down[1:],
        router[0], small_grad, *router[1:],
    )
    kinds = []
    for kind in range(5):
        qkv, out, up, down, router, norm = (results[5 * index + kind] for index in range(6))
        kinds += [qkv, turned(out), up, down.T, router.T, norm]
    return (block_output, input_grad, *kinds, lamb_norms)


def solution(mesh):
    qkv, out = P("dp", None, "mp", None), P("mp", None, "dp")
    up, down, router, norms = P("dp", "mp"), P("mp", "dp"), P("dp", None), P(None, "dp")
    rows, tokens = P("dp", None), P("dp")
    matrices = (qkv, out, up, down, router)
    return jax.shard_map(
        local,
        mesh=mesh,
        in_specs=(
            rows, rows, tokens, tokens, tokens, tokens,
            *matrices, norms, norms,
            qkv, qkv, out, out, up, up, down, down, router, router, norms, norms,
        ),
        out_specs=(rows, rows, *((*matrices, norms) * 5), P()),
        check_vma=False,
    )
```

time: 283 us -> 236 us (0.83)
  other arithmetic: 19.9 us -> 0 us
  local copies, waits for them, and re-layouts: 16.4 us -> 3.19 us
  between operations: 9.77 us -> 1.36 us
  Pallas kernels: 236 us -> 231 us
    reduce_sum x6 -> x0, other arithmetic: 8.76 us -> none  [the longest x5 8.15 us: local(): jnp.sum(stepped[index][2] * stepped[index][2]) * shares[index]]
    convert_element_type x10 -> x0, other arithmetic: 8.18 us -> none  [the longest x5 6.8 us: local(): value.astype(BF16)]
    pallas_call x1, Pallas kernels: 14.4 us -> 6.68 us  [renew(): pl.pallas_call(renew_kernel, grid=(steps,), in_specs=in_specs, out_specs=...]
    concatenate x1 -> x0, local copies, waits for them, and re-layouts: 5.35 us -> none  [local(): jnp.concatenate([jnp.stack(squares), jnp.zeros((118,), F32)])[None]]
    unnamed x76 -> x7, local copies, waits for them, and re-layouts: 5.91 us -> 3.19 us
where the time goes in v3:
time: 236 us; the launch traced here: 235 us
  Pallas kernels  231 us (98%)
  local copies, waits for them, and re-layouts  3.19 us (1%)
    pallas_call x1, Pallas kernels, layer(): pl.pallas_call(layer_kernel, out_shape=(jax.ShapeDtypeStruct((128, 2048),...  224 us
    pallas_call x1, Pallas kernels, renew(): pl.pallas_call(renew_kernel, grid=(steps,), in_specs=in_specs, out_specs=...  6.68 us

profile of v3, /device:TPU:0, one launch (start us, length us, event | category | flops | bytes accessed | tf_op | source)
XLA Modules:
  0.0 235.4 jit_solution(16680618722557557955)
XLA Ops:
  1.3 224.2 %layer.1 = (bf16[128,2048]{1,0:T(8,128)(2,1)}, f32[128,2048]{1,0:T(8,128)}, f32[32,3,8,128]{3,2,1,0:T(8,128)}, bf16[8,32,128]{2,1,0:T(8,128)(2,1)}, bf16[32,4096...) custom-call(f32[32,3,8,128]{3,2,1,0:T(8,128)} %refs_0_.1, ...), custom_call_target="tpu_custom_call" | custom-call | tf_op jit(solution)/shard_map/layer/pallas_call | solution.py:826
  225.5 0.0 copy-start.1
  225.5 6.7 %renew.1 = (f32[32,3,8,128]{3,2,1,0:T(8,128)}, f32[32,3,8,128]{3,2,1,0:T(8,128)}, f32[32,3,8,128]{3,2,1,0:T(8,128)}, f32[32,3,8,128]{3,2,1,0:T(8,128)}, bf16[32,...) custom-call(f32[8,128]{1,0:T(8,128)} %get-tuple-element.74.norms, ...), custom_call_target="tpu_custom_call" | custom-call | tf_op jit(solution)/shard_map/renew/pallas_call | solution.py:917
  232.2 0.0 copy-start
  232.2 1.4 copy.60
  233.6 0.0 copy-done.1
  233.6 0.8 copy.64
  234.4 0.0 copy-done
  234.4 1.0 copy.65
Async XLA Ops:
  225.5 8.1 %copy-start.1 = (bf16[128,2048]{1,0:T(8,128)(2,1)S(1)}, bf16[128,2048]{1,0:T(8,128)(2,1)}, u32[]{:S(2)}) copy-start(bf16[128,2048]{1,0:T(8,128)(2,1)} %get-tuple-element.177) | copy-start | bytes 1572868
  232.2 2.2 copy-start

commit v4 on v3

v4 whole, which is shorter than its diff:
```python
import jax
import jax.numpy as jnp
import numpy as np
from jax import lax
from jax.experimental import pallas as pl
from jax.experimental.pallas import tpu as pltpu
from jax.sharding import PartitionSpec as P

STEP = 5

BETA_ONE = 0.5
BETA_TWO = 0.5
ADAM_EPS = 1e-06
DECAY_RATE = 0.01
LEARN_RATE = 0.5
NORM_RATE = 0.1
NORM_EPS = 1e-05
ROPE_BASE = 10000.0

MESH = pl.DeviceIdType.MESH
BF16 = jnp.bfloat16
F32 = jnp.float32
VMEM = pl.BlockSpec(memory_space=pltpu.VMEM)
ANY = pl.BlockSpec(memory_space=pl.ANY)
DMA = pltpu.SemaphoreType.DMA
ALL = slice(None)
LOW, HIGH = pl.ds(0, 64), pl.ds(64, 64)


def place():
    index = lax.axis_index("dp")
    return lax.div(index, 16), lax.rem(lax.div(index, 4), 4), lax.rem(index, 4), lax.axis_index("mp")


def ring(value, step):
    return lax.rem(value + (step + 4), 4)


def device(x, y, z, core):
    return (x * 16 + y * 4 + z, core)


def greet(peers):
    barrier = pltpu.get_barrier_semaphore()
    for peer in peers:
        pl.semaphore_signal(barrier, inc=1, device_id=peer, device_id_type=MESH)
    return lambda: pl.semaphore_wait(barrier, len(peers))


def send(src, dst, send_sem, recv_sem, peer):
    copy = pltpu.make_async_remote_copy(
        src_ref=src, dst_ref=dst, send_sem=send_sem, recv_sem=recv_sem, device_id=peer, device_id_type=MESH
    )
    copy.start()
    return copy


def span(index, size):
    return pl.ds(pl.multiple_of(index * size, size), size)


def dot(left, right, dims):
    return lax.dot_general(left, right, ((dims[:1], dims[1:]), ((), ())), preferred_element_type=F32)


class Links:
    def __init__(self, send_sems, recv_sems):
        self.x, self.y, self.z, self.core = x, y, z, core = place()
        self.xs = {k: device(ring(x, k), y, z, core) for k in (1, 2, 3)}
        self.ys = {k: device(x, ring(y, k), z, core) for k in (1, 2, 3)}
        self.zs = {k: device(x, y, ring(z, k), core) for k in (1, 2, 3)}
        self.others = {k: device(x, y, ring(z, k), 1 - core) for k in (1, 2, 3)}
        self.partner = device(x, y, z, 1 - core)
        self.send_sems, self.recv_sems, self.used = send_sems, recv_sems, 0

    def go(self, src, dst, peer):
        number = self.used
        self.used += 1
        return send(src, dst, self.send_sems.at[number], self.recv_sems.at[number], peer)


class Gather:
    def __init__(self, links, first, second):
        self.links, self.parts, self.number, self.copies = links, (first, second), 0, []

    def advance(self):
        for copy in self.copies:
            copy.wait()
        x, y = self.links.x, self.links.y
        xp, xm, yp, ym = self.links.xs[1], self.links.xs[3], self.links.ys[1], self.links.ys[3]
        xb, xa, yb, ya = ring(x, -1), ring(x, 1), ring(y, -1), ring(y, 1)
        moves = {
            0: (((x, y, ALL), xp), ((x, y, ALL), xm), ((x, y, ALL), yp), ((x, y, ALL), ym)),
            1: (((xb, y, LOW), xp), ((xa, y, HIGH), xm), ((x, yb, LOW), yp), ((x, ya, HIGH), ym)),
            2: (((ALL, y, ALL), yp), ((ALL, y, ALL), ym), ((x, ALL, ALL), xp), ((x, ALL, ALL), xm)),
            3: (((ALL, yb, LOW), yp), ((ALL, ya, HIGH), ym), ((xb, ALL, LOW), xp), ((xa, ALL, HIGH), xm)),
        }.get(self.number, ())
        self.number += 1
        self.copies = []
        for index, (where, peer) in enumerate(moves):
            ref, columns = self.parts[index // 2]
            block = ref.at[where + (columns,)]
            self.copies.append(self.links.go(block, block, peer))


def add_into(ref, blocks, columns, sources, row, count):
    steps = count // 16

    def one(index, carry):
        number = lax.div(index, steps)
        step = pl.multiple_of(lax.rem(index, steps) * 16, 16)
        to = blocks[1](number) + (pl.ds(row + step, 16), columns)
        here = ref[to].astype(F32)
        for source, first_row in sources:
            place_in = ((number,) if blocks[0] > 1 else ()) + (pl.ds(first_row + step, 16), ALL)
            here = here + source[place_in].astype(F32)
        ref[to] = here.astype(BF16)
        return carry

    lax.fori_loop(0, blocks[0] * steps, one, 0)


class Scatter:
    def __init__(self, links, first, second, buffers):
        self.links, self.parts = links, (first, second)
        self.buffers = (buffers[:4], buffers[4:])
        self.number, self.halves, self.rest = 0, [], []

    def lanes(self, phase):
        x, y = self.links.x, self.links.y
        found = []
        for part in (0, 1):
            ref, columns = self.parts[part]
            along_y = part == phase
            peers = self.links.ys if along_y else self.links.xs
            if phase == 0 and along_y:
                where, count, each = (lambda k: (ALL, ring(y, k))), 4, (lambda k: lambda i: (i, ring(y, k)))
            elif phase == 0:
                where, count, each = (lambda k: (ring(x, k), ALL)), 4, (lambda k: lambda i: (ring(x, k), i))
            elif along_y:
                where, count, each = (lambda k: (x, ring(y, k))), 1, (lambda k: lambda i: (x, ring(y, k)))
            else:
                where, count, each = (lambda k: (ring(x, k), y)), 1, (lambda k: lambda i: (ring(x, k), y))
            one, two = self.buffers[part][2 * phase : 2 * phase + 2]
            found.append((ref, columns, where, count, each, peers, one, two))
        return found

    def begin(self, phase):
        self.halves, self.rest = [], []
        for ref, columns, where, count, each, peers, one, two in self.lanes(phase):
            self.halves.append(self.links.go(ref.at[where(2) + (LOW, columns)], one.at[0], peers[1]))
            self.halves.append(self.links.go(ref.at[where(2) + (HIGH, columns)], one.at[1], peers[3]))
        for ref, columns, where, count, each, peers, one, two in self.lanes(phase):
            lead = (ALL,) if count > 1 else ()
            self.rest.append(
                self.links.go(ref.at[where(1) + (HIGH, columns)], two.at[(0,) + lead + (HIGH,)], peers[1])
            )
            self.rest.append(
                self.links.go(ref.at[where(-1) + (LOW, columns)], two.at[(1,) + lead + (LOW,)], peers[3])
            )

    def middle(self, phase):
        lanes = self.lanes(phase)
        for side in (0, 1):
            for part in (0, 1):
                ref, columns, where, count, each, peers, one, two = lanes[part]
                lead = (ALL,) if count > 1 else ()
                step, rows, row = ((1, LOW, 0), (-1, HIGH, 64))[side]
                self.halves[2 * part + side].wait()
                add_into(ref, (count, each(step)), columns, [(one.at[side], 0)], row, 64)
                self.rest.append(
                    self.links.go(
                        ref.at[where(step) + (rows, columns)], two.at[(side,) + lead + (rows,)], peers[(1, 3)[side]]
                    )
                )

    def end(self, phase):
        for copy in self.rest:
            copy.wait()
        for ref, columns, where, count, each, peers, one, two in self.lanes(phase):
            add_into(ref, (count, each(0)), columns, [(two.at[0], 0), (two.at[1], 0)], 0, 128)

    def advance(self):
        if self.number == 0:
            self.begin(0)
        elif self.number == 1:
            self.middle(0)
        elif self.number == 2:
            self.end(0)
            self.begin(1)
        elif self.number == 3:
            self.middle(1)
        elif self.number == 4:
            self.end(1)
        self.number += 1


class Spread:
    def __init__(self, links, ref):
        self.links, self.ref = links, ref

    def start(self, own=True):
        links = self.links
        here = self.ref.at[links.z, links.core]
        self.passed = [links.go(here, here, links.partner)] if own else []
        self.flying = [links.go(here, here, links.zs[k]) for k in (1, 3)]

    def relay(self):
        links = self.links
        self.far = []
        for side, k, rows in ((0, 1, pl.ds(0, 32)), (1, 3, pl.ds(32, 32))):
            self.flying[side].wait_recv()
            block = self.ref.at[ring(links.z, -k), links.core]
            half = block.at[rows]
            self.far.append(links.go(half, half, links.zs[k]))
            self.passed.append(links.go(block, block, links.partner))

    def finish(self):
        links = self.links
        for copy in self.far:
            copy.wait_recv()
        block = self.ref.at[ring(links.z, 2), links.core]
        self.passed.append(links.go(block, block, links.partner))
        for copy in self.flying + self.far:
            copy.wait_send()
        for copy in self.passed:
            copy.wait()


TILES, TILE = 4, 512


class Merge:
    def __init__(self, links, left, weights, buffers, out):
        self.links, self.left, self.weights, self.out = links, left, weights, out
        self.near, self.near_in, self.far_in, self.tmp = buffers
        self.crossing, self.flying = [], []

    def tile(self, half, j):
        rows = self.weights[j]
        left = self.left[:, half]
        return dot(left.reshape(256, left.shape[-1]), rows.reshape(TILE, rows.shape[-1]), (1, 1))

    def cross(self):
        for j in range(TILES):
            self.near[j] = self.tile(1 - self.links.core, j).astype(BF16).reshape(4, 64, TILE)
            self.crossing.append(self.links.go(self.near.at[j], self.near_in.at[j], self.links.partner))

    def along(self, leave=True):
        for j in range(TILES):
            value = self.tile(self.links.core, j)
            self.crossing[j].wait()
            value = value + self.near_in[j].astype(F32).reshape(256, TILE)
            self.tmp[...] = value
            self.near[j] = value.astype(BF16).reshape(4, 64, TILE)
            if leave:
                self.leave(j)
            self.out[:, TILE * j : TILE * j + TILE] = self.tmp[span(self.links.z, 64), :]

    def leave(self, j=None):
        links = self.links
        for k in (2, 1, 3):
            if j is None:
                src, dst = self.near.at[:, ring(links.z, k)], self.far_in.at[k - 1]
            else:
                src, dst = self.near.at[j, ring(links.z, k)], self.far_in.at[k - 1, j]
            self.flying.append(links.go(src, dst, links.zs[k]))

    def arrive(self):
        for copy in self.flying:
            copy.wait()

    def rows(self, rows):
        value = self.out[rows, :]
        for k in range(3):
            parts = [self.far_in[k, j, rows, :] for j in range(TILES)]
            value = value + jnp.concatenate(parts, axis=1).astype(F32)
        return value


def norm_parts(value):
    centre = value - jnp.mean(value, axis=-1, keepdims=True)
    inverse = lax.rsqrt(jnp.mean(centre * centre, axis=-1, keepdims=True) + NORM_EPS)
    return centre * inverse, inverse


def norm_back(scaled, inverse, gain_row, upstream):
    dscaled = upstream * gain_row
    inner = (
        dscaled
        - jnp.mean(dscaled, axis=-1, keepdims=True)
        - scaled * jnp.mean(dscaled * scaled, axis=-1, keepdims=True)
    )
    return inner * inverse


def fold(value):
    return value[0:8, :] + value[8:16, :]


def fold_lanes(value):
    total = None
    for row in range(0, value.shape[0], 8):
        for lane in range(0, value.shape[1], 128):
            part = value[row : row + 8, lane : lane + 128]
            total = part if total is None else total + part
    return total


def columns_tile(columns):
    lane = lax.broadcasted_iota(jnp.int32, (16, 128), 1)
    tile = jnp.zeros((16, 128), F32)
    for index, column in enumerate(columns):
        tile = jnp.where(lane == index, column, tile)
    return tile


def as_columns(rows):
    return jnp.concatenate([rows, jnp.zeros((120, 128), F32)], axis=0).T


def turn(value):
    return pltpu.roll(value, 64, 1)


def moment_step(weight, gradient, first_moment, second_moment, decay_rate):
    first_moment = BETA_ONE * first_moment + (1.0 - BETA_ONE) * gradient
    second_moment = BETA_TWO * second_moment + (1.0 - BETA_TWO) * gradient * gradient
    update = (
        first_moment
        / (1.0 - BETA_ONE**STEP)
        / (jnp.sqrt(second_moment / (1.0 - BETA_TWO**STEP)) + ADAM_EPS)
        + decay_rate * weight
    )
    return (first_moment, second_moment, update)


LINK_COPIES = 324
LOCAL_COPIES = 28


def layer_kernel(
    qkv_w, out_w, up_w, down_w, qkv_m, qkv_v, out_m, out_v, up_m, up_v, down_m, down_v, block_in, cotangent,
    router_w, router_m, router_v, gains, biases, head_count, width_route, forced_width, slot_index, cosines, sines,
    block_out, input_grad, qkv_grad, out_grad, up_grad, down_grad, small_grad, norms,
    own_q, own_o, own_u, own_d, pack_q, pack_o, pack_u, pack_d, mom_q, mom_o, mom_f,
    wq, wo, wu, wd, small_slots, small_grid, small, small_near,
    token_rows, tokens, gate_slots, gates, info,
    a_one, a_two, branch, hidden_low,
    rows_in, upstream_in, hidden, n_one, n_two, merged, merged_too, out_rows, grad_rows,
    wide, qkv, probs, mixed, d_mixed, d_qkv, act, up_low,
    near_a, near_in_a, far_in_a, near_b, near_in_b, far_in_b, tmp,
    gate_part, gate_near, gate_far, small_sum, sx_in, sy_in, sz_in, got_q, squares, slots,
    *rest,
):
    buffers, (local_sems, send_sems, recv_sems) = rest[:-3], rest[-3:]
    links = Links(send_sems, recv_sems)
    x, y, z, core = links.x, links.y, links.z, links.core
    own_32, own_64 = span(z, 32), span(core, 64)
    set_a = (near_a, near_in_a, far_in_a, tmp)
    set_b = (near_b, near_in_b, far_in_b, tmp)
    local_used, pending = [0], {}

    def keep(src, dst):
        copy = pltpu.make_async_copy(src, dst, local_sems.at[local_used[0]])
        local_used[0] += 1
        copy.start()
        return copy

    def wait(name):
        for copy in pending.pop(name):
            copy.wait()

    def in_blocks(count, step):
        def one(i, carry):
            step(i, span(i, 16))
            return carry

        lax.fori_loop(0, count, one, 0)

    def to_group(moves):
        copies = []
        for k in (2, 1, 3):
            for src, dst in moves(ring(z, k)):
                copies.append(links.go(src, dst, links.zs[k]))
        for src, dst in moves(z):
            copies.append(keep(src, dst))
        return copies

    def to_all(ref, *sets):
        return [links.go(ref, ref, peer) for peers in sets for peer in peers.values()]

    def begin():
        greeted = greet(
            [*links.xs.values(), *links.ys.values(), *links.zs.values(), *links.others.values(), links.partner]
        )
        loads = [keep(qkv_w, own_q), keep(out_w, own_o), keep(up_w, own_u), keep(down_w, own_d)]
        pending["rows"] = [keep(block_in.at[own_64], rows_in), keep(cotangent.at[own_64], upstream_in)]
        pending["branch"] = [keep(cotangent.at[pl.ds(64 * h, 64)], branch.at[z, h]) for h in (0, 1)]
        pending["mom_u"] = [keep(up_m, mom_f.at[0]), keep(up_v, mom_f.at[1])]
        pending["mom_q"] = [keep(qkv_m, mom_q.at[0]), keep(qkv_v, mom_q.at[1])]
        pending["mom_o"] = [keep(out_m, mom_o.at[0]), keep(out_v, mom_o.at[1])]
        small_slots[z] = jnp.zeros((8, 128), F32)
        small_slots[z, 0:4, 0:32] = router_w[...].astype(BF16).astype(F32)
        small_slots[z, 4:6, 0:32] = gains[...].astype(BF16).astype(F32)
        small_slots[z, 6:8, 0:32] = biases[...].astype(BF16).astype(F32)
        small_slots[z] = pltpu.roll(small_slots[z], 32 * z, 1)
        bucket_row = jnp.where(forced_width[...] < 4, forced_width[...], width_route[...])
        token_rows[z] = jnp.zeros((8, 128), F32)
        token_rows[z, 0:1, :] = head_count[...].astype(F32)
        token_rows[z, 1:2, :] = bucket_row.astype(F32)
        token_rows[z, 2:3, :] = jnp.where(slot_index[...] >= 0, 1.0, 0.0)
        gates[z] = jnp.zeros((128, 128), F32)
        gate_part[...] = jnp.zeros_like(gate_part)
        small_sum[...] = jnp.zeros_like(small_sum)
        squares[...] = jnp.zeros_like(squares)
        loads[0].wait()
        for c in range(3):
            for head in range(8):
                at = 256 * c + 128 * (head % 2)
                pack_q[head // 2, :, at : at + 128] = own_q[:, c, head, :].astype(BF16)
        for load in loads[1:]:
            load.wait()

        def pack(i, rows):
            pack_u[rows, :] = own_u[rows, :].astype(BF16)
            pack_d[rows, :] = own_d[rows, :].astype(BF16)
            for head in range(8):
                pack_o[head, rows, :] = own_o[head, rows, :].astype(BF16)

        in_blocks(2, pack)
        wait("rows")
        wait("branch")
        greeted()

    ring_q = Gather(links, (wq, pl.ds(0, 384)), (wq, pl.ds(384, 384)))
    ring_o = Gather(links, (wo, pl.ds(0, 128)), (wo, pl.ds(128, 128)))
    ring_d = Gather(links, (wd, pl.ds(0, 512)), (wd, pl.ds(512, 512)))
    ring_u = Gather(links, (wu, pl.ds(0, 512)), (wu, pl.ds(512, 512)))

    def slices_q():
        pending["q"] = to_group(lambda to: [(pack_q.at[to], wq.at[x, y, own_32, :])])
        pending["small"] = to_all(small_slots.at[z], links.zs)
        pending["tokens"] = to_all(token_rows.at[z], links.zs)

    def slices_o():
        pending["o"] = to_group(
            lambda to: [(pack_o.at[2 * to + h], wo.at[x, y, own_32, pl.ds(128 * h, 128)]) for h in (0, 1)]
        )

    def slices_d():
        pending["d"] = to_group(lambda to: [(pack_d.at[:, span(to, 1024)], wd.at[x, y, own_32, :])])

    def slices_u():
        pending["u"] = to_group(lambda to: [(pack_u.at[:, span(to, 1024)], wu.at[x, y, own_32, :])])

    def small_x():
        wait("small")
        small_grid[x, y] = small_slots[0] + small_slots[1] + small_slots[2] + small_slots[3]
        pending["small"] = to_all(small_grid.at[x, y], links.xs)

    def small_y():
        wait("small")
        pending["small"] = to_all(small_grid.at[:, y], links.ys)

    def small_rows():
        wait("small")
        for p in range(16):
            small[:, 128 * p : 128 * p + 128] = small_grid[p // 4, p % 4]

    def token_columns():
        wait("tokens")
        for row in range(4):
            tokens[row] = as_columns(token_rows[row])

    rows_one, rows_branch = Spread(links, a_one), Spread(links, branch)
    rows_two, rows_back = Spread(links, a_two), Spread(links, hidden_low)

    def norm_one():
        def step(i, rows):
            scaled, inverse = norm_parts(rows_in[rows, :].astype(F32))
            n_one[rows, :] = scaled
            info[0, rows, :] = columns_tile([inverse])

        in_blocks(4, step)

    def rows_one_start():
        def step(i, rows):
            a_one[z, core, rows, :] = (n_one[rows, :] * small[4:5, :] + small[6:7, :]).astype(BF16)

        in_blocks(4, step)
        rows_one.start()

    lane = lax.broadcasted_iota(jnp.int32, (128, 128), 1)
    causal = lax.broadcasted_iota(jnp.int32, (128, 128), 0) >= lane
    scale = 128 ** (-0.5)

    def queries():
        for c in range(3):
            part = wq[:, :, :, 256 * c : 256 * c + 256].reshape(2048, 256)
            wide[:, 256 * c : 256 * c + 256] = dot(a_one[...].reshape(512, 2048), part, (1, 0))

    def spots(index):
        row, head = lax.div(index, 2), lax.rem(index, 2)
        used = jnp.where((core * 8 + z * 2 + head).astype(F32) < tokens[row][:, 0:1], 1.0, 0.0)
        return row, span(row, 128), [span(2 * c + head, 128) for c in range(3)], used

    def attend(first, last):
        turned_sines = jnp.where(lane < 64, -sines[...], sines[...])

        def one(index, carry):
            row, rows, (q_at, k_at, v_at), used = spots(index)

            def rotate(value):
                return value * cosines[...] + turn(value) * turned_sines

            q = (rotate(wide[rows, q_at]) * scale).astype(BF16)
            k = rotate(wide[rows, k_at]).astype(BF16)
            v = wide[rows, v_at].astype(BF16)
            qkv[rows, q_at], qkv[rows, k_at], qkv[rows, v_at] = q, k, v
            scores = jnp.where(causal, dot(q, k, (1, 1)), -1e30)
            powers = jnp.exp(scores - jnp.max(scores, axis=-1, keepdims=True))
            share = powers / jnp.sum(powers, axis=-1, keepdims=True)
            probs[index] = share
            mixed[row, :, :, q_at] = (dot(share.astype(BF16), v, (1, 0)) * used).astype(BF16).reshape(2, 64, 128)
            return carry

        lax.fori_loop(first, last, one, 0)

    merge_one = Merge(links, mixed, wo, set_a, merged)

    def norm_two():
        def step(i, rows):
            value = rows_in[rows, :].astype(F32) + merge_one.rows(rows)
            hidden[rows, :] = value
            scaled, inverse = norm_parts(value)
            n_two[rows, :] = scaled
            low = (scaled * small[5:6, :] + small[7:8, :]).astype(BF16)
            a_two[z, core, rows, :] = low
            low = low.astype(F32)
            logits = [jnp.sum(low * small[b : b + 1, :], axis=-1, keepdims=True) for b in range(4)]
            top = jnp.maximum(jnp.maximum(logits[0], logits[1]), jnp.maximum(logits[2], logits[3]))
            powers = [jnp.exp(logit - top) for logit in logits]
            whole = powers[0] + powers[1] + powers[2] + powers[3]
            chances = [power / whole for power in powers]
            at = span(core * 4 + i, 16)
            own = tokens[z, at, :]
            bucket, kept = own[:, 1:2], own[:, 2:3]
            gate = jnp.zeros_like(bucket)
            for b in range(4):
                gate = jnp.where(bucket == b, chances[b], gate)
            info[1, rows, :] = columns_tile([inverse, gate, *chances])
            gates[z, at, :] = columns_tile([gate * kept])

        in_blocks(4, step)

    def rows_two_start():
        rows_two.start()
        gate_slots[z, core] = gates[z].T[0:8, :]
        pending["gates"] = to_all(gate_slots.at[z, core], links.zs, links.others, {0: links.partner})

    def rows_two_finish():
        rows_two.finish()
        wait("gates")
        for row in range(4):
            gates[row] = as_columns(gate_slots[row, 0] + gate_slots[row, 1])

    def units_back():
        def one(t, carry):
            at = span(t, 256)
            wide[:, at] = dot(branch[...].reshape(512, 2048), wd[:, :, :, at].reshape(2048, 256), (1, 0))
            return carry

        lax.fori_loop(0, 4, one, 0)

    def units():
        quarter = (core * 2 + lax.div(z, 2)).astype(F32)
        used_units = tokens[...].reshape(512, 128)[:, 1:2] >= quarter
        gate_all = gates[...].reshape(512, 128)[:, 0:1]

        def one(t, carry):
            at = span(t, 256)
            up = dot(a_two[...].reshape(512, 2048), wu[:, :, :, at].reshape(2048, 256), (1, 0))
            up = jnp.where(used_units, jnp.maximum(up, 0.0), 0.0)
            low = (up * up).astype(BF16)
            act[:, :, :, at] = low.reshape(4, 2, 64, 256)
            back = wide[:, at]
            up_low[:, :, :, at] = (back * gate_all * 2.0 * up).astype(BF16).reshape(4, 2, 64, 256)
            pairs = (low.astype(F32) * back).astype(BF16)
            gate_part[...] += dot(jnp.ones((8, 256), BF16), pairs, (1, 1))
            return carry

        lax.fori_loop(0, 4, one, 0)
        pending["gate"] = [links.go(gate_part, gate_near, links.partner)]

    merge_u = Merge(links, up_low, wu, set_b, merged_too)
    merge_f = Merge(links, act, wd, set_a, merged)

    def merge_u_out():
        merge_u.cross()
        wait("gate")
        gate_part[...] = gate_part[...] + gate_near[...]
        pending["gate"] = [
            links.go(gate_part.at[:, span(ring(z, k), 128)], gate_far.at[k - 1], links.zs[k]) for k in (1, 2, 3)
        ]
        merge_u.along()

    def merge_u_in():
        wait("gate")
        gate_far[3] = gate_part[:, span(z, 128)] + gate_far[0] + gate_far[1] + gate_far[2]
        info[2] = as_columns(gate_far[3])
        merge_u.arrive()

    def branch_rows():
        def step(i, rows):
            token = lax.rem(i, 8)
            gate = gates[lax.div(i, 8), span(token, 16), :][:, 0:1]
            at = (lax.div(i, 8), lax.div(token, 4), span(lax.rem(token, 4), 16))
            branch[at] = (branch[at].astype(F32) * gate).astype(BF16)

        in_blocks(32, step)

    def outer(left, right, target):
        def one(i, carry):
            part = left[:, :, :, span(i, 256)].reshape(512, 256)
            value = dot(part, right[...].reshape(512, right.shape[-1]), (0, 0)).astype(BF16)
            row, first = lax.div(i, 2), lax.rem(i, 2) * 2
            target[row, first] = value[0:128]
            target[row, first + 1] = value[128:256]
            return carry

        lax.fori_loop(0, 8, one, 0)

    def back_two():
        def step(i, rows):
            at = span(core * 4 + i, 16)
            upstream = upstream_in[rows, :].astype(F32)
            own, tile = tokens[z, at, :], info[1, rows, :]
            bucket, kept = own[:, 1:2], own[:, 2:3]
            inverse, gate = tile[:, 0:1], tile[:, 1:2]
            gate_grad = info[2, at, :][:, 0:1] * kept
            low = a_two[z, core, rows, :].astype(F32)
            grad = merge_u.rows(rows).astype(BF16).astype(F32)
            for b in range(4):
                hot = jnp.where(bucket == b, 1.0, 0.0)
                logit_grad = tile[:, 2 + b : 3 + b] * (hot - gate) * gate_grad
                grad = grad + logit_grad * small[b : b + 1, :]
                small_sum[b] += fold(logit_grad * low)
            scaled = n_two[rows, :]
            small_sum[5] += fold(grad * scaled)
            small_sum[7] += fold(grad)
            back = upstream + norm_back(scaled, inverse, small[5:6, :], grad)
            n_two[rows, :] = back
            hidden_low[z, core, rows, :] = back.astype(BF16)

        in_blocks(4, step)

    def mixed_back():
        d_mixed[...] = dot(hidden_low[...].reshape(512, 2048), wo[...].reshape(2048, 256), (1, 0)).astype(BF16)

    def attend_back():
        def one(index, carry):
            row, rows, (q_at, k_at, v_at), used = spots(index)
            share = probs[index]
            q, k, v = qkv[rows, q_at], qkv[rows, k_at], qkv[rows, v_at]
            grad = (d_mixed[rows, q_at].astype(F32) * used).astype(BF16)
            value_grad = dot(share.astype(BF16), grad, (0, 0))
            share_grad = dot(grad, v, (1, 1))
            inner = jnp.sum(share * share_grad, axis=-1, keepdims=True)
            score_grad = (share * (share_grad - inner)).astype(BF16)

            def rotate_back(value):
                return value * cosines[...] - turn(value * sines[...]) * jnp.where(lane < 64, -1.0, 1.0)

            def put(at, value):
                d_qkv[row, :, :, at] = value.astype(BF16).reshape(2, 64, 128)

            put(q_at, rotate_back(dot(score_grad, k, (1, 0)) * scale))
            put(k_at, rotate_back(dot(score_grad, q, (0, 0))))
            put(v_at, value_grad)
            return carry

        lax.fori_loop(0, 8, one, 0)

    merge_q = Merge(links, d_qkv, wq, set_b, merged_too)
    sums_u = Scatter(links, (wu, pl.ds(0, 512)), (wu, pl.ds(512, 512)), buffers[0:8])
    sums_d = Scatter(links, (wd, pl.ds(0, 512)), (wd, pl.ds(512, 512)), buffers[8:16])
    sums_q = Scatter(links, (wq, pl.ds(0, 384)), (wq, pl.ds(384, 384)), buffers[16:24])
    sums_o = Scatter(links, (wo, pl.ds(0, 128)), (wo, pl.ds(128, 128)), buffers[24:32])

    def output_rows():
        merge_f.arrive()

        def step(i, rows):
            kept = tokens[z, span(core * 4 + i, 16), :][:, 2:3]
            produced = merge_f.rows(rows).astype(BF16).astype(F32) * kept
            out_rows[rows, :] = (hidden[rows, :] + info[1, rows, :][:, 1:2] * produced).astype(BF16)

        in_blocks(4, step)
        here = block_out.at[own_64]
        pending["output"] = [keep(out_rows, here), links.go(out_rows, here, links.partner)]

    def back_one():
        merge_q.arrive()

        def step(i, rows):
            grad = merge_q.rows(rows)
            scaled, inverse = n_one[rows, :], info[0, rows, :][:, 0:1]
            small_sum[4] += fold(grad * scaled)
            small_sum[6] += fold(grad)
            grad_rows[rows, :] = n_two[rows, :] + norm_back(scaled, inverse, small[4:5, :], grad)

        in_blocks(4, step)
        for r in range(8):
            small[r : r + 1, :] = jnp.sum(small_sum[r], axis=0, keepdims=True)
        pending["small"] = [links.go(small, small_near, links.partner)]
        here = input_grad.at[own_64]
        pending["input"] = [keep(grad_rows, here), links.go(grad_rows, here, links.partner)]

    def small_to_x():
        wait("small")
        small[...] = small[...] + small_near[...]
        pending["small"] = [
            links.go(small.at[:, span(ring(x, k), 512)], sx_in.at[k], links.xs[k]) for k in (1, 2, 3)
        ]

    def small_to_y():
        wait("small")
        sx_in[0] = small[:, span(x, 512)] + sx_in[1] + sx_in[2] + sx_in[3]
        pending["small"] = [
            links.go(sx_in.at[0, :, span(ring(y, k), 128)], sy_in.at[k], links.ys[k]) for k in (1, 2, 3)
        ]

    def small_to_z():
        wait("small")
        sz_in[z] = sx_in[0, :, span(y, 128)] + sy_in[1] + sy_in[2] + sy_in[3]
        pending["small"] = to_all(sz_in.at[z], links.zs)

    def small_done():
        wait("small")
        small_grad[...] = pltpu.roll(sz_in[0] + sz_in[1] + sz_in[2] + sz_in[3], 128 - 32 * z, 1)
        _, _, update = moment_step(
            router_w[...], small_grad[0:4, 0:32], router_m[...], router_v[...], DECAY_RATE
        )
        squares[8, 0:4, 0:32] = 0.5 * router_w[...] * router_w[...]
        squares[9, 0:4, 0:32] = 0.5 * update * update

    def owners_u():
        pending["own_u"] = to_group(lambda to: [(wu.at[x, y, span(to, 32), :], up_grad.at[:, span(z, 1024)])])

    def owners_d():
        pending["own_d"] = to_group(lambda to: [(wd.at[x, y, span(to, 32), :], down_grad.at[:, span(z, 1024)])])

    def owners_o():
        pending["own_o"] = to_group(
            lambda to: [
                (wo.at[x, y, span(to, 32), pl.ds(128 * h, 128)], out_grad.at[2 * z + h]) for h in (0, 1)
            ]
        )

    def owners_q():
        pending["own_q"] = to_group(lambda to: [(wq.at[x, y, span(to, 32), :], got_q.at[z])])

    def squares_wide(number, weights, grads):
        def one(i, carry):
            rows, columns = span(lax.div(i, 4), 16), span(lax.rem(i, 4), 1024)
            weight = weights[rows, columns]
            _, _, update = moment_step(
                weight, grads[rows, columns].astype(F32), mom_f[0, rows, columns], mom_f[1, rows, columns], DECAY_RATE
            )
            squares[2 * number] += fold_lanes(weight * weight)
            squares[2 * number + 1] += fold_lanes(update * update)
            return carry

        lax.fori_loop(0, 8, one, 0)

    def squares_u():
        wait("own_u")
        wait("mom_u")
        squares_wide(2, own_u, up_grad)
        pending["mom_d"] = [keep(down_m, mom_f.at[0]), keep(down_v, mom_f.at[1])]

    def squares_d():
        wait("own_d")
        wait("mom_d")
        squares_wide(3, own_d, down_grad)

    def squares_o():
        wait("own_o")
        wait("mom_o")

        def one(head, carry):
            weight = own_o[head]
            _, _, update = moment_step(
                weight, out_grad[head].astype(F32), mom_o[0, head], mom_o[1, head], DECAY_RATE
            )
            squares[2] += fold_lanes(weight * weight)
            squares[3] += fold_lanes(update * update)
            return carry

        lax.fori_loop(0, 8, one, 0)

    def squares_q():
        wait("own_q")
        wait("mom_q")
        for c in range(3):
            for head in range(8):
                at = 256 * c + 128 * (head % 2)
                qkv_grad[:, c, head, :] = got_q[head // 2, :, at : at + 128].astype(F32)

        def one(i, carry):
            rows = pl.ds(i * 4, 4)
            weight = own_q[rows]
            _, _, update = moment_step(weight, qkv_grad[rows], mom_q[0, rows], mom_q[1, rows], DECAY_RATE)
            squares[0] += jnp.sum(jnp.sum(weight * weight, axis=0), axis=0)
            squares[1] += jnp.sum(jnp.sum(update * update, axis=0), axis=0)
            return carry

        lax.fori_loop(0, 8, one, 0)

    def totals():
        lanes = lax.broadcasted_iota(jnp.int32, (8, 128), 1)
        tile = jnp.zeros((8, 128), F32)
        for number in range(10):
            value = jnp.sum(jnp.sum(squares[number], axis=0, keepdims=True), axis=1, keepdims=True)
            tile = jnp.where(lanes == number // 2 + 5 * (number % 2), value, tile)
        here = 4 * core + z
        sets = ((links.zs, links.others, {0: links.partner}), (links.ys,), (links.xs,))
        for axis, (me, peers) in enumerate(zip((here, y, x), sets)):
            slots[axis, me] = tile
            for copy in to_all(slots.at[axis, me], *peers):
                copy.wait()
            tile = slots[axis, 0]
            for k in range(1, 8 if axis == 0 else 4):
                tile = tile + slots[axis, k]
        norms[...] = tile

    begin()
    slices_q()
    small_x()
    wait("q")
    ring_q.advance()
    slices_o()
    wait("o")
    ring_o.advance()
    slices_u()
    rows_branch.start(own=False)
    slices_d()
    ring_q.advance()
    norm_one()
    small_y()
    ring_o.advance()
    ring_q.advance()
    small_rows()
    rows_one_start()
    token_columns()
    wait("d")
    ring_d.advance()
    ring_q.advance()
    rows_one.relay()
    ring_d.advance()
    ring_o.advance()
    ring_q.advance()
    wait("u")
    ring_u.advance()
    rows_one.finish()
    rows_branch.relay()
    queries()
    ring_o.advance()
    ring_d.advance()
    attend(0, 4)
    ring_u.advance()
    attend(4, 8)
    ring_o.advance()
    merge_one.cross()
    merge_one.along()
    ring_u.advance()
    merge_one.arrive()
    ring_d.advance()
    norm_two()
    rows_two_start()
    rows_branch.finish()
    ring_u.advance()
    rows_two.relay()
    ring_d.advance()
    units_back()
    rows_two_finish()
    ring_u.advance()
    units()
    merge_u_out()
    outer(a_two, up_low, wu)
    sums_u.advance()
    merge_f.cross()
    merge_f.along(leave=False)
    merge_u_in()
    back_two()
    rows_back.start()
    branch_rows()
    outer(branch, act, wd)
    sums_d.advance()
    rows_back.relay()
    rows_back.finish()
    mixed_back()
    sums_u.advance()
    attend_back()
    sums_d.advance()
    merge_q.cross()
    merge_q.along()
    sums_u.advance()
    outer(a_one, d_qkv, wq)
    sums_q.advance()
    back_one()
    merge_f.leave()
    sums_d.advance()
    outer(hidden_low, mixed, wo)
    small_to_x()
    sums_q.advance()
    sums_u.advance()
    sums_u.advance()
    sums_o.advance()
    sums_d.advance()
    small_to_y()
    sums_q.advance()
    owners_u()
    sums_o.advance()
    sums_d.advance()
    owners_d()
    sums_q.advance()
    sums_o.advance()
    small_to_z()
    output_rows()
    sums_q.advance()
    owners_q()
    small_done()
    sums_o.advance()
    squares_u()
    sums_o.advance()
    owners_o()
    squares_d()
    squares_q()
    squares_o()
    totals()
    wait("output")
    wait("input")


def layer(*operands):
    def vmem(*shape, kind=BF16):
        return pltpu.VMEM(shape, kind)

    def merge_buffers():
        return [vmem(TILES, 4, 64, TILE), vmem(TILES, 4, 64, TILE), vmem(3, TILES, 64, TILE)]

    def sum_buffers(width):
        return [
            vmem(2, 4, 64, width), vmem(2, 4, 128, width), vmem(2, 64, width), vmem(2, 128, width),
        ] * 2

    rows, rows_low, tokens = vmem(64, 2048, kind=F32), vmem(64, 2048), vmem(4, 2, 64, 2048)
    tile = vmem(4, 8, 128, kind=F32)
    return pl.pallas_call(
        layer_kernel,
        out_shape=(
            jax.ShapeDtypeStruct((128, 2048), BF16),
            jax.ShapeDtypeStruct((128, 2048), F32),
            jax.ShapeDtypeStruct((32, 3, 8, 128), F32),
            jax.ShapeDtypeStruct((8, 32, 128), BF16),
            jax.ShapeDtypeStruct((32, 4096), BF16),
            jax.ShapeDtypeStruct((32, 4096), BF16),
            jax.ShapeDtypeStruct((8, 128), F32),
            jax.ShapeDtypeStruct((8, 128), F32),
        ),
        in_specs=[ANY] * 14 + [VMEM] * 11,
        out_specs=(ANY, ANY) + (VMEM,) * 6,
        scratch_shapes=[
            vmem(32, 3, 8, 128, kind=F32), vmem(8, 32, 128, kind=F32), vmem(32, 4096, kind=F32),
            vmem(32, 4096, kind=F32),
            vmem(4, 32, 768), vmem(8, 32, 128), vmem(32, 4096), vmem(32, 4096),
            vmem(2, 32, 3, 8, 128, kind=F32), vmem(2, 8, 32, 128, kind=F32), vmem(2, 32, 4096, kind=F32),
            vmem(4, 4, 128, 768), vmem(4, 4, 128, 256), vmem(4, 4, 128, 1024), vmem(4, 4, 128, 1024),
            tile, vmem(4, 4, 8, 128, kind=F32), vmem(8, 2048, kind=F32), vmem(8, 2048, kind=F32),
            tile, vmem(4, 128, 128, kind=F32), vmem(4, 2, 8, 128, kind=F32), vmem(4, 128, 128, kind=F32),
            vmem(3, 128, 128, kind=F32),
            tokens, tokens, tokens, tokens,
            rows_low, rows_low, rows, rows, rows, rows, rows, rows_low, rows,
            vmem(512, 1024, kind=F32), vmem(512, 768), vmem(8, 128, 128, kind=F32),
            vmem(4, 2, 64, 256), vmem(512, 256), vmem(4, 2, 64, 768), vmem(4, 2, 64, 1024), vmem(4, 2, 64, 1024),
            *merge_buffers(), *merge_buffers(), vmem(256, TILE, kind=F32),
            vmem(8, 512, kind=F32), vmem(8, 512, kind=F32), tile,
            vmem(8, 8, 2048, kind=F32), vmem(4, 8, 512, kind=F32), tile, tile,
            vmem(4, 32, 768), vmem(10, 8, 128, kind=F32), vmem(3, 8, 8, 128, kind=F32),
            *sum_buffers(512), *sum_buffers(512), *sum_buffers(384), *sum_buffers(128),
            DMA((LOCAL_COPIES,)), DMA((LINK_COPIES,)), DMA((LINK_COPIES,)),
        ],
        compiler_params=pltpu.CompilerParams(
            collective_id=0, has_side_effects=True, vmem_limit_bytes=63 * 2**20
        ),
        name="layer",
    )(*operands)


def renew_kernel(norms, small_grad, gains, biases, norm_m, norm_v, *refs):
    ins, outs = refs[:20], refs[20:]
    sums = norms[0:1, :]
    for index in range(5):
        weight, grad, m, v = (ref[...] for ref in ins[4 * index : 4 * index + 4])
        grad = grad[0:4, 0:32] if index == 4 else grad.astype(F32)
        first, second, update = moment_step(weight, grad, m, v, DECAY_RATE)
        ratio = LEARN_RATE * (jnp.sqrt(sums[:, index : index + 1]) / jnp.sqrt(sums[:, index + 5 : index + 6]))
        ratio = ratio.reshape((1,) * weight.ndim)
        new = weight - ratio * update
        for ref, value in zip(outs[5 * index : 5 * index + 5], (grad, first, second, new, new.astype(BF16))):
            ref[...] = value
    grad = small_grad[4:8, 0:32]
    master = jnp.concatenate([gains[...], biases[...]], axis=0)
    first, second, update = moment_step(master, grad, norm_m[...], norm_v[...], 0.0)
    new = master - NORM_RATE * update
    for ref, value in zip(outs[25:30], (grad, first, second, new, new.astype(BF16))):
        ref[...] = value
    row = lax.broadcasted_iota(jnp.int32, (8, 128), 0)
    lane = lax.broadcasted_iota(jnp.int32, (8, 128), 1)
    tile = jnp.zeros((8, 128), F32)
    for index in range(10):
        here = (row == index % 5) & (lane == index // 5)
        tile = jnp.where(here, jnp.sqrt(sums[:, index : index + 1]), tile)
    outs[30][...] = tile[0:5, 0:2]


def renew(norms, small_grad, gains, biases, norm_m, norm_v, *matrices):
    steps = 4

    def whole(shape):
        return pl.BlockSpec(shape, lambda i: (0,) * len(shape))

    blocks = (
        pl.BlockSpec((32 // steps, 3, 8, 128), lambda i: (i, 0, 0, 0)),
        pl.BlockSpec((8 // steps, 32, 128), lambda i: (i, 0, 0)),
        pl.BlockSpec((32, 4096 // steps), lambda i: (0, i)),
        pl.BlockSpec((32, 4096 // steps), lambda i: (0, i)),
        whole((4, 32)),
    )
    shapes = ((32, 3, 8, 128), (8, 32, 128), (32, 4096), (32, 4096), (4, 32), (4, 32))
    in_specs = [whole((8, 128)), whole((8, 128)), whole((2, 32)), whole((2, 32)), whole((4, 32)), whole((4, 32))]
    out_specs, out_shape = [], []
    for index, block in enumerate(blocks):
        in_specs += [block, whole((8, 128)) if index == 4 else block, block, block]
    for block, shape in zip((*blocks, whole((4, 32))), shapes):
        out_specs += [block] * 5
        out_shape += [jax.ShapeDtypeStruct(shape, kind) for kind in (F32, F32, F32, F32, BF16)]
    out_specs.append(whole((5, 2)))
    out_shape.append(jax.ShapeDtypeStruct((5, 2), F32))
    return pl.pallas_call(
        renew_kernel,
        grid=(steps,),
        in_specs=in_specs,
        out_specs=out_specs,
        out_shape=out_shape,
        compiler_params=pltpu.CompilerParams(vmem_limit_bytes=63 * 2**20),
        name="renew",
    )(norms, small_grad, gains, biases, norm_m, norm_v, *matrices)


def rotary_tables(length, size):
    half_size = size // 2
    frequency = ROPE_BASE ** (-(np.arange(half_size) * 2.0 / size))
    angles = np.arange(length)[:, None] * frequency[None, :]
    cosine_table = np.concatenate([np.cos(angles), np.cos(angles)], axis=-1)
    sine_table = np.concatenate([np.sin(angles), np.sin(angles)], axis=-1)
    return (cosine_table.astype(np.float32), sine_table.astype(np.float32))


def local(
    block_input,
    cotangent,
    head_count,
    width_route,
    forced_width,
    slot_index,
    qkv_weight,
    out_weight,
    up_weight,
    down_weight,
    router_weight,
    norm_gains,
    norm_biases,
    qkv_first,
    qkv_second,
    out_first,
    out_second,
    up_first,
    up_second,
    down_first,
    down_second,
    router_first,
    router_second,
    norm_first,
    norm_second,
):
    def turned(value):
        return value.transpose(0, 2, 1)

    out = turned(out_weight), turned(out_first), turned(out_second)
    down = down_weight.T, down_first.T, down_second.T
    router = router_weight.T, router_first.T, router_second.T
    block_output, input_grad, *grads, small_grad, norms = layer(
        qkv_weight, out[0], up_weight, down[0],
        qkv_first, qkv_second, *out[1:], up_first, up_second, *down[1:],
        block_input, cotangent, *router, norm_gains, norm_biases,
        *(value.reshape(1, -1) for value in (head_count, width_route, forced_width, slot_index)),
        *rotary_tables(128, 128),
    )
    *results, lamb_norms = renew(
        norms, small_grad, norm_gains, norm_biases, norm_first, norm_second,
        qkv_weight, grads[0], qkv_first, qkv_second,
        out[0], grads[1], *out[1:],
        up_weight, grads[2], up_first, up_second,
        down[0], grads[3], *down[1:],
        router[0], small_grad, *router[1:],
    )
    kinds = []
    for kind in range(5):
        qkv, out, up, down, router, norm = (results[5 * index + kind] for index in range(6))
        kinds += [qkv, turned(out), up, down.T, router.T, norm]
    return (block_output, input_grad, *kinds, lamb_norms)


def solution(mesh):
    qkv, out = P("dp", None, "mp", None), P("mp", None, "dp")
    up, down, router, norms = P("dp", "mp"), P("mp", "dp"), P("dp", None), P(None, "dp")
    rows, tokens = P("dp", None), P("dp")
    matrices = (qkv, out, up, down, router)
    return jax.shard_map(
        local,
        mesh=mesh,
        in_specs=(
            rows, rows, tokens, tokens, tokens, tokens,
            *matrices, norms, norms,
            qkv, qkv, out, out, up, up, down, down, router, router, norms, norms,
        ),
        out_specs=(rows, rows, *((*matrices, norms) * 5), P()),
        check_vma=False,
    )
```

time: 236 us -> 209 us (0.89)
  Pallas kernels: 231 us -> 204 us
    pallas_call x1, Pallas kernels: 224 us -> 198 us  [layer(): pl.pallas_call(layer_kernel, out_shape=(jax.ShapeDtypeStruct((128, 2048),...]
where the time goes in v4:
time: 209 us
  Pallas kernels  204 us (98%)
  local copies, waits for them, and re-layouts  3.19 us (2%)
    pallas_call x1, Pallas kernels, layer(): pl.pallas_call(layer_kernel, out_shape=(jax.ShapeDtypeStruct((128, 2048),...  198 us
    pallas_call x1, Pallas kernels, renew(): pl.pallas_call(renew_kernel, grid=(steps,), in_specs=in_specs, out_specs=...  6.68 us

profile of v4, /device:TPU:0, one launch (start us, length us, event | category | flops | bytes accessed | tf_op | source)
XLA Modules:
  0.0 208.9 jit_solution(17846752169117790815)
XLA Ops:
  1.3 197.6 %layer.1 = (bf16[128,2048]{1,0:T(8,128)(2,1)}, f32[128,2048]{1,0:T(8,128)}, f32[32,3,8,128]{3,2,1,0:T(8,128)}, bf16[8,32,128]{2,1,0:T(8,128)(2,1)}, bf16[32,4096...) custom-call(f32[32,3,8,128]{3,2,1,0:T(8,128)} %refs_0_.1, ...), custom_call_target="tpu_custom_call" | custom-call | tf_op jit(solution)/shard_map/layer/pallas_call | solution.py:961
  199.0 0.0 copy-start.1
  199.0 6.7 %renew.1 = (f32[32,3,8,128]{3,2,1,0:T(8,128)}, f32[32,3,8,128]{3,2,1,0:T(8,128)}, f32[32,3,8,128]{3,2,1,0:T(8,128)}, f32[32,3,8,128]{3,2,1,0:T(8,128)}, bf16[32,...) custom-call(f32[8,128]{1,0:T(8,128)} %get-tuple-element.74.norms, ...), custom_call_target="tpu_custom_call" | custom-call | tf_op jit(solution)/shard_map/renew/pallas_call | solution.py:1052
  205.7 0.0 copy-start
  205.7 1.4 copy.60
  207.1 0.0 copy-done.1
  207.1 0.8 copy.64
  207.9 0.0 copy-done
  207.9 1.0 copy.65
Async XLA Ops:
  199.0 8.1 %copy-start.1 = (bf16[128,2048]{1,0:T(8,128)(2,1)S(1)}, bf16[128,2048]{1,0:T(8,128)(2,1)}, u32[]{:S(2)}) copy-start(bf16[128,2048]{1,0:T(8,128)(2,1)} %get-tuple-element.177) | copy-start | bytes 1572868
  205.7 2.2 %copy-start = (f32[128,2048]{1,0:T(8,128)S(1)}, f32[128,2048]{1,0:T(8,128)}, u32[]{:S(2)}) copy-start(f32[128,2048]{1,0:T(8,128)} %get-tuple-element.178) | copy-start | bytes 3145732

commit v5 on v4

--- a/solution.py
+++ b/solution.py
@@ -77,6 +77,23 @@
         number = self.used
         self.used += 1
         return send(src, dst, self.send_sems.at[number], self.recv_sems.at[number], peer)
+
+    def together(self, moves, whole):
+        number = self.used
+        self.used += 1
+        sems = self.send_sems.at[number], self.recv_sems.at[number]
+        for src, dst, peer in moves:
+            send(src, dst, *sems, peer)
+        return Bundle(whole, *sems)
+
+
+class Bundle:
+    def __init__(self, whole, *sems):
+        self.whole, self.sems = whole, sems
+
+    def wait(self):
+        for sem in self.sems:
+            pltpu.make_async_copy(self.whole, self.whole, sem).wait()
 
 
 class Gather:
@@ -95,12 +112,18 @@
             2: (((ALL, y, ALL), yp), ((ALL, y, ALL), ym), ((x, ALL, ALL), xp), ((x, ALL, ALL), xm)),
             3: (((ALL, yb, LOW), yp), ((ALL, ya, HIGH), ym), ((xb, ALL, LOW), xp), ((xa, ALL, HIGH), xm)),
         }.get(self.number, ())
+        if moves:
+            pairs = [(self.parts[index // 2][0].at[where + (self.parts[index // 2][1],)], peer)
+                     for index, (where, peer) in enumerate(moves)]
+            ref, columns = self.parts[0]
+            whole = (
+                ref.at[0, :, :, columns], ref.at[0, pl.ds(0, 2), :, columns],
+                ref.at[:, :, :, columns], ref.at[pl.ds(0, 2), :, :, columns],
+            )[self.number]
+            self.copies = [self.links.together([(block, block, peer) for block, peer in pairs], whole)]
+        else:
+            self.copies = []
         self.number += 1
-        self.copies = []
-        for index, (where, peer) in enumerate(moves):
-            ref, columns = self.parts[index // 2]
-            block = ref.at[where + (columns,)]
-            self.copies.append(self.links.go(block, block, peer))
 
 
 def add_into(ref, blocks, columns, sources, row, count):
@@ -147,20 +170,19 @@
 
     def begin(self, phase):
         self.halves, self.rest = [], []
+        links = self.links
         for ref, columns, where, count, each, peers, one, two in self.lanes(phase):
-            self.halves.append(self.links.go(ref.at[where(2) + (LOW, columns)], one.at[0], peers[1]))
-            self.halves.append(self.links.go(ref.at[where(2) + (HIGH, columns)], one.at[1], peers[3]))
+            self.halves.append(links.go(ref.at[where(2) + (LOW, columns)], one.at[0], peers[1]))
+            self.halves.append(links.go(ref.at[where(2) + (HIGH, columns)], one.at[1], peers[3]))
+        moves = []
         for ref, columns, where, count, each, peers, one, two in self.lanes(phase):
             lead = (ALL,) if count > 1 else ()
-            self.rest.append(
-                self.links.go(ref.at[where(1) + (HIGH, columns)], two.at[(0,) + lead + (HIGH,)], peers[1])
-            )
-            self.rest.append(
-                self.links.go(ref.at[where(-1) + (LOW, columns)], two.at[(1,) + lead + (LOW,)], peers[3])
-            )
+            moves.append((ref.at[where(1) + (HIGH, columns)], two.at[(0,) + lead + (HIGH,)], peers[1]))
+            moves.append((ref.at[where(-1) + (LOW, columns)], two.at[(1,) + lead + (LOW,)], peers[3]))
+        self.rest.append(links.together(moves, self.buffers[0][2 * phase + 1]))
 
     def middle(self, phase):
-        lanes = self.lanes(phase)
+        lanes, self.last = self.lanes(phase), []
         for side in (0, 1):
             for part in (0, 1):
                 ref, columns, where, count, each, peers, one, two = lanes[part]
@@ -168,14 +190,14 @@
                 step, rows, row = ((1, LOW, 0), (-1, HIGH, 64))[side]
                 self.halves[2 * part + side].wait()
                 add_into(ref, (count, each(step)), columns, [(one.at[side], 0)], row, 64)
-                self.rest.append(
+                self.last.append(
                     self.links.go(
                         ref.at[where(step) + (rows, columns)], two.at[(side,) + lead + (rows,)], peers[(1, 3)[side]]
                     )
                 )
 
     def end(self, phase):
-        for copy in self.rest:
+        for copy in self.rest + self.last:
             copy.wait()
         for ref, columns, where, count, each, peers, one, two in self.lanes(phase):
             add_into(ref, (count, each(0)), columns, [(two.at[0], 0), (two.at[1], 0)], 0, 128)
@@ -251,20 +273,17 @@
             value = self.tile(self.links.core, j)
             self.crossing[j].wait()
             value = value + self.near_in[j].astype(F32).reshape(256, TILE)
-            self.tmp[...] = value
+            self.tmp[0:256, 0:TILE] = value
             self.near[j] = value.astype(BF16).reshape(4, 64, TILE)
             if leave:
                 self.leave(j)
-            self.out[:, TILE * j : TILE * j + TILE] = self.tmp[span(self.links.z, 64), :]
-
-    def leave(self, j=None):
+            self.out[:, TILE * j : TILE * j + TILE] = self.tmp[span(self.links.z, 64), 0:TILE]
+
+    def leave(self, j=ALL):
         links = self.links
-        for k in (2, 1, 3):
-            if j is None:
-                src, dst = self.near.at[:, ring(links.z, k)], self.far_in.at[k - 1]
-            else:
-                src, dst = self.near.at[j, ring(links.z, k)], self.far_in.at[k - 1, j]
-            self.flying.append(links.go(src, dst, links.zs[k]))
+        whole = self.far_in.at[:, j]
+        moves = [(self.near.at[j, ring(links.z, k)], self.far_in.at[k - 1, j], links.zs[k]) for k in (2, 1, 3)]
+        self.flying.append(links.together(moves, whole))
 
     def arrive(self):
         for copy in self.flying:
@@ -326,39 +345,35 @@
 def moment_step(weight, gradient, first_moment, second_moment, decay_rate):
     first_moment = BETA_ONE * first_moment + (1.0 - BETA_ONE) * gradient
     second_moment = BETA_TWO * second_moment + (1.0 - BETA_TWO) * gradient * gradient
-    update = (
-        first_moment
-        / (1.0 - BETA_ONE**STEP)
-        / (jnp.sqrt(second_moment / (1.0 - BETA_TWO**STEP)) + ADAM_EPS)
-        + decay_rate * weight
-    )
+    one, two = 1.0 / (1.0 - BETA_ONE**STEP), 1.0 / (1.0 - BETA_TWO**STEP)
+    update = (first_moment * one) / (jnp.sqrt(second_moment * two) + ADAM_EPS) + decay_rate * weight
     return (first_moment, second_moment, update)
 
 
-LINK_COPIES = 324
-LOCAL_COPIES = 28
+LINK_COPIES = 194
+LOCAL_COPIES = 43
 
 
 def layer_kernel(
     qkv_w, out_w, up_w, down_w, qkv_m, qkv_v, out_m, out_v, up_m, up_v, down_m, down_v, block_in, cotangent,
     router_w, router_m, router_v, gains, biases, head_count, width_route, forced_width, slot_index, cosines, sines,
     block_out, input_grad, qkv_grad, out_grad, up_grad, down_grad, small_grad, norms,
-    own_q, own_o, own_u, own_d, pack_q, pack_o, pack_u, pack_d, mom_q, mom_o, mom_f,
-    wq, wo, wu, wd, small_slots, small_grid, small, small_near,
+    own_q, own_o, own_u, own_d, pack_q, pack_o, pack_u, pack_d, mom_q, mom_o,
+    wq, wo, wu, wd, grad_q, grad_d, small_slots, small_grid, small, small_near,
     token_rows, tokens, gate_slots, gates, info,
     a_one, a_two, branch, hidden_low,
-    rows_in, upstream_in, hidden, n_one, n_two, merged, merged_too, out_rows, grad_rows,
-    wide, qkv, probs, mixed, d_mixed, d_qkv, act, up_low,
-    near_a, near_in_a, far_in_a, near_b, near_in_b, far_in_b, tmp,
-    gate_part, gate_near, gate_far, small_sum, sx_in, sy_in, sz_in, got_q, squares, slots,
+    rows_in, upstream_in, hidden, n_one, n_two, merged, merged_too, out_rows,
+    wide, qkv, probs, mixed, d_mixed, d_qkv, act, act_gated, up_low,
+    near_a, near_in_a, far_in_a, near_b, near_in_b, far_in_b,
+    gate_part, gate_near, gate_far, small_sum, sx_in, sy_in, sz_in, squares, slots,
     *rest,
 ):
     buffers, (local_sems, send_sems, recv_sems) = rest[:-3], rest[-3:]
     links = Links(send_sems, recv_sems)
     x, y, z, core = links.x, links.y, links.z, links.core
     own_32, own_64 = span(z, 32), span(core, 64)
-    set_a = (near_a, near_in_a, far_in_a, tmp)
-    set_b = (near_b, near_in_b, far_in_b, tmp)
+    set_a = (near_a, near_in_a, far_in_a, wide)
+    set_b = (near_b, near_in_b, far_in_b, wide)
     local_used, pending = [0], {}
 
     def keep(src, dst):
@@ -387,8 +402,8 @@
             copies.append(keep(src, dst))
         return copies
 
-    def to_all(ref, *sets):
-        return [links.go(ref, ref, peer) for peers in sets for peer in peers.values()]
+    def to_all(here, whole, *sets):
+        return [links.together([(here, here, peer) for peers in sets for peer in peers.values()], whole)]
 
     def begin():
         greeted = greet(
@@ -397,7 +412,6 @@
         loads = [keep(qkv_w, own_q), keep(out_w, own_o), keep(up_w, own_u), keep(down_w, own_d)]
         pending["rows"] = [keep(block_in.at[own_64], rows_in), keep(cotangent.at[own_64], upstream_in)]
         pending["branch"] = [keep(cotangent.at[pl.ds(64 * h, 64)], branch.at[z, h]) for h in (0, 1)]
-        pending["mom_u"] = [keep(up_m, mom_f.at[0]), keep(up_v, mom_f.at[1])]
         pending["mom_q"] = [keep(qkv_m, mom_q.at[0]), keep(qkv_v, mom_q.at[1])]
         pending["mom_o"] = [keep(out_m, mom_o.at[0]), keep(out_v, mom_o.at[1])]
         small_slots[z] = jnp.zeros((8, 128), F32)
@@ -440,8 +454,8 @@
 
     def slices_q():
         pending["q"] = to_group(lambda to: [(pack_q.at[to], wq.at[x, y, own_32, :])])
-        pending["small"] = to_all(small_slots.at[z], links.zs)
-        pending["tokens"] = to_all(token_rows.at[z], links.zs)
+        pending["small"] = to_all(small_slots.at[z], small_slots.at[pl.ds(0, 3)], links.zs)
+        pending["tokens"] = to_all(token_rows.at[z], token_rows.at[pl.ds(0, 3)], links.zs)
 
     def slices_o():
         pending["o"] = to_group(
@@ -457,11 +471,11 @@
     def small_x():
         wait("small")
         small_grid[x, y] = small_slots[0] + small_slots[1] + small_slots[2] + small_slots[3]
-        pending["small"] = to_all(small_grid.at[x, y], links.xs)
+        pending["small"] = to_all(small_grid.at[x, y], small_grid.at[0, pl.ds(0, 3)], links.xs)
 
     def small_y():
         wait("small")
-        pending["small"] = to_all(small_grid.at[:, y], links.ys)
+        pending["small"] = to_all(small_grid.at[:, y], small_grid.at[:, pl.ds(0, 3)], links.ys)
 
     def small_rows():
         wait("small")
@@ -557,7 +571,8 @@
     def rows_two_start():
         rows_two.start()
         gate_slots[z, core] = gates[z].T[0:8, :]
-        pending["gates"] = to_all(gate_slots.at[z, core], links.zs, links.others, {0: links.partner})
+        whole = slots.at[0, pl.ds(0, 7), pl.ds(0, 8)]
+        pending["gates"] = to_all(gate_slots.at[z, core], whole, links.zs, links.others, {0: links.partner})
 
     def rows_two_finish():
         rows_two.finish()
@@ -584,6 +599,7 @@
             up = jnp.where(used_units, jnp.maximum(up, 0.0), 0.0)
             low = (up * up).astype(BF16)
             act[:, :, :, at] = low.reshape(4, 2, 64, 256)
+            act_gated[:, :, :, at] = (low.astype(F32) * gate_all).astype(BF16).reshape(4, 2, 64, 256)
             back = wide[:, at]
             up_low[:, :, :, at] = (back * gate_all * 2.0 * up).astype(BF16).reshape(4, 2, 64, 256)
             pairs = (low.astype(F32) * back).astype(BF16)
@@ -600,25 +616,14 @@
         merge_u.cross()
         wait("gate")
         gate_part[...] = gate_part[...] + gate_near[...]
-        pending["gate"] = [
-            links.go(gate_part.at[:, span(ring(z, k), 128)], gate_far.at[k - 1], links.zs[k]) for k in (1, 2, 3)
-        ]
-        merge_u.along()
+        moves = [(gate_part.at[:, span(ring(z, k), 128)], gate_far.at[k - 1], links.zs[k]) for k in (1, 2, 3)]
+        pending["gate"] = [links.together(moves, gate_far.at[pl.ds(0, 3)])]
 
     def merge_u_in():
         wait("gate")
         gate_far[3] = gate_part[:, span(z, 128)] + gate_far[0] + gate_far[1] + gate_far[2]
         info[2] = as_columns(gate_far[3])
         merge_u.arrive()
-
-    def branch_rows():
-        def step(i, rows):
-            token = lax.rem(i, 8)
-            gate = gates[lax.div(i, 8), span(token, 16), :][:, 0:1]
-            at = (lax.div(i, 8), lax.div(token, 4), span(lax.rem(token, 4), 16))
-            branch[at] = (branch[at].astype(F32) * gate).astype(BF16)
-
-        in_blocks(32, step)
 
     def outer(left, right, target):
         def one(i, carry):
@@ -684,8 +689,8 @@
 
     merge_q = Merge(links, d_qkv, wq, set_b, merged_too)
     sums_u = Scatter(links, (wu, pl.ds(0, 512)), (wu, pl.ds(512, 512)), buffers[0:8])
-    sums_d = Scatter(links, (wd, pl.ds(0, 512)), (wd, pl.ds(512, 512)), buffers[8:16])
-    sums_q = Scatter(links, (wq, pl.ds(0, 384)), (wq, pl.ds(384, 384)), buffers[16:24])
+    sums_d = Scatter(links, (grad_d, pl.ds(0, 512)), (grad_d, pl.ds(512, 512)), buffers[8:16])
+    sums_q = Scatter(links, (grad_q, pl.ds(0, 384)), (grad_q, pl.ds(384, 384)), buffers[16:24])
     sums_o = Scatter(links, (wo, pl.ds(0, 128)), (wo, pl.ds(128, 128)), buffers[24:32])
 
     def output_rows():
@@ -708,33 +713,31 @@
             scaled, inverse = n_one[rows, :], info[0, rows, :][:, 0:1]
             small_sum[4] += fold(grad * scaled)
             small_sum[6] += fold(grad)
-            grad_rows[rows, :] = n_two[rows, :] + norm_back(scaled, inverse, small[4:5, :], grad)
+            n_two[rows, :] = n_two[rows, :] + norm_back(scaled, inverse, small[4:5, :], grad)
 
         in_blocks(4, step)
         for r in range(8):
             small[r : r + 1, :] = jnp.sum(small_sum[r], axis=0, keepdims=True)
         pending["small"] = [links.go(small, small_near, links.partner)]
         here = input_grad.at[own_64]
-        pending["input"] = [keep(grad_rows, here), links.go(grad_rows, here, links.partner)]
+        pending["input"] = [keep(n_two, here), links.go(n_two, here, links.partner)]
 
     def small_to_x():
         wait("small")
         small[...] = small[...] + small_near[...]
-        pending["small"] = [
-            links.go(small.at[:, span(ring(x, k), 512)], sx_in.at[k], links.xs[k]) for k in (1, 2, 3)
-        ]
+        moves = [(small.at[:, span(ring(x, k), 512)], sx_in.at[k], links.xs[k]) for k in (1, 2, 3)]
+        pending["small"] = [links.together(moves, sx_in.at[pl.ds(1, 3)])]
 
     def small_to_y():
         wait("small")
         sx_in[0] = small[:, span(x, 512)] + sx_in[1] + sx_in[2] + sx_in[3]
-        pending["small"] = [
-            links.go(sx_in.at[0, :, span(ring(y, k), 128)], sy_in.at[k], links.ys[k]) for k in (1, 2, 3)
-        ]
+        moves = [(sx_in.at[0, :, span(ring(y, k), 128)], sy_in.at[k], links.ys[k]) for k in (1, 2, 3)]
+        pending["small"] = [links.together(moves, sy_in.at[pl.ds(1, 3)])]
 
     def small_to_z():
         wait("small")
         sz_in[z] = sx_in[0, :, span(y, 128)] + sy_in[1] + sy_in[2] + sy_in[3]
-        pending["small"] = to_all(sz_in.at[z], links.zs)
+        pending["small"] = to_all(sz_in.at[z], sz_in.at[pl.ds(0, 3)], links.zs)
 
     def small_done():
         wait("small")
@@ -746,27 +749,36 @@
         squares[9, 0:4, 0:32] = 0.5 * update * update
 
     def owners_u():
-        pending["own_u"] = to_group(lambda to: [(wu.at[x, y, span(to, 32), :], up_grad.at[:, span(z, 1024)])])
+        pending["own_u"] = to_group(lambda to: [(wu.at[x, y, span(to, 32), :], pack_u.at[:, span(z, 1024)])])
 
     def owners_d():
-        pending["own_d"] = to_group(lambda to: [(wd.at[x, y, span(to, 32), :], down_grad.at[:, span(z, 1024)])])
+        pending["own_d"] = to_group(lambda to: [(grad_d.at[x, y, span(to, 32), :], pack_d.at[:, span(z, 1024)])])
 
     def owners_o():
         pending["own_o"] = to_group(
             lambda to: [
-                (wo.at[x, y, span(to, 32), pl.ds(128 * h, 128)], out_grad.at[2 * z + h]) for h in (0, 1)
+                (wo.at[x, y, span(to, 32), pl.ds(128 * h, 128)], pack_o.at[2 * z + h]) for h in (0, 1)
             ]
         )
 
     def owners_q():
-        pending["own_q"] = to_group(lambda to: [(wq.at[x, y, span(to, 32), :], got_q.at[z])])
+        pending["own_q"] = to_group(lambda to: [(grad_q.at[x, y, span(to, 32), :], pack_q.at[z])])
+
+    def moments_wide():
+        for number, (name, first, second) in enumerate((("mom_u", up_m, up_v), ("mom_d", down_m, down_v))):
+            pending[name] = [
+                keep(ref.at[:, pl.ds(1024 * c, 1024)], wide.at[pl.ds(256 * number + 128 * kind + 32 * c, 32)])
+                for kind, ref in enumerate((first, second))
+                for c in range(4)
+            ]
 
     def squares_wide(number, weights, grads):
         def one(i, carry):
             rows, columns = span(lax.div(i, 4), 16), span(lax.rem(i, 4), 1024)
             weight = weights[rows, columns]
+            at = lax.rem(i, 4) * 2 + lax.div(i, 4) + (number - 2) * 16
             _, _, update = moment_step(
-                weight, grads[rows, columns].astype(F32), mom_f[0, rows, columns], mom_f[1, rows, columns], DECAY_RATE
+                weight, grads[rows, columns].astype(F32), wide[span(at, 16), :], wide[span(at + 8, 16), :], DECAY_RATE
             )
             squares[2 * number] += fold_lanes(weight * weight)
             squares[2 * number + 1] += fold_lanes(update * update)
@@ -777,22 +789,24 @@
     def squares_u():
         wait("own_u")
         wait("mom_u")
-        squares_wide(2, own_u, up_grad)
-        pending["mom_d"] = [keep(down_m, mom_f.at[0]), keep(down_v, mom_f.at[1])]
+        pending["results"] = [keep(pack_u, up_grad)]
+        squares_wide(2, own_u, pack_u)
 
     def squares_d():
         wait("own_d")
         wait("mom_d")
-        squares_wide(3, own_d, down_grad)
+        pending["results"].append(keep(pack_d, down_grad))
+        squares_wide(3, own_d, pack_d)
 
     def squares_o():
         wait("own_o")
         wait("mom_o")
+        pending["results"].append(keep(pack_o, out_grad))
 
         def one(head, carry):
             weight = own_o[head]
             _, _, update = moment_step(
-                weight, out_grad[head].astype(F32), mom_o[0, head], mom_o[1, head], DECAY_RATE
+                weight, pack_o[head].astype(F32), mom_o[0, head], mom_o[1, head], DECAY_RATE
             )
             squares[2] += fold_lanes(weight * weight)
             squares[3] += fold_lanes(update * update)
@@ -806,7 +820,7 @@
         for c in range(3):
             for head in range(8):
                 at = 256 * c + 128 * (head % 2)
-                qkv_grad[:, c, head, :] = got_q[head // 2, :, at : at + 128].astype(F32)
+                qkv_grad[:, c, head, :] = pack_q[head // 2, :, at : at + 128].astype(F32)
 
         def one(i, carry):
             rows = pl.ds(i * 4, 4)
@@ -819,129 +833,128 @@
         lax.fori_loop(0, 8, one, 0)
 
     def totals():
-        lanes = lax.broadcasted_iota(jnp.int32, (8, 128), 1)
-        tile = jnp.zeros((8, 128), F32)
-        for number in range(10):
-            value = jnp.sum(jnp.sum(squares[number], axis=0, keepdims=True), axis=1, keepdims=True)
-            tile = jnp.where(lanes == number // 2 + 5 * (number % 2), value, tile)
         here = 4 * core + z
         sets = ((links.zs, links.others, {0: links.partner}), (links.ys,), (links.xs,))
+        tile = jnp.sum(squares[...], axis=1)
         for axis, (me, peers) in enumerate(zip((here, y, x), sets)):
             slots[axis, me] = tile
-            for copy in to_all(slots.at[axis, me], *peers):
+            count = 8 if axis == 0 else 4
+            for copy in to_all(slots.at[axis, me], slots.at[axis, pl.ds(0, count - 1)], *peers):
                 copy.wait()
             tile = slots[axis, 0]
-            for k in range(1, 8 if axis == 0 else 4):
+            for k in range(1, count):
                 tile = tile + slots[axis, k]
         norms[...] = tile
 
     begin()
     slices_q()
     small_x()
+    norm_one()
+    small_y()
     wait("q")
     ring_q.advance()
     slices_o()
+    slices_u()
+    small_rows()
     wait("o")
     ring_o.advance()
-    slices_u()
+    rows_one_start()
+    token_columns()
+    ring_q.advance()
+    ring_o.advance()
     rows_branch.start(own=False)
-    slices_d()
+    wait("u")
+    ring_u.advance()
     ring_q.advance()
-    norm_one()
-    small_y()
+    rows_one.relay()
     ring_o.advance()
     ring_q.advance()
-    small_rows()
-    rows_one_start()
-    token_columns()
+    slices_d()
+    rows_one.finish()
     wait("d")
     ring_d.advance()
-    ring_q.advance()
-    rows_one.relay()
-    ring_d.advance()
+    rows_branch.relay()
+    ring_u.advance()
     ring_o.advance()
     ring_q.advance()
-    wait("u")
-    ring_u.advance()
-    rows_one.finish()
-    rows_branch.relay()
     queries()
-    ring_o.advance()
-    ring_d.advance()
     attend(0, 4)
     ring_u.advance()
+    ring_o.advance()
     attend(4, 8)
-    ring_o.advance()
     merge_one.cross()
     merge_one.along()
-    ring_u.advance()
+    ring_d.advance()
+    ring_d.advance()
     merge_one.arrive()
-    ring_d.advance()
     norm_two()
     rows_two_start()
+    ring_d.advance()
     rows_branch.finish()
     ring_u.advance()
     rows_two.relay()
+    rows_two_finish()
     ring_d.advance()
     units_back()
-    rows_two_finish()
     ring_u.advance()
     units()
     merge_u_out()
+    outer(branch, act_gated, grad_d)
+    sums_d.advance()
+    merge_u.along()
     outer(a_two, up_low, wu)
     sums_u.advance()
-    merge_f.cross()
-    merge_f.along(leave=False)
     merge_u_in()
     back_two()
     rows_back.start()
-    branch_rows()
-    outer(branch, act, wd)
+    merge_f.cross()
     sums_d.advance()
+    merge_f.along(leave=False)
     rows_back.relay()
+    sums_u.advance()
     rows_back.finish()
+    merge_f.leave()
     mixed_back()
-    sums_u.advance()
     attend_back()
     sums_d.advance()
+    sums_u.advance()
+    outer(a_one, d_qkv, grad_q)
+    sums_q.advance()
     merge_q.cross()
     merge_q.along()
+    moments_wide()
     sums_u.advance()
-    outer(a_one, d_qkv, wq)
+    outer(hidden_low, mixed, wo)
+    sums_d.advance()
+    sums_o.advance()
+    sums_u.advance()
+    owners_u()
     sums_q.advance()
+    output_rows()
+    sums_o.advance()
     back_one()
-    merge_f.leave()
-    sums_d.advance()
-    outer(hidden_low, mixed, wo)
     small_to_x()
+    sums_o.advance()
     sums_q.advance()
-    sums_u.advance()
-    sums_u.advance()
-    sums_o.advance()
-    sums_d.advance()
-    small_to_y()
-    sums_q.advance()
-    owners_u()
-    sums_o.advance()
+    squares_u()
     sums_d.advance()
     owners_d()
+    small_to_y()
+    sums_o.advance()
     sums_q.advance()
+    small_to_z()
     sums_o.advance()
-    small_to_z()
-    output_rows()
+    owners_o()
     sums_q.advance()
     owners_q()
     small_done()
-    sums_o.advance()
-    squares_u()
-    sums_o.advance()
-    owners_o()
+    squares_o()
     squares_d()
     squares_q()
-    squares_o()
     totals()
     wait("output")
     wait("input")
+    wait("results")
 
 
 def layer(*operands):
@@ -968,27 +981,28 @@
             jax.ShapeDtypeStruct((32, 4096), BF16),
             jax.ShapeDtypeStruct((32, 4096), BF16),
             jax.ShapeDtypeStruct((8, 128), F32),
-            jax.ShapeDtypeStruct((8, 128), F32),
+            jax.ShapeDtypeStruct((16, 128), F32),
         ),
         in_specs=[ANY] * 14 + [VMEM] * 11,
-        out_specs=(ANY, ANY) + (VMEM,) * 6,
+        out_specs=(ANY, ANY, VMEM, ANY, ANY, ANY, VMEM, VMEM),
         scratch_shapes=[
             vmem(32, 3, 8, 128, kind=F32), vmem(8, 32, 128, kind=F32), vmem(32, 4096, kind=F32),
             vmem(32, 4096, kind=F32),
             vmem(4, 32, 768), vmem(8, 32, 128), vmem(32, 4096), vmem(32, 4096),
-            vmem(2, 32, 3, 8, 128, kind=F32), vmem(2, 8, 32, 128, kind=F32), vmem(2, 32, 4096, kind=F32),
+            vmem(2, 32, 3, 8, 128, kind=F32), vmem(2, 8, 32, 128, kind=F32),
             vmem(4, 4, 128, 768), vmem(4, 4, 128, 256), vmem(4, 4, 128, 1024), vmem(4, 4, 128, 1024),
+            vmem(4, 4, 128, 768), vmem(4, 4, 128, 1024),
             tile, vmem(4, 4, 8, 128, kind=F32), vmem(8, 2048, kind=F32), vmem(8, 2048, kind=F32),
             tile, vmem(4, 128, 128, kind=F32), vmem(4, 2, 8, 128, kind=F32), vmem(4, 128, 128, kind=F32),
             vmem(3, 128, 128, kind=F32),
             tokens, tokens, tokens, tokens,
-            rows_low, rows_low, rows, rows, rows, rows, rows, rows_low, rows,
+            rows_low, rows_low, rows, rows, rows, rows, rows, rows_low,
             vmem(512, 1024, kind=F32), vmem(512, 768), vmem(8, 128, 128, kind=F32),
-            vmem(4, 2, 64, 256), vmem(512, 256), vmem(4, 2, 64, 768), vmem(4, 2, 64, 1024), vmem(4, 2, 64, 1024),
-            *merge_buffers(), *merge_buffers(), vmem(256, TILE, kind=F32),
+            vmem(4, 2, 64, 256), vmem(512, 256), vmem(4, 2, 64, 768), vmem(4, 2, 64, 1024), vmem(4, 2, 64, 1024), vmem(4, 2, 64, 1024),
+            *merge_buffers(), *merge_buffers(),
             vmem(8, 512, kind=F32), vmem(8, 512, kind=F32), tile,
             vmem(8, 8, 2048, kind=F32), vmem(4, 8, 512, kind=F32), tile, tile,
-            vmem(4, 32, 768), vmem(10, 8, 128, kind=F32), vmem(3, 8, 8, 128, kind=F32),
+            vmem(16, 8, 128, kind=F32), vmem(3, 8, 16, 128, kind=F32),
             *sum_buffers(512), *sum_buffers(512), *sum_buffers(384), *sum_buffers(128),
             DMA((LOCAL_COPIES,)), DMA((LINK_COPIES,)), DMA((LINK_COPIES,)),
         ],
@@ -1000,13 +1014,15 @@
 
 
 def renew_kernel(norms, small_grad, gains, biases, norm_m, norm_v, *refs):
-    ins, outs = refs[:20], refs[20:]
-    sums = norms[0:1, :]
+    ins, outs = refs[:22], refs[22:]
+    outs[31][...] = ins[20][...]
+    outs[32][...] = ins[21][...]
+    sums = jnp.sqrt(jnp.sum(norms[...], axis=1, keepdims=True))
     for index in range(5):
         weight, grad, m, v = (ref[...] for ref in ins[4 * index : 4 * index + 4])
         grad = grad[0:4, 0:32] if index == 4 else grad.astype(F32)
         first, second, update = moment_step(weight, grad, m, v, DECAY_RATE)
-        ratio = LEARN_RATE * (jnp.sqrt(sums[:, index : index + 1]) / jnp.sqrt(sums[:, index + 5 : index + 6]))
+        ratio = LEARN_RATE * (sums[2 * index : 2 * index + 1, :] / sums[2 * index + 1 : 2 * index + 2, :])
         ratio = ratio.reshape((1,) * weight.ndim)
         new = weight - ratio * update
         for ref, value in zip(outs[5 * index : 5 * index + 5], (grad, first, second, new, new.astype(BF16))):
@@ -1021,9 +1037,9 @@
     lane = lax.broadcasted_iota(jnp.int32, (8, 128), 1)
     tile = jnp.zeros((8, 128), F32)
     for index in range(10):
-        here = (row == index % 5) & (lane == index // 5)
-        tile = jnp.where(here, jnp.sqrt(sums[:, index : index + 1]), tile)
-    outs[30][...] = tile[0:5, 0:2]
+        here = (row == index % 2) & (lane == index // 2)
+        tile = jnp.where(here, sums[index : index + 1, :], tile)
+    outs[30][...] = tile[0:2, 0:5]
 
 
 def renew(norms, small_grad, gains, biases, norm_m, norm_v, *matrices):
@@ -1040,15 +1056,19 @@
         whole((4, 32)),
     )
     shapes = ((32, 3, 8, 128), (8, 32, 128), (32, 4096), (32, 4096), (4, 32), (4, 32))
-    in_specs = [whole((8, 128)), whole((8, 128)), whole((2, 32)), whole((2, 32)), whole((4, 32)), whole((4, 32))]
+    in_specs = [whole((16, 128)), whole((8, 128)), whole((2, 32)), whole((2, 32)), whole((4, 32)), whole((4, 32))]
     out_specs, out_shape = [], []
     for index, block in enumerate(blocks):
         in_specs += [block, whole((8, 128)) if index == 4 else block, block, block]
     for block, shape in zip((*blocks, whole((4, 32))), shapes):
         out_specs += [block] * 5
         out_shape += [jax.ShapeDtypeStruct(shape, kind) for kind in (F32, F32, F32, F32, BF16)]
-    out_specs.append(whole((5, 2)))
-    out_shape.append(jax.ShapeDtypeStruct((5, 2), F32))
+    out_specs.append(whole((2, 5)))
+    out_shape.append(jax.ShapeDtypeStruct((2, 5), F32))
+    rows = pl.BlockSpec((128 // steps, 2048), lambda i: (i, 0))
+    in_specs += [rows, rows]
+    out_specs += [rows, rows]
+    out_shape += [jax.ShapeDtypeStruct((128, 2048), kind) for kind in (BF16, F32)]
     return pl.pallas_call(
         renew_kernel,
         grid=(steps,),
@@ -1109,19 +1129,20 @@
         *(value.reshape(1, -1) for value in (head_count, width_route, forced_width, slot_index)),
         *rotary_tables(128, 128),
     )
-    *results, lamb_norms = renew(
+    *results, lamb_norms, block_output, input_grad = renew(
         norms, small_grad, norm_gains, norm_biases, norm_first, norm_second,
         qkv_weight, grads[0], qkv_first, qkv_second,
         out[0], grads[1], *out[1:],
         up_weight, grads[2], up_first, up_second,
         down[0], grads[3], *down[1:],
         router[0], small_grad, *router[1:],
+        block_output, input_grad,
     )
     kinds = []
     for kind in range(5):
         qkv, out, up, down, router, norm = (results[5 * index + kind] for index in range(6))
         kinds += [qkv, turned(out), up, down.T, router.T, norm]
-    return (block_output, input_grad, *kinds, lamb_norms)
+    return (block_output, input_grad, *kinds, lamb_norms.T)
 
 
 def solution(mesh):

time: 209 us -> 201 us (0.962)
  Pallas kernels: 204 us -> 199 us
  local copies, waits for them, and re-layouts: 3.19 us -> 0 us
    pallas_call x1, Pallas kernels: 198 us -> 191 us  [layer(): pl.pallas_call(layer_kernel, out_shape=(jax.ShapeDtypeStruct((128, 2048),...]
    unnamed x7 -> x0, local copies, waits for them, and re-layouts: 3.19 us -> none
where the time goes in v5:
time: 201 us
  Pallas kernels  199 us (99%)
    pallas_call x1, Pallas kernels, layer(): pl.pallas_call(layer_kernel, out_shape=(jax.ShapeDtypeStruct((128, 2048),...  191 us
    pallas_call x1, Pallas kernels, renew(): pl.pallas_call(renew_kernel, grid=(steps,), in_specs=in_specs, out_specs=...  7.98 us

profile of v5, /device:TPU:0, one launch (start us, length us, event | category | flops | bytes accessed | tf_op | source)
XLA Modules:
  0.0 200.8 jit_solution(9042674361540539154)
XLA Ops:
  1.3 191.3 %layer.1 = (bf16[128,2048]{1,0:T(8,128)(2,1)}, f32[128,2048]{1,0:T(8,128)}, f32[32,3,8,128]{3,2,1,0:T(8,128)}, bf16[8,32,128]{2,1,0:T(8,128)(2,1)}, bf16[32,4096...) custom-call(f32[32,3,8,128]{3,2,1,0:T(8,128)} %refs_0_.1, ...), custom_call_target="tpu_custom_call" | custom-call | tf_op jit(solution)/shard_map/layer/pallas_call | solution.py:974
  192.7 8.0 %renew.1 = (f32[32,3,8,128]{3,2,1,0:T(8,128)}, f32[32,3,8,128]{3,2,1,0:T(8,128)}, f32[32,3,8,128]{3,2,1,0:T(8,128)}, f32[32,3,8,128]{3,2,1,0:T(8,128)}, bf16[32,...) custom-call(f32[16,128]{1,0:T(8,128)} %get-tuple-element.74.norms, ...), custom_call_target="tpu_custom_call" | custom-call | tf_op jit(solution)/shard_map/renew/pallas_call | solution.py:1072

commit v6 on v5

--- a/solution.py
+++ b/solution.py
@@ -70,6 +70,7 @@
         self.ys = {k: device(x, ring(y, k), z, core) for k in (1, 2, 3)}
         self.zs = {k: device(x, y, ring(z, k), core) for k in (1, 2, 3)}
         self.others = {k: device(x, y, ring(z, k), 1 - core) for k in (1, 2, 3)}
+        self.across = {(i, j): device(ring(x, i), ring(y, j), z, core) for i in (1, 2, 3) for j in (1, 2, 3)}
         self.partner = device(x, y, z, 1 - core)
         self.send_sems, self.recv_sems, self.used = send_sems, recv_sems, 0
 
@@ -78,18 +79,24 @@
         self.used += 1
         return send(src, dst, self.send_sems.at[number], self.recv_sems.at[number], peer)
 
-    def together(self, moves, whole):
+    def bundle(self, whole):
         number = self.used
         self.used += 1
-        sems = self.send_sems.at[number], self.recv_sems.at[number]
-        for src, dst, peer in moves:
-            send(src, dst, *sems, peer)
-        return Bundle(whole, *sems)
+        return Bundle(whole, self.send_sems.at[number], self.recv_sems.at[number])
+
+    def together(self, moves, whole):
+        bundle = self.bundle(whole)
+        for move in moves:
+            bundle.go(*move)
+        return bundle
 
 
 class Bundle:
     def __init__(self, whole, *sems):
         self.whole, self.sems = whole, sems
+
+    def go(self, src, dst, peer):
+        send(src, dst, *self.sems, peer)
 
     def wait(self):
         for sem in self.sems:
@@ -182,7 +189,8 @@
         self.rest.append(links.together(moves, self.buffers[0][2 * phase + 1]))
 
     def middle(self, phase):
-        lanes, self.last = self.lanes(phase), []
+        lanes, last = self.lanes(phase), self.links.bundle(self.buffers[0][2 * phase + 1])
+        self.rest.append(last)
         for side in (0, 1):
             for part in (0, 1):
                 ref, columns, where, count, each, peers, one, two = lanes[part]
@@ -190,14 +198,12 @@
                 step, rows, row = ((1, LOW, 0), (-1, HIGH, 64))[side]
                 self.halves[2 * part + side].wait()
                 add_into(ref, (count, each(step)), columns, [(one.at[side], 0)], row, 64)
-                self.last.append(
-                    self.links.go(
-                        ref.at[where(step) + (rows, columns)], two.at[(side,) + lead + (rows,)], peers[(1, 3)[side]]
-                    )
+                last.go(
+                    ref.at[where(step) + (rows, columns)], two.at[(side,) + lead + (rows,)], peers[(1, 3)[side]]
                 )
 
     def end(self, phase):
-        for copy in self.rest + self.last:
+        for copy in self.rest:
             copy.wait()
         for ref, columns, where, count, each, peers, one, two in self.lanes(phase):
             add_into(ref, (count, each(0)), columns, [(two.at[0], 0), (two.at[1], 0)], 0, 128)
@@ -224,29 +230,29 @@
     def start(self, own=True):
         links = self.links
         here = self.ref.at[links.z, links.core]
-        self.passed = [links.go(here, here, links.partner)] if own else []
+        self.passed = links.bundle(self.ref.at[pl.ds(0, 4 if own else 3), 0])
+        if own:
+            self.passed.go(here, here, links.partner)
         self.flying = [links.go(here, here, links.zs[k]) for k in (1, 3)]
 
     def relay(self):
         links = self.links
-        self.far = []
+        self.far = links.bundle(self.ref.at[0, 0])
         for side, k, rows in ((0, 1, pl.ds(0, 32)), (1, 3, pl.ds(32, 32))):
             self.flying[side].wait_recv()
             block = self.ref.at[ring(links.z, -k), links.core]
             half = block.at[rows]
-            self.far.append(links.go(half, half, links.zs[k]))
-            self.passed.append(links.go(block, block, links.partner))
+            self.far.go(half, half, links.zs[k])
+            self.passed.go(block, block, links.partner)
 
     def finish(self):
         links = self.links
-        for copy in self.far:
-            copy.wait_recv()
+        self.far.wait()
         block = self.ref.at[ring(links.z, 2), links.core]
-        self.passed.append(links.go(block, block, links.partner))
-        for copy in self.flying + self.far:
+        self.passed.go(block, block, links.partner)
+        for copy in self.flying:
             copy.wait_send()
-        for copy in self.passed:
-            copy.wait()
+        self.passed.wait()
 
 
 TILES, TILE = 4, 512
@@ -256,7 +262,7 @@
     def __init__(self, links, left, weights, buffers, out):
         self.links, self.left, self.weights, self.out = links, left, weights, out
         self.near, self.near_in, self.far_in, self.tmp = buffers
-        self.crossing, self.flying = [], []
+        self.crossing, self.flying = [], None
 
     def tile(self, half, j):
         rows = self.weights[j]
@@ -281,13 +287,13 @@
 
     def leave(self, j=ALL):
         links = self.links
-        whole = self.far_in.at[:, j]
-        moves = [(self.near.at[j, ring(links.z, k)], self.far_in.at[k - 1, j], links.zs[k]) for k in (2, 1, 3)]
-        self.flying.append(links.together(moves, whole))
+        if self.flying is None:
+            self.flying = links.bundle(self.far_in)
+        for k in (2, 1, 3):
+            self.flying.go(self.near.at[j, ring(links.z, k)], self.far_in.at[k - 1, j], links.zs[k])
 
     def arrive(self):
-        for copy in self.flying:
-            copy.wait()
+        self.flying.wait()
 
     def rows(self, rows):
         value = self.out[rows, :]
@@ -350,8 +356,8 @@
     return (first_moment, second_moment, update)
 
 
-LINK_COPIES = 194
-LOCAL_COPIES = 43
+LINK_COPIES = 123
+LOCAL_COPIES = 29
 
 
 def layer_kernel(
@@ -371,10 +377,10 @@
     buffers, (local_sems, send_sems, recv_sems) = rest[:-3], rest[-3:]
     links = Links(send_sems, recv_sems)
     x, y, z, core = links.x, links.y, links.z, links.core
-    own_32, own_64 = span(z, 32), span(core, 64)
+    own_32, own_64, plane = span(z, 32), span(core, 64), 4 * x + y
     set_a = (near_a, near_in_a, far_in_a, wide)
     set_b = (near_b, near_in_b, far_in_b, wide)
-    local_used, pending = [0], {}
+    local_used, pending = [0], {"results": []}
 
     def keep(src, dst):
         copy = pltpu.make_async_copy(src, dst, local_sems.at[local_used[0]])
@@ -393,21 +399,20 @@
 
         lax.fori_loop(0, count, one, 0)
 
-    def to_group(moves):
-        copies = []
+    def to_group(whole, moves):
+        bundle = links.bundle(whole)
         for k in (2, 1, 3):
             for src, dst in moves(ring(z, k)):
-                copies.append(links.go(src, dst, links.zs[k]))
-        for src, dst in moves(z):
-            copies.append(keep(src, dst))
-        return copies
+                bundle.go(src, dst, links.zs[k])
+        return [bundle, *(keep(src, dst) for src, dst in moves(z))]
 
     def to_all(here, whole, *sets):
         return [links.together([(here, here, peer) for peers in sets for peer in peers.values()], whole)]
 
     def begin():
         greeted = greet(
-            [*links.xs.values(), *links.ys.values(), *links.zs.values(), *links.others.values(), links.partner]
+            [peer for peers in (links.xs, links.ys, links.across, links.zs, links.others) for peer in peers.values()]
+            + [links.partner]
         )
         loads = [keep(qkv_w, own_q), keep(out_w, own_o), keep(up_w, own_u), keep(down_w, own_d)]
         pending["rows"] = [keep(block_in.at[own_64], rows_in), keep(cotangent.at[own_64], upstream_in)]
@@ -419,22 +424,21 @@
         small_slots[z, 4:6, 0:32] = gains[...].astype(BF16).astype(F32)
         small_slots[z, 6:8, 0:32] = biases[...].astype(BF16).astype(F32)
         small_slots[z] = pltpu.roll(small_slots[z], 32 * z, 1)
-        bucket_row = jnp.where(forced_width[...] < 4, forced_width[...], width_route[...])
+        bucket_row = jnp.where(forced_width[0] < 4, forced_width[0], width_route[...])
         token_rows[z] = jnp.zeros((8, 128), F32)
         token_rows[z, 0:1, :] = head_count[...].astype(F32)
         token_rows[z, 1:2, :] = bucket_row.astype(F32)
         token_rows[z, 2:3, :] = jnp.where(slot_index[...] >= 0, 1.0, 0.0)
-        gates[z] = jnp.zeros((128, 128), F32)
-        gate_part[...] = jnp.zeros_like(gate_part)
-        small_sum[...] = jnp.zeros_like(small_sum)
-        squares[...] = jnp.zeros_like(squares)
         loads[0].wait()
         for c in range(3):
             for head in range(8):
                 at = 256 * c + 128 * (head % 2)
                 pack_q[head // 2, :, at : at + 128] = own_q[:, c, head, :].astype(BF16)
-        for load in loads[1:]:
-            load.wait()
+        pending["loads"] = loads[1:]
+        greeted()
+
+    def pack_rest():
+        wait("loads")
 
         def pack(i, rows):
             pack_u[rows, :] = own_u[rows, :].astype(BF16)
@@ -443,9 +447,10 @@
                 pack_o[head, rows, :] = own_o[head, rows, :].astype(BF16)
 
         in_blocks(2, pack)
-        wait("rows")
-        wait("branch")
-        greeted()
+        gates[z] = jnp.zeros((128, 128), F32)
+        gate_part[...] = jnp.zeros_like(gate_part)
+        small_sum[...] = jnp.zeros_like(small_sum)
+        squares[...] = jnp.zeros_like(squares)
 
     ring_q = Gather(links, (wq, pl.ds(0, 384)), (wq, pl.ds(384, 384)))
     ring_o = Gather(links, (wo, pl.ds(0, 128)), (wo, pl.ds(128, 128)))
@@ -453,20 +458,24 @@
     ring_u = Gather(links, (wu, pl.ds(0, 512)), (wu, pl.ds(512, 512)))
 
     def slices_q():
-        pending["q"] = to_group(lambda to: [(pack_q.at[to], wq.at[x, y, own_32, :])])
+        pending["q"] = to_group(
+            pack_q.at[pl.ds(0, 3)], lambda to: [(pack_q.at[to], wq.at[x, y, own_32, :])])
         pending["small"] = to_all(small_slots.at[z], small_slots.at[pl.ds(0, 3)], links.zs)
         pending["tokens"] = to_all(token_rows.at[z], token_rows.at[pl.ds(0, 3)], links.zs)
 
     def slices_o():
         pending["o"] = to_group(
+            pack_o.at[pl.ds(0, 6)],
             lambda to: [(pack_o.at[2 * to + h], wo.at[x, y, own_32, pl.ds(128 * h, 128)]) for h in (0, 1)]
         )
 
     def slices_d():
-        pending["d"] = to_group(lambda to: [(pack_d.at[:, span(to, 1024)], wd.at[x, y, own_32, :])])
+        pending["d"] = to_group(
+            pack_d.at[:, pl.ds(0, 3072)], lambda to: [(pack_d.at[:, span(to, 1024)], wd.at[x, y, own_32, :])])
 
     def slices_u():
-        pending["u"] = to_group(lambda to: [(pack_u.at[:, span(to, 1024)], wu.at[x, y, own_32, :])])
+        pending["u"] = to_group(
+            pack_u.at[:, pl.ds(0, 3072)], lambda to: [(pack_u.at[:, span(to, 1024)], wu.at[x, y, own_32, :])])
 
     def small_x():
         wait("small")
@@ -491,12 +500,18 @@
     rows_two, rows_back = Spread(links, a_two), Spread(links, hidden_low)
 
     def norm_one():
+        wait("rows")
+
         def step(i, rows):
             scaled, inverse = norm_parts(rows_in[rows, :].astype(F32))
             n_one[rows, :] = scaled
             info[0, rows, :] = columns_tile([inverse])
 
         in_blocks(4, step)
+
+    def rows_branch_start():
+        wait("branch")
+        rows_branch.start(own=False)
 
     def rows_one_start():
         def step(i, rows):
@@ -749,28 +764,36 @@
         squares[9, 0:4, 0:32] = 0.5 * update * update
 
     def owners_u():
-        pending["own_u"] = to_group(lambda to: [(wu.at[x, y, span(to, 32), :], pack_u.at[:, span(z, 1024)])])
+        pending["own_u"] = to_group(
+            pack_u.at[:, pl.ds(0, 3072)], lambda to: [(wu.at[x, y, span(to, 32), :], pack_u.at[:, span(z, 1024)])])
 
     def owners_d():
-        pending["own_d"] = to_group(lambda to: [(grad_d.at[x, y, span(to, 32), :], pack_d.at[:, span(z, 1024)])])
+        pending["own_d"] = to_group(
+            pack_d.at[:, pl.ds(0, 3072)], lambda to: [(grad_d.at[x, y, span(to, 32), :], pack_d.at[:, span(z, 1024)])])
 
     def owners_o():
         pending["own_o"] = to_group(
+            pack_o.at[pl.ds(0, 6)],
             lambda to: [
                 (wo.at[x, y, span(to, 32), pl.ds(128 * h, 128)], pack_o.at[2 * z + h]) for h in (0, 1)
             ]
         )
 
     def owners_q():
-        pending["own_q"] = to_group(lambda to: [(grad_q.at[x, y, span(to, 32), :], pack_q.at[z])])
+        pending["own_q"] = to_group(
+            pack_q.at[pl.ds(0, 3)], lambda to: [(grad_q.at[x, y, span(to, 32), :], pack_q.at[z])])
 
     def moments_wide():
         for number, (name, first, second) in enumerate((("mom_u", up_m, up_v), ("mom_d", down_m, down_v))):
-            pending[name] = [
-                keep(ref.at[:, pl.ds(1024 * c, 1024)], wide.at[pl.ds(256 * number + 128 * kind + 32 * c, 32)])
-                for kind, ref in enumerate((first, second))
-                for c in range(4)
-            ]
+            sem = local_sems.at[local_used[0]]
+            local_used[0] += 1
+            for kind, ref in enumerate((first, second)):
+                for c in range(4):
+                    src = ref.at[:, pl.ds(1024 * c, 1024)]
+                    dst = wide.at[pl.ds(256 * number + 128 * kind + 32 * c, 32)]
+                    pltpu.make_async_copy(src, dst, sem).start()
+            whole = wide.at[pl.ds(256 * number, 256)]
+            pending[name] = [pltpu.make_async_copy(whole, whole, sem)]
 
     def squares_wide(number, weights, grads):
         def one(i, carry):
@@ -789,7 +812,7 @@
     def squares_u():
         wait("own_u")
         wait("mom_u")
-        pending["results"] = [keep(pack_u, up_grad)]
+        pending["results"].append(keep(pack_u, up_grad))
         squares_wide(2, own_u, pack_u)
 
     def squares_d():
@@ -833,13 +856,12 @@
         lax.fori_loop(0, 8, one, 0)
 
     def totals():
-        here = 4 * core + z
-        sets = ((links.zs, links.others, {0: links.partner}), (links.ys,), (links.xs,))
+        here = (4 * core + z, plane)
+        sets = ((links.zs, links.others, {0: links.partner}), (links.xs, links.ys, links.across))
         tile = jnp.sum(squares[...], axis=1)
-        for axis, (me, peers) in enumerate(zip((here, y, x), sets)):
-            slots[axis, me] = tile
-            count = 8 if axis == 0 else 4
-            for copy in to_all(slots.at[axis, me], slots.at[axis, pl.ds(0, count - 1)], *peers):
+        for axis, count in enumerate((8, 16)):
+            slots[axis, here[axis]] = tile
+            for copy in to_all(slots.at[axis, here[axis]], slots.at[axis, pl.ds(0, count - 1)], *sets[axis]):
                 copy.wait()
             tile = slots[axis, 0]
             for k in range(1, count):
@@ -848,109 +870,110 @@
 
     begin()
     slices_q()
+    norm_one()
+    pack_rest()
     small_x()
-    norm_one()
-    small_y()
+    slices_d()
+    slices_o()
     wait("q")
     ring_q.advance()
-    slices_o()
-    slices_u()
-    small_rows()
     wait("o")
     ring_o.advance()
+    token_columns()
+    small_y()
+    rows_branch_start()
+    ring_q.advance()
+    wait("d")
+    ring_d.advance()
+    small_rows()
+    ring_o.advance()
+    ring_q.advance()
+    ring_d.advance()
     rows_one_start()
-    token_columns()
-    ring_q.advance()
-    ring_o.advance()
-    rows_branch.start(own=False)
-    wait("u")
-    ring_u.advance()
-    ring_q.advance()
     rows_one.relay()
     ring_o.advance()
     ring_q.advance()
-    slices_d()
+    slices_u()
     rows_one.finish()
-    wait("d")
+    ring_o.advance()
+    rows_branch.relay()
+    wait("u")
+    ring_u.advance()
     ring_d.advance()
-    rows_branch.relay()
-    ring_u.advance()
-    ring_o.advance()
     ring_q.advance()
     queries()
     attend(0, 4)
+    attend(4, 8)
+    ring_o.advance()
+    merge_one.cross()
     ring_u.advance()
-    ring_o.advance()
-    attend(4, 8)
-    merge_one.cross()
     merge_one.along()
+    ring_u.advance()
+    rows_branch.finish()
+    merge_one.arrive()
     ring_d.advance()
-    ring_d.advance()
-    merge_one.arrive()
     norm_two()
     rows_two_start()
-    ring_d.advance()
-    rows_branch.finish()
     ring_u.advance()
     rows_two.relay()
-    rows_two_finish()
     ring_d.advance()
     units_back()
+    rows_two_finish()
     ring_u.advance()
     units()
-    merge_u_out()
     outer(branch, act_gated, grad_d)
     sums_d.advance()
+    merge_u_out()
     merge_u.along()
     outer(a_two, up_low, wu)
     sums_u.advance()
+    merge_f.cross()
+    merge_f.along(leave=False)
+    sums_d.advance()
     merge_u_in()
     back_two()
     rows_back.start()
-    merge_f.cross()
-    sums_d.advance()
-    merge_f.along(leave=False)
     rows_back.relay()
     sums_u.advance()
+    sums_d.advance()
     rows_back.finish()
-    merge_f.leave()
     mixed_back()
     attend_back()
+    merge_f.leave()
     sums_d.advance()
     sums_u.advance()
     outer(a_one, d_qkv, grad_q)
     sums_q.advance()
     merge_q.cross()
     merge_q.along()
-    moments_wide()
+    sums_d.advance()
+    outer(hidden_low, mixed, wo)
+    sums_o.advance()
+    sums_q.advance()
+    sums_o.advance()
+    output_rows()
     sums_u.advance()
-    outer(hidden_low, mixed, wo)
-    sums_d.advance()
     sums_o.advance()
+    sums_q.advance()
+    owners_d()
+    back_one()
     sums_u.advance()
+    sums_o.advance()
     owners_u()
     sums_q.advance()
-    output_rows()
-    sums_o.advance()
-    back_one()
+    moments_wide()
     small_to_x()
-    sums_o.advance()
-    sums_q.advance()
-    squares_u()
-    sums_d.advance()
-    owners_d()
-    small_to_y()
-    sums_o.advance()
-    sums_q.advance()
-    small_to_z()
+    squares_d()
     sums_o.advance()
     owners_o()
     sums_q.advance()
     owners_q()
+    small_to_y()
+    squares_u()
+    squares_o()
+    small_to_z()
+    squares_q()
     small_done()
-    squares_o()
-    squares_d()
-    squares_q()
     totals()
     wait("output")
     wait("input")
@@ -983,7 +1006,7 @@
             jax.ShapeDtypeStruct((8, 128), F32),
             jax.ShapeDtypeStruct((16, 128), F32),
         ),
-        in_specs=[ANY] * 14 + [VMEM] * 11,
+        in_specs=[ANY] * 14 + [VMEM] * 7 + [pl.BlockSpec(memory_space=pltpu.SMEM)] + [VMEM] * 3,
         out_specs=(ANY, ANY, VMEM, ANY, ANY, ANY, VMEM, VMEM),
         scratch_shapes=[
             vmem(32, 3, 8, 128, kind=F32), vmem(8, 32, 128, kind=F32), vmem(32, 4096, kind=F32),
@@ -1002,7 +1025,7 @@
             *merge_buffers(), *merge_buffers(),
             vmem(8, 512, kind=F32), vmem(8, 512, kind=F32), tile,
             vmem(8, 8, 2048, kind=F32), vmem(4, 8, 512, kind=F32), tile, tile,
-            vmem(16, 8, 128, kind=F32), vmem(3, 8, 16, 128, kind=F32),
+            vmem(16, 8, 128, kind=F32), vmem(2, 16, 16, 128, kind=F32),
             *sum_buffers(512), *sum_buffers(512), *sum_buffers(384), *sum_buffers(128),
             DMA((LOCAL_COPIES,)), DMA((LINK_COPIES,)), DMA((LINK_COPIES,)),
         ],
@@ -1043,7 +1066,7 @@
 
 
 def renew(norms, small_grad, gains, biases, norm_m, norm_v, *matrices):
-    steps = 4
+    steps = 2
 
     def whole(shape):
         return pl.BlockSpec(shape, lambda i: (0,) * len(shape))
@@ -1126,7 +1149,7 @@
         qkv_weight, out[0], up_weight, down[0],
         qkv_first, qkv_second, *out[1:], up_first, up_second, *down[1:],
         block_input, cotangent, *router, norm_gains, norm_biases,
-        *(value.reshape(1, -1) for value in (head_count, width_route, forced_width, slot_index)),
+        head_count.reshape(1, -1), width_route.reshape(1, -1), forced_width, slot_index.reshape(1, -1),
         *rotary_tables(128, 128),
     )
     *results, lamb_norms, block_output, input_grad = renew(

time: 201 us -> 194 us (0.965)
  Pallas kernels: 199 us -> 193 us
    pallas_call x1, Pallas kernels: 191 us -> 185 us  [layer(): pl.pallas_call(layer_kernel, out_shape=(jax.ShapeDtypeStruct((128, 2048),...]
where the time goes in v6:
time: 194 us
  Pallas kernels  193 us (99%)
    pallas_call x1, Pallas kernels, layer(): pl.pallas_call(layer_kernel, out_shape=(jax.ShapeDtypeStruct((128, 2048),...  185 us
    pallas_call x1, Pallas kernels, renew(): pl.pallas_call(renew_kernel, grid=(steps,), in_specs=in_specs, out_specs=...  7.32 us

profile of v6, /device:TPU:0, one launch (start us, length us, event | category | flops | bytes accessed | tf_op | source)
XLA Modules:
  0.0 194.3 jit_solution(2758945728705425524)
XLA Ops:
  1.3 185.5 %layer.1 = (bf16[128,2048]{1,0:T(8,128)(2,1)}, f32[128,2048]{1,0:T(8,128)}, f32[32,3,8,128]{3,2,1,0:T(8,128)}, bf16[8,32,128]{2,1,0:T(8,128)(2,1)}, bf16[32,4096...) custom-call(f32[32,3,8,128]{3,2,1,0:T(8,128)} %refs_0_.1, ...), custom_call_target="tpu_custom_call" | custom-call | tf_op jit(solution)/shard_map/layer/pallas_call | solution.py:997
  186.8 7.3 %renew.1 = (f32[32,3,8,128]{3,2,1,0:T(8,128)}, f32[32,3,8,128]{3,2,1,0:T(8,128)}, f32[32,3,8,128]{3,2,1,0:T(8,128)}, f32[32,3,8,128]{3,2,1,0:T(8,128)}, bf16[32,...) custom-call(f32[16,128]{1,0:T(8,128)} %get-tuple-element.74.norms, ...), custom_call_target="tpu_custom_call" | custom-call | tf_op jit(solution)/shard_map/renew/pallas_call | solution.py:1095

commit v7 on v6

--- a/solution.py
+++ b/solution.py
@@ -397,7 +397,7 @@
             step(i, span(i, 16))
             return carry
 
-        lax.fori_loop(0, count, one, 0)
+        lax.fori_loop(0, count, one, 0, unroll=2)
 
     def to_group(whole, moves):
         bundle = links.bundle(whole)
@@ -529,32 +529,33 @@
             part = wq[:, :, :, 256 * c : 256 * c + 256].reshape(2048, 256)
             wide[:, 256 * c : 256 * c + 256] = dot(a_one[...].reshape(512, 2048), part, (1, 0))
 
-    def spots(index):
-        row, head = lax.div(index, 2), lax.rem(index, 2)
+    def spots(row, head):
         used = jnp.where((core * 8 + z * 2 + head).astype(F32) < tokens[row][:, 0:1], 1.0, 0.0)
-        return row, span(row, 128), [span(2 * c + head, 128) for c in range(3)], used
-
-    def attend(first, last):
+        return span(row, 128), [pl.ds(128 * (2 * c + head), 128) for c in range(3)], used
+
+    def attend(first):
         turned_sines = jnp.where(lane < 64, -sines[...], sines[...])
 
-        def one(index, carry):
-            row, rows, (q_at, k_at, v_at), used = spots(index)
-
-            def rotate(value):
-                return value * cosines[...] + turn(value) * turned_sines
-
+        def rotate(value):
+            return value * cosines[...] + turn(value) * turned_sines
+
+        found = []
+        for row, head in [(first + r, h) for r in (0, 1) for h in (0, 1)]:
+            rows, spots_at, used = spots(row, head)
+            q_at, k_at, v_at = spots_at
             q = (rotate(wide[rows, q_at]) * scale).astype(BF16)
             k = rotate(wide[rows, k_at]).astype(BF16)
             v = wide[rows, v_at].astype(BF16)
-            qkv[rows, q_at], qkv[rows, k_at], qkv[rows, v_at] = q, k, v
             scores = jnp.where(causal, dot(q, k, (1, 1)), -1e30)
             powers = jnp.exp(scores - jnp.max(scores, axis=-1, keepdims=True))
             share = powers / jnp.sum(powers, axis=-1, keepdims=True)
-            probs[index] = share
-            mixed[row, :, :, q_at] = (dot(share.astype(BF16), v, (1, 0)) * used).astype(BF16).reshape(2, 64, 128)
-            return carry
-
-        lax.fori_loop(first, last, one, 0)
+            heads = (dot(share.astype(BF16), v, (1, 0)) * used).astype(BF16)
+            found.append((row, head, rows, spots_at, (q, k, v), share, heads))
+        for row, head, rows, spots_at, values, share, heads in found:
+            for at, value in zip(spots_at, values):
+                qkv[rows, at] = value
+            probs[2 * row + head] = share
+            mixed[row, :, :, spots_at[0]] = heads.reshape(2, 64, 128)
 
     merge_one = Merge(links, mixed, wo, set_a, merged)
 
@@ -642,14 +643,12 @@
 
     def outer(left, right, target):
         def one(i, carry):
-            part = left[:, :, :, span(i, 256)].reshape(512, 256)
+            part = left[:, :, :, span(i, 512)].reshape(512, 512)
             value = dot(part, right[...].reshape(512, right.shape[-1]), (0, 0)).astype(BF16)
-            row, first = lax.div(i, 2), lax.rem(i, 2) * 2
-            target[row, first] = value[0:128]
-            target[row, first + 1] = value[128:256]
+            target[i] = value.reshape(4, 128, right.shape[-1])
             return carry
 
-        lax.fori_loop(0, 8, one, 0)
+        lax.fori_loop(0, 4, one, 0)
 
     def back_two():
         def step(i, rows):
@@ -679,28 +678,28 @@
         d_mixed[...] = dot(hidden_low[...].reshape(512, 2048), wo[...].reshape(2048, 256), (1, 0)).astype(BF16)
 
     def attend_back():
-        def one(index, carry):
-            row, rows, (q_at, k_at, v_at), used = spots(index)
-            share = probs[index]
-            q, k, v = qkv[rows, q_at], qkv[rows, k_at], qkv[rows, v_at]
-            grad = (d_mixed[rows, q_at].astype(F32) * used).astype(BF16)
-            value_grad = dot(share.astype(BF16), grad, (0, 0))
-            share_grad = dot(grad, v, (1, 1))
-            inner = jnp.sum(share * share_grad, axis=-1, keepdims=True)
-            score_grad = (share * (share_grad - inner)).astype(BF16)
-
-            def rotate_back(value):
-                return value * cosines[...] - turn(value * sines[...]) * jnp.where(lane < 64, -1.0, 1.0)
-
-            def put(at, value):
+        def rotate_back(value):
+            return value * cosines[...] - turn(value * sines[...]) * jnp.where(lane < 64, -1.0, 1.0)
+
+        def one(pair, carry):
+            found = []
+            for row, head in [(2 * pair + r, h) for r in (0, 1) for h in (0, 1)]:
+                rows, (q_at, k_at, v_at), used = spots(row, head)
+                share = probs[2 * row + head]
+                q, k, v = qkv[rows, q_at], qkv[rows, k_at], qkv[rows, v_at]
+                grad = (d_mixed[rows, q_at].astype(F32) * used).astype(BF16)
+                value_grad = dot(share.astype(BF16), grad, (0, 0))
+                share_grad = dot(grad, v, (1, 1))
+                inner = jnp.sum(share * share_grad, axis=-1, keepdims=True)
+                score_grad = (share * (share_grad - inner)).astype(BF16)
+                found.append((row, q_at, rotate_back(dot(score_grad, k, (1, 0)) * scale)))
+                found.append((row, k_at, rotate_back(dot(score_grad, q, (0, 0)))))
+                found.append((row, v_at, value_grad))
+            for row, at, value in found:
                 d_qkv[row, :, :, at] = value.astype(BF16).reshape(2, 64, 128)
-
-            put(q_at, rotate_back(dot(score_grad, k, (1, 0)) * scale))
-            put(k_at, rotate_back(dot(score_grad, q, (0, 0))))
-            put(v_at, value_grad)
             return carry
 
-        lax.fori_loop(0, 8, one, 0)
+        lax.fori_loop(0, 2, one, 0)
 
     merge_q = Merge(links, d_qkv, wq, set_b, merged_too)
     sums_u = Scatter(links, (wu, pl.ds(0, 512)), (wu, pl.ds(512, 512)), buffers[0:8])
@@ -872,28 +871,28 @@
     slices_q()
     norm_one()
     pack_rest()
-    small_x()
-    slices_d()
     slices_o()
     wait("q")
     ring_q.advance()
+    small_x()
+    slices_d()
+    small_y()
     wait("o")
     ring_o.advance()
-    token_columns()
-    small_y()
     rows_branch_start()
     ring_q.advance()
     wait("d")
     ring_d.advance()
+    ring_o.advance()
     small_rows()
+    rows_one_start()
+    token_columns()
+    ring_q.advance()
+    rows_one.relay()
+    slices_u()
     ring_o.advance()
     ring_q.advance()
     ring_d.advance()
-    rows_one_start()
-    rows_one.relay()
-    ring_o.advance()
-    ring_q.advance()
-    slices_u()
     rows_one.finish()
     ring_o.advance()
     rows_branch.relay()
@@ -902,20 +901,20 @@
     ring_d.advance()
     ring_q.advance()
     queries()
-    attend(0, 4)
-    attend(4, 8)
+    attend(0)
+    attend(2)
     ring_o.advance()
     merge_one.cross()
     ring_u.advance()
     merge_one.along()
+    rows_branch.finish()
     ring_u.advance()
-    rows_branch.finish()
     merge_one.arrive()
-    ring_d.advance()
     norm_two()
     rows_two_start()
+    ring_d.advance()
+    rows_two.relay()
     ring_u.advance()
-    rows_two.relay()
     ring_d.advance()
     units_back()
     rows_two_finish()
@@ -925,11 +924,11 @@
     sums_d.advance()
     merge_u_out()
     merge_u.along()
+    merge_f.cross()
     outer(a_two, up_low, wu)
     sums_u.advance()
-    merge_f.cross()
+    sums_d.advance()
     merge_f.along(leave=False)
-    sums_d.advance()
     merge_u_in()
     back_two()
     rows_back.start()
@@ -937,43 +936,43 @@
     sums_u.advance()
     sums_d.advance()
     rows_back.finish()
+    merge_f.leave()
     mixed_back()
     attend_back()
-    merge_f.leave()
     sums_d.advance()
-    sums_u.advance()
     outer(a_one, d_qkv, grad_q)
     sums_q.advance()
     merge_q.cross()
     merge_q.along()
+    moments_wide()
+    sums_u.advance()
     sums_d.advance()
     outer(hidden_low, mixed, wo)
     sums_o.advance()
     sums_q.advance()
+    sums_u.advance()
+    back_one()
     sums_o.advance()
     output_rows()
+    small_to_x()
+    sums_q.advance()
     sums_u.advance()
-    sums_o.advance()
-    sums_q.advance()
     owners_d()
-    back_one()
-    sums_u.advance()
+    small_to_y()
     sums_o.advance()
     owners_u()
     sums_q.advance()
-    moments_wide()
-    small_to_x()
-    squares_d()
+    small_to_z()
+    sums_o.advance()
+    sums_q.advance()
+    owners_q()
+    squares_u()
+    small_done()
     sums_o.advance()
     owners_o()
-    sums_q.advance()
-    owners_q()
-    small_to_y()
-    squares_u()
+    squares_d()
+    squares_q()
     squares_o()
-    small_to_z()
-    squares_q()
-    small_done()
     totals()
     wait("output")
     wait("input")

time: 194 us -> 187 us (0.964)
  Pallas kernels: 193 us -> 186 us
    pallas_call x1, Pallas kernels: 185 us -> 178 us  [layer(): pl.pallas_call(layer_kernel, out_shape=(jax.ShapeDtypeStruct((128, 2048),...]
where the time goes in v7:
time: 187 us
  Pallas kernels  186 us (99%)
    pallas_call x1, Pallas kernels, layer(): pl.pallas_call(layer_kernel, out_shape=(jax.ShapeDtypeStruct((128, 2048),...  178 us
    pallas_call x1, Pallas kernels, renew(): pl.pallas_call(renew_kernel, grid=(steps,), in_specs=in_specs, out_specs=...  7.43 us

profile of v7, /device:TPU:0, one launch (start us, length us, event | category | flops | bytes accessed | tf_op | source)
XLA Modules:
  0.0 187.2 jit_solution(9960087048209129846)
XLA Ops:
  1.3 178.2 %layer.1 = (bf16[128,2048]{1,0:T(8,128)(2,1)}, f32[128,2048]{1,0:T(8,128)}, f32[32,3,8,128]{3,2,1,0:T(8,128)}, bf16[8,32,128]{2,1,0:T(8,128)(2,1)}, bf16[32,4096...) custom-call(f32[32,3,8,128]{3,2,1,0:T(8,128)} %refs_0_.1, ...), custom_call_target="tpu_custom_call" | custom-call | tf_op jit(solution)/shard_map/layer/pallas_call | solution.py:996
  179.6 7.4 %renew.1 = (f32[32,3,8,128]{3,2,1,0:T(8,128)}, f32[32,3,8,128]{3,2,1,0:T(8,128)}, f32[32,3,8,128]{3,2,1,0:T(8,128)}, f32[32,3,8,128]{3,2,1,0:T(8,128)}, bf16[32,...) custom-call(f32[16,128]{1,0:T(8,128)} %get-tuple-element.74.norms, ...), custom_call_target="tpu_custom_call" | custom-call | tf_op jit(solution)/shard_map/renew/pallas_call | solution.py:1094
